TPU v7x, 32 devices: a whole 2x2x4 slice. The times are simulated.
32 devices in a mesh: section: 2 (over core), seq: 8 (over z, y), head: 2 (over x).
Axes of the slice: x: 2, y: 2, z: 4, core: 2. Of those that a mesh axis runs over, the one named last changes fastest.
Arguments:
- boundary_in: float32 [2, 2, 2048, 768], P('section', None, ('seq', 'head')), may hold values from -6 to 6
- short_items: int32 [1, 3], replicated, may hold values from 1 to 4, 8 in all within a row
- norm_gains: float32 [2, 2, 768], P('section'), may hold values from 0.5 to 1.5
- norm_biases: float32 [2, 2, 768], P('section'), may hold values from -1.2 to 1.2
- projection_in: float32 [2, 768, 3, 768], P('section', None, None, 'head'), may hold values from -0.21875 to 0.21875
- head_bias: float32 [2, 2, 768], P('section', None, 'head'), may hold values from -1.2 to 1.2
- projection_out: float32 [2, 768, 768], P('section', 'head'), may hold values from -1.75 to 1.75
- residual_bias: float32 [2, 2, 768], P('section'), may hold values from -1.2 to 1.2
- up_weight: float32 [2, 768, 3072], P('section', None, 'head'), may hold values from -0.21875 to 0.21875
- up_bias: float32 [2, 3072], P('section', 'head'), may hold values from -1.2 to 1.2
- down_weight: float32 [2, 3072, 768], P('section', 'head'), may hold values from -0.109375 to 0.109375
- memory_tokens: float32 [2, 16, 768], P('section', 'head'), may hold values from -6 to 6
- query_memory: float32 [2, 768, 384], P('section'), may hold values from -0.21875 to 0.21875
- key_memory: float32 [2, 768, 384], P('section'), may hold values from -0.21875 to 0.21875
- value_memory: float32 [2, 768, 768], P('section', None, 'head'), may hold values from -1.75 to 1.75
Outputs:
- boundary_out: float32 [2, 2, 2048, 768], P('section', None, ('seq', 'head'))
- grad_norm_gains: float32 [2, 2, 768], P('section')
- grad_norm_biases: float32 [2, 2, 768], P('section')
- grad_projection_in: float32 [2, 768, 3, 768], P('section', None, None, 'head')
- grad_head_bias: float32 [2, 2, 768], P('section', None, 'head')
- grad_projection_out: float32 [2, 768, 768], P('section', 'head')
- grad_residual_bias: float32 [2, 2, 768], P('section')
- grad_up_weight: float32 [2, 768, 3072], P('section', None, 'head')
- grad_up_bias: float32 [2, 3072], P('section', 'head')
- grad_down_weight: float32 [2, 3072, 768], P('section', 'head')
- grad_memory_tokens: float32 [2, 16, 768], P('section', 'head')
- grad_query_memory: float32 [2, 768, 384], P('section')
- grad_key_memory: float32 [2, 768, 384], P('section')
- grad_value_memory: float32 [2, 768, 768], P('section', None, 'head')
Inputs may be any that keep to these rules, and one draw needn't show every extreme that they name: `short_items`: each row lists, in order along the segments, the segment counts of one micro-batch's items; every row sums to 8.
All inputs are finite; a program needn't handle non-finite values.
Results may differ from a plain program's by a relative error of at most 0.0003.
Values sent between devices are 32-bit elements; how exact they have to be, the bound alone decides.
A program may use at most 320 MiB of HBM per device.

v0:
```python
import math

import jax
import jax.numpy as jnp
from jax import lax
from jax.sharding import PartitionSpec as P

HEAD_DIM = 64


EPSILON = 1e-05
HIGHEST_PRECISION = lax.Precision.HIGHEST


def entering(part, axis, combine, identity, reverse):
    count = lax.axis_size(axis)
    place = lax.axis_index(axis)
    ahead = count - 1 - place if reverse else place
    gathered = jax.tree.map(lambda a: lax.all_gather(a, axis), part)
    state = jax.tree.map(lambda a, e: jnp.zeros_like(a) + jnp.asarray(e, a.dtype), part, identity)

    def one(turn, state):
        source = count - 1 - turn if reverse else turn
        return combine(
            state, jax.tree.map(lambda a: lax.dynamic_index_in_dim(a, source, 0, False), gathered)
        )

    return lax.fori_loop(0, ahead, one, state)


def passed_along(value, axis, steps):
    count = lax.axis_size(axis)
    first, last = (max(0, -steps), min(count, count - steps))
    return lax.ppermute(value, axis, [(source, source + steps) for source in range(first, last)])


def matmul(left_mat, right_mat):
    return jnp.dot(
        left_mat, right_mat, precision=HIGHEST_PRECISION, preferred_element_type=jnp.float32
    )


def normalize(values_in, gain_row, bias_row):
    centred = values_in - jnp.mean(values_in, axis=-1, keepdims=True)
    spread = jnp.mean(centred * centred, axis=-1, keepdims=True)
    return centred * lax.rsqrt(spread + EPSILON) * gain_row + bias_row


def features(projected):
    halves = jnp.concatenate([jax.nn.softplus(projected), jax.nn.softplus(-projected)], axis=-1)
    return jnp.concatenate(
        [halves * jnp.roll(halves, rolled_by, axis=-1) for rolled_by in (1, 2, 3)], axis=-1
    )


def gelu_tanh(values_in):
    return jax.nn.gelu(values_in, approximate=True)


def spread_rows(local_rows):
    return lax.all_gather(local_rows, "head", axis=0, tiled=True)


def collect_rows(left_rows, right_mat, row_count):

    def term_rows():
        picked = lax.slice_in_dim(left_rows, 0, lax.axis_size("head") * row_count, axis=0)
        if right_mat is None:
            return picked
        return matmul(picked, right_mat)

    return lax.psum_scatter(term_rows(), "head", scatter_dimension=0, tiled=True)


def chain_combine(earlier, later):
    keep_share = 1.0 - later[2]
    return (
        later[0] + keep_share * earlier[0],
        later[1] + keep_share * earlier[1],
        jnp.maximum(earlier[2], later[2]),
    )


def chain_identity(update_a, update_z):
    return (jnp.zeros_like(update_a), jnp.zeros_like(update_z), jnp.zeros((), jnp.float32))


def row_places(head_count, local_count, seg_count, mem_count):
    ordinal = jnp.arange(head_count * local_count)
    owner = ordinal // local_count
    within = ordinal % local_count
    return jnp.where(
        within < seg_count,
        owner * seg_count + within,
        head_count * seg_count + owner * mem_count + within - seg_count,
    )


def split_heads(projected, part_number):
    return projected[:, part_number].reshape(projected.shape[0], -1, HEAD_DIM)


def attention_scores(projected, places):
    scores = jnp.einsum(
        "qhe,khe->hqk",
        split_heads(projected, 0),
        split_heads(projected, 1),
        precision=HIGHEST_PRECISION,
    ) / math.sqrt(HEAD_DIM)
    return jnp.where((places[:, None] >= places[None, :])[None], scores, -1e30)


def attention_forward(projected, places):
    scores = attention_scores(projected, places)
    row_top = jnp.max(scores, axis=-1, keepdims=True)
    exponent = jnp.exp(scores - row_top)
    row_total = jnp.sum(exponent, axis=-1, keepdims=True)
    attended = jnp.einsum(
        "hqk,khe->qhe", exponent / row_total, split_heads(projected, 2), precision=HIGHEST_PRECISION
    )
    return (attended.reshape(projected.shape[0], -1), (row_top + jnp.log(row_total))[..., 0])


def attention_backward(projected, attended, logsum, d_attended, places):
    row_count = projected.shape[0]
    soft_weights = jnp.exp(attention_scores(projected, places) - logsum[..., None])
    grad_heads = d_attended.reshape(row_count, -1, HEAD_DIM)
    out_heads = attended.reshape(row_count, -1, HEAD_DIM)
    d_value = jnp.einsum("hqk,qhe->khe", soft_weights, grad_heads, precision=HIGHEST_PRECISION)
    d_soft = jnp.einsum(
        "qhe,khe->hqk", grad_heads, split_heads(projected, 2), precision=HIGHEST_PRECISION
    )
    inner_dot = jnp.sum(grad_heads * out_heads, axis=-1).T
    d_scores = soft_weights * (d_soft - inner_dot[..., None]) / math.sqrt(HEAD_DIM)
    d_query = jnp.einsum(
        "hqk,khe->qhe", d_scores, split_heads(projected, 1), precision=HIGHEST_PRECISION
    )
    d_key = jnp.einsum(
        "hqk,qhe->khe", d_scores, split_heads(projected, 0), precision=HIGHEST_PRECISION
    )
    return jnp.stack([d_query, d_key, d_value], axis=1).reshape(row_count, 3, -1)


def layer_forward(inputs, params, item_flag, places, memory_state):
    head_count = lax.axis_size("head")
    seg_count = inputs.shape[0]
    all_rows = jnp.concatenate([inputs, params["memory"]], axis=0)
    local_count = all_rows.shape[0]
    normed = normalize(all_rows, params["gains"][0], params["biases"][0])
    normed_all = spread_rows(normed)
    head_width = params["proj_in"].shape[2]
    bias_rows = jnp.stack(
        [params["head_bias"][0], jnp.zeros((head_width,), jnp.float32), params["head_bias"][1]]
    )
    projected = (
        matmul(normed_all, params["proj_in"].reshape(-1, 3 * head_width)).reshape(-1, 3, head_width)
        + bias_rows
    )
    attended, logsum = attention_forward(projected, places)
    hidden = (
        all_rows + collect_rows(attended, params["proj_out"], local_count) + params["residual"][0]
    )
    mixed_rows = normalize(hidden, params["gains"][1], params["biases"][1])
    mixed_all = spread_rows(mixed_rows)
    inner_pre = matmul(mixed_all, params["up"]) + params["up_bias"]
    inner_act = gelu_tanh(inner_pre)
    result = hidden + collect_rows(inner_act, params["down"], local_count) + params["residual"][1]
    result_all = spread_rows(result).reshape(head_count, local_count, -1)
    seg_all = result_all[:, :seg_count].reshape(head_count * seg_count, -1)
    mem_all = result_all[:, seg_count:].reshape(-1, result_all.shape[2])
    key_proj = matmul(mem_all, params["key_mem"])
    key_feats = features(key_proj)
    value_rows = matmul(mem_all, params["value_mem"])
    if memory_state is None:
        update_a = matmul(value_rows.T, key_feats)
        update_z = jnp.sum(key_feats, axis=0)
        prefix_a, prefix_z, _ = entering(
            (update_a, update_z, item_flag),
            "seq",
            chain_combine,
            chain_identity(update_a, update_z),
            False,
        )
        memory_state = ((1.0 - item_flag) * prefix_a, (1.0 - item_flag) * prefix_z)
    query_proj = matmul(seg_all, params["query_mem"])
    query_feats = features(query_proj)
    numerator = matmul(query_feats, memory_state[0].T)
    denominator = matmul(query_feats, memory_state[1][:, None]) + 1.0
    read_rows = numerator / denominator
    read_local = lax.all_to_all(read_rows, "head", split_axis=0, concat_axis=1, tiled=True)
    return dict(
        inputs=inputs,
        all_rows=all_rows,
        normed_all=normed_all,
        projected=projected,
        attended=attended,
        logsum=logsum,
        hidden=hidden,
        mixed_all=mixed_all,
        inner_pre=inner_pre,
        inner_act=inner_act,
        seg_all=seg_all,
        mem_all=mem_all,
        key_proj=key_proj,
        key_feats=key_feats,
        value_rows=value_rows,
        query_proj=query_proj,
        query_feats=query_feats,
        denominator=denominator,
        read_rows=read_rows,
        state_a=memory_state[0],
        state_z=memory_state[1],
        output=result[:seg_count] + read_local,
    )


def layer_backward(grad_rows, record, params, item_flag, places):
    head_count = lax.axis_size("head")
    seg_count = grad_rows.shape[0]
    local_count = record["all_rows"].shape[0]
    mem_count = local_count - seg_count
    d_read = lax.all_to_all(grad_rows, "head", split_axis=1, concat_axis=0, tiled=True)
    denominator = record["denominator"]
    d_numer = d_read / denominator
    d_denom = -jnp.sum(d_read * record["read_rows"], axis=-1, keepdims=True) / denominator
    d_query_feats = matmul(d_numer, record["state_a"]) + d_denom * record["state_z"][None, :]
    keep_share = 1.0 - item_flag
    grad_state_a = keep_share * matmul(d_numer.T, record["query_feats"])
    grad_state_z = keep_share * jnp.sum(d_denom * record["query_feats"], axis=0)
    back_a, back_z, _ = entering(
        (grad_state_a, grad_state_z, item_flag),
        "seq",
        chain_combine,
        chain_identity(grad_state_a, grad_state_z),
        True,
    )
    d_query_proj = jax.vjp(features, record["query_proj"])[1](d_query_feats)[0]
    d_values = matmul(record["key_feats"], back_a.T)
    d_key_feats = matmul(record["value_rows"], back_a) + back_z[None, :]
    d_key_proj = jax.vjp(features, record["key_proj"])[1](d_key_feats)[0]
    d_seg = matmul(d_query_proj, params["query_mem"].T)
    d_mem = matmul(d_key_proj, params["key_mem"].T) + matmul(d_values, params["value_mem"].T)
    width_full = d_seg.shape[1]
    d_result_all = jnp.concatenate(
        [
            d_seg.reshape(head_count, seg_count, width_full),
            d_mem.reshape(head_count, mem_count, width_full),
        ],
        axis=1,
    ).reshape(head_count * local_count, width_full)
    residual_grad = jnp.concatenate(
        [grad_rows, jnp.zeros((mem_count, width_full), jnp.float32)], axis=0
    )
    d_result = collect_rows(d_result_all, None, local_count) + residual_grad
    d_result_rows = spread_rows(d_result)
    grad_down = matmul(record["inner_act"].T, d_result_rows)
    d_inner = matmul(d_result_rows, params["down"].T)
    d_pre = jax.vjp(gelu_tanh, record["inner_pre"])[1](d_inner)[0]
    grad_up = matmul(record["mixed_all"].T, d_pre)
    d_mixed = collect_rows(d_pre, params["up"].T, local_count)
    d_hidden_norm, gain_two, bias_two = jax.vjp(
        normalize, record["hidden"], params["gains"][1], params["biases"][1]
    )[1](d_mixed)
    d_hidden = d_result + d_hidden_norm
    d_hidden_rows = spread_rows(d_hidden)
    grad_out = matmul(record["attended"].T, d_hidden_rows)
    d_attended = matmul(d_hidden_rows, params["proj_out"].T)
    d_projected = attention_backward(
        record["projected"], record["attended"], record["logsum"], d_attended, places
    )
    flat_grad = d_projected.reshape(d_projected.shape[0], -1)
    grad_in = matmul(record["normed_all"].T, flat_grad).reshape(params["proj_in"].shape)
    grad_head_bias = jnp.stack(
        [jnp.sum(d_projected[:, 0], axis=0), jnp.sum(d_projected[:, 2], axis=0)]
    )
    d_normed = collect_rows(flat_grad, params["proj_in"].reshape(width_full, -1).T, local_count)
    d_rows_norm, gain_one, bias_one = jax.vjp(
        normalize, record["all_rows"], params["gains"][0], params["biases"][0]
    )[1](d_normed)
    d_rows = d_hidden + d_rows_norm
    sharded = (
        grad_in,
        grad_head_bias,
        grad_out,
        grad_up,
        jnp.sum(d_pre, axis=0),
        grad_down,
        d_rows[seg_count:],
        matmul(record["mem_all"].T, d_values),
    )
    shared = (
        jnp.stack([gain_one, gain_two]),
        jnp.stack([bias_one, bias_two]),
        jnp.stack([jnp.sum(d_hidden, axis=0), jnp.sum(d_result, axis=0)]),
        matmul(record["seg_all"].T, d_query_proj),
        matmul(record["mem_all"].T, d_key_proj),
    )
    return (d_rows[:seg_count], sharded, shared)


def shards(
    boundary_in,
    short_items,
    norm_gains,
    norm_biases,
    projection_in,
    head_bias,
    projection_out,
    residual_bias,
    up_weight,
    up_bias,
    down_weight,
    memory_tokens,
    query_memory,
    key_memory,
    value_memory,
):
    section_place = lax.axis_index("section")
    sections = lax.axis_size("section")
    head_count = lax.axis_size("head")
    seq_place = lax.axis_index("seq")
    micro_total = boundary_in.shape[1]
    seg_count = boundary_in.shape[2]
    mem_count = memory_tokens.shape[1]
    params = dict(
        gains=norm_gains[0],
        biases=norm_biases[0],
        proj_in=projection_in[0],
        head_bias=head_bias[0],
        proj_out=projection_out[0],
        residual=residual_bias[0],
        up=up_weight[0],
        up_bias=up_bias[0],
        down=down_weight[0],
        memory=memory_tokens[0],
        query_mem=query_memory[0],
        key_mem=key_memory[0],
        value_mem=value_memory[0],
    )
    places = row_places(head_count, seg_count + mem_count, seg_count, mem_count)
    flag_list = [(seq_place == 0).astype(jnp.float32)]
    micro_number = 0
    counts = short_items[micro_number]
    bounds = jnp.cumsum(counts) - counts
    flag_list.append(jnp.any(bounds == seq_place).astype(jnp.float32))
    flags = jnp.stack(flag_list)
    tick_total = micro_total + sections - 1
    received = jnp.zeros_like(boundary_in[0, 0])
    records = []
    outputs = []
    for step_number in range(tick_total):
        micro_index = jnp.clip(step_number - section_place, 0, micro_total - 1)
        source = boundary_in[0, min(step_number, micro_total - 1)]
        inputs = jnp.where(section_place == 0, source, received)
        record = layer_forward(inputs, params, flags[micro_index], places, None)
        records.append(record)
        outputs.append(record["output"])
        if step_number + 1 < tick_total:
            received = passed_along(record["output"], "section", 1)
    stacked_inputs = jnp.stack([entry["inputs"] for entry in records])
    stacked_a = jnp.stack([entry["state_a"] for entry in records])
    stacked_z = jnp.stack([entry["state_z"] for entry in records])
    back_received = jnp.zeros_like(boundary_in[0, 0])
    grads_input = []
    total_sharded = None
    total_shared = None
    for step_number in range(tick_total):
        raw_index = step_number - (sections - 1 - section_place)
        valid = jnp.logical_and(raw_index >= 0, raw_index < micro_total).astype(jnp.float32)
        micro_index = jnp.clip(raw_index, 0, micro_total - 1)
        forward_tick = jnp.clip(micro_index + section_place, 0, tick_total - 1)
        item_flag = flags[micro_index]
        grad_in = jnp.where(
            section_place == sections - 1,
            boundary_in[0, min(step_number, micro_total - 1)],
            back_received,
        )
        record = layer_forward(
            stacked_inputs[forward_tick],
            params,
            item_flag,
            places,
            (stacked_a[forward_tick], stacked_z[forward_tick]),
        )
        grad_x, sharded, shared = layer_backward(grad_in, record, params, item_flag, places)
        sharded = jax.tree.map(lambda grad_part: valid * grad_part, sharded)
        shared = jax.tree.map(lambda grad_part: valid * grad_part, shared)
        if total_sharded is None:
            total_sharded = sharded
            total_shared = shared
        else:
            total_sharded = jax.tree.map(
                lambda running, fresh: running + fresh, total_sharded, sharded
            )
            total_shared = jax.tree.map(
                lambda running, fresh: running + fresh, total_shared, shared
            )
        grads_input.append(grad_x)
        if step_number + 1 < tick_total:
            back_received = passed_along(grad_x, "section", -1)
    (
        grad_in_proj,
        grad_heads_bias,
        grad_out_proj,
        grad_up_w,
        grad_up_b,
        grad_down_w,
        grad_mem,
        grad_value_w,
    ) = total_sharded
    shares = (
        lax.psum_scatter(grad_in_proj, "seq", scatter_dimension=0, tiled=True),
        lax.psum_scatter(grad_out_proj, "seq", scatter_dimension=1, tiled=True),
        lax.psum_scatter(grad_up_w, "seq", scatter_dimension=0, tiled=True),
        lax.psum_scatter(grad_up_b, "seq", scatter_dimension=0, tiled=True),
        lax.psum_scatter(grad_down_w, "seq", scatter_dimension=1, tiled=True),
        lax.psum_scatter(grad_mem, "seq", scatter_dimension=1, tiled=True),
        lax.psum_scatter(grad_value_w, "seq", scatter_dimension=0, tiled=True),
    )
    grad_in_proj, grad_out_proj, grad_up_w, grad_up_b, grad_down_w, grad_mem, grad_value_w = (
        lax.all_gather(shares[0], "seq", axis=0, tiled=True),
        lax.all_gather(shares[1], "seq", axis=1, tiled=True),
        lax.all_gather(shares[2], "seq", axis=0, tiled=True),
        lax.all_gather(shares[3], "seq", axis=0, tiled=True),
        lax.all_gather(shares[4], "seq", axis=1, tiled=True),
        lax.all_gather(shares[5], "seq", axis=1, tiled=True),
        lax.all_gather(shares[6], "seq", axis=0, tiled=True),
    )
    grad_heads_bias = lax.psum(grad_heads_bias, "seq")
    grad_gains, grad_biases, grad_residual, grad_query_w, grad_key_w = total_shared
    grad_gains, grad_biases, grad_residual, grad_query_w, grad_key_w = lax.psum(
        (grad_gains, grad_biases, grad_residual, grad_query_w, grad_key_w), ("seq", "head")
    )
    finished_grads = jnp.stack(
        [grads_input[micro_number + sections - 1] for micro_number in range(micro_total)]
    )
    finished_outputs = jnp.stack(
        [outputs[micro_number + sections - 1] for micro_number in range(micro_total)]
    )
    boundary_out = jnp.where(section_place == 0, finished_grads, finished_outputs)[None]
    return (
        boundary_out,
        grad_gains[None],
        grad_biases[None],
        grad_in_proj[None],
        grad_heads_bias[None],
        grad_out_proj[None],
        grad_residual[None],
        grad_up_w[None],
        grad_up_b[None],
        grad_down_w[None],
        grad_mem[None],
        grad_query_w[None],
        grad_key_w[None],
        grad_value_w[None],
    )


def solution(mesh):
    return jax.shard_map(
        shards,
        mesh=mesh,
        in_specs=(
            P("section", None, ("seq", "head"), None),
            P(),
            P("section", None, None),
            P("section", None, None),
            P("section", None, None, "head"),
            P("section", None, "head"),
            P("section", "head", None),
            P("section", None, None),
            P("section", None, "head"),
            P("section", "head"),
            P("section", "head", None),
            P("section", "head", None),
            P("section", None, None),
            P("section", None, None),
            P("section", None, "head"),
        ),
        out_specs=(
            P("section", None, ("seq", "head"), None),
            P("section", None, None),
            P("section", None, None),
            P("section", None, None, "head"),
            P("section", None, "head"),
            P("section", "head", None),
            P("section", None, None),
            P("section", None, "head"),
            P("section", "head"),
            P("section", "head", None),
            P("section", "head", None),
            P("section", None, None),
            P("section", None, None),
            P("section", None, "head"),
        ),
        check_vma=False,
    )
```

profile of v0, /device:TPU:0, one launch (start us, length us, event | category | flops | bytes accessed | tf_op | source)
XLA Modules:
  0.0 5612.7 jit_solution(9188557044949605396)
XLA Ops:
  11.4 13.3 all_gather.177
  49.1 19.3 reduce-scatter.30.cloned.1.call-done
  94.3 18.1 reduce-scatter.32.cloned.1.call-done
  145.6 47.6 all-reduce.50
  197.2 49.8 all-gather.12
  249.3 425.7 %all-gather.41.cloned.1.call-done = f32[3072,2304]{1,0:T(8,128)} async-done(((f32[384,2304]{1,0:T(8,128)}), f32[3072,2304]{1,0:T(8,128)}) %all-gather.41.cloned.1.call-update) | async-done | bytes 28311568 | tf_op jit(solution)/shard_map/all_gather | solution.py:19
  699.9 12.8 all_gather.185
  733.2 67.9 %reduce-scatter.34.cloned.1.call-done = f32[136,768]{1,0:T(8,128)} async-done(((f32[272,768]{1,0:T(8,128)}), f32[136,768]{1,0:T(8,128)}) %reduce-scatter.34.cloned.1.call-update) | async-done | bytes 417808 | tf_op jit(solution)/shard_map/reduce_scatter | solution.py:72
  829.7 18.1 reduce-scatter.36.cloned.1.call-done
  874.1 71.1 %all-gather.13 = f32[8,1,2304]{2,1,0:T(1,128)S(1)} all-gather(f32[1,1,2304]{2,1,0:T(1,128)S(1)} %reshape.923), channel_id=5, replica_groups=mesh['section'=2,'seq'=8,'head'=2] {'seq'}, dimensions={0}, use_global_device_ids=true | all-gather | bytes 82944 | tf_op jit(solution)/shard_map/all_gather | solution.py:19
  948.1 462.4 %all-gather.43.cloned.1.call-done = f32[3072,2304]{1,0:T(8,128)} async-done(((f32[384,2304]{1,0:T(8,128)}), f32[3072,2304]{1,0:T(8,128)}) %all-gather.43.cloned.1.call-update) | async-done | bytes 28311568 | tf_op jit(solution)/shard_map/all_gather | solution.py:19
  1439.7 12.9 all_gather.196
  1509.5 33.1 reduce-scatter.42.cloned.1.call-done
  1542.7 41.9 reduce-scatter.38.cloned.1.call-done
  1616.5 17.3 all_gather.197
  1645.9 18.1 reduce-scatter.44.cloned.1.call-done
  1714.1 51.6 all-gather.14
  1770.5 457.9 %all-gather.45.cloned.1.call-done = f32[3072,2304]{1,0:T(8,128)} async-done(((f32[384,2304]{1,0:T(8,128)}), f32[3072,2304]{1,0:T(8,128)}) %all-gather.45.cloned.1.call-update) | async-done | bytes 28311568 | tf_op jit(solution)/shard_map/all_gather | solution.py:19
  2278.7 91.9 %all-gather.15 = f32[8,1,2304]{2,1,0:T(1,128)S(1)} all-gather(f32[1,1,2304]{2,1,0:T(1,128)S(1)} %reshape.927), channel_id=9, replica_groups=mesh['section'=2,'seq'=8,'head'=2] {'seq'}, dimensions={0}, use_global_device_ids=true | all-gather | bytes 82944 | tf_op jit(solution)/shard_map/all_gather | solution.py:19
  2375.5 460.2 %all-gather.47.cloned.1.call-done = f32[3072,2304]{1,0:T(8,128)} async-done(((f32[384,2304]{1,0:T(8,128)}), f32[3072,2304]{1,0:T(8,128)}) %all-gather.47.cloned.1.call-update) | async-done | bytes 28311568 | tf_op jit(solution)/shard_map/all_gather | solution.py:19
  2837.7 46.1 while.93
  2894.6 15.3 reduce-scatter.46.cloned.1.call-done
  2939.5 18.0 reduce-scatter.48.cloned.1.call-done
  2997.8 18.0 reduce-scatter.50.cloned.1.call-done
  3054.3 17.1 all_gather.210
  3095.5 18.1 reduce-scatter.52.cloned.1.call-done
  3144.7 16.9 all_gather.211
  3245.3 59.0 %all-gather.16 = f32[8,1,2304]{2,1,0:T(1,128)S(1)} all-gather(f32[1,1,2304]{2,1,0:T(1,128)S(1)} %reshape.929), channel_id=11, replica_groups=mesh['section'=2,'seq'=8,'head'=2] {'seq'}, dimensions={0}, use_global_device_ids=true | all-gather | bytes 82944 | tf_op jit(solution)/shard_map/all_gather | solution.py:19
  3310.0 457.0 %all-gather.49.cloned.1.call-done = f32[3072,2304]{1,0:T(8,128)} async-done(((f32[384,2304]{1,0:T(8,128)}), f32[3072,2304]{1,0:T(8,128)}) %all-gather.49.cloned.1.call-update) | async-done | bytes 28311568 | tf_op jit(solution)/shard_map/all_gather | solution.py:19
  3769.1 46.1 while.94
  3825.9 15.3 reduce-scatter.56.cloned.1.call-done
  3870.8 18.1 reduce-scatter.58.cloned.1.call-done
  3929.5 16.8 all_gather.221
  4003.1 56.9 %all-gather.17 = f32[8,1,2304]{2,1,0:T(1,128)S(1)} all-gather(f32[1,1,2304]{2,1,0:T(1,128)S(1)} %reshape.931), channel_id=13, replica_groups=mesh['section'=2,'seq'=8,'head'=2] {'seq'}, dimensions={0}, use_global_device_ids=true | all-gather | bytes 82944 | tf_op jit(solution)/shard_map/all_gather | solution.py:19
  4064.1 458.6 %all-gather.51.cloned.1.call-done = f32[3072,2304]{1,0:T(8,128)} async-done(((f32[384,2304]{1,0:T(8,128)}), f32[3072,2304]{1,0:T(8,128)}) %all-gather.51.cloned.1.call-update) | async-done | bytes 28311568 | tf_op jit(solution)/shard_map/all_gather | solution.py:19
  4524.7 46.1 while.95
  4581.6 15.3 reduce-scatter.66.cloned.1.call-done
  4799.4 82.6 %reduce-scatter.72.cloned.1.call-done = f32[96,3,384]{2,0,1:T(8,128)} async-done(((f32[768,3,384]{2,0,1:T(8,128)}), f32[96,3,384]{2,0,1:T(8,128)}) %reduce-scatter.72.cloned.1.call-update) | async-done | bytes 442384 | tf_op jit(solution)/shard_map/reduce_scatter | solution.py:412
  4882.1 99.6 %reduce-scatter.78.cloned.1.call-done = f32[1536,96]{0,1:T(8,128)} async-done(((f32[1536,768]{0,1:T(8,128)}), f32[1536,96]{0,1:T(8,128)}) %reduce-scatter.78.cloned.1.call-update) | async-done | bytes 589840 | tf_op jit(solution)/shard_map/reduce_scatter | solution.py:416
  4981.7 99.8 %reduce-scatter.76.cloned.1.call-done = f32[96,1536]{1,0:T(8,128)} async-done(((f32[768,1536]{1,0:T(8,128)}), f32[96,1536]{1,0:T(8,128)}) %reduce-scatter.76.cloned.1.call-update) | async-done | bytes 589840 | tf_op jit(solution)/shard_map/reduce_scatter | solution.py:414
  5120.4 20.7 all-reduce.46
  5141.5 33.0 all-reduce.49
  5175.2 72.5 %all-reduce.47 = (f32[1,2,768]{2,1,0:T(2,128)}, f32[1,2,768]{2,1,0:T(2,128)}, f32[1,2,768]{2,1,0:T(2,128)}) all-reduce(f32[1,2,768]{2,1,0:T(2,128)S(1)} %fusion.508, f32[1,2,768]{2,1,0:T(2,128)S(1)} %fusion.511, f32[1,2,768]{2,1,0:T(2,128)S(1)} %fusion.514), channel_id=1, replica_groups=mesh['section'=2,'seq'=8,'head'=2] {'seq','head'}, use_global_device_ids=true, to_apply=%region_101.104 | all-reduce | flops 4608 | bytes 36864 | tf_op jit(solution)/shard_map/psum | solution.py:431
  5249.6 30.9 all-gather.18
  5283.8 13.8 all-gather.31.cloned.1.call-done
  5297.6 80.6 %all-gather.37.cloned.1.call-done = f32[1536,768]{0,1:T(8,128)} async-done(((f32[1536,96]{0,1:T(8,128)}), f32[1536,768]{0,1:T(8,128)}) %all-gather.37.cloned.1.call-update) | async-done | bytes 4718608 | tf_op jit(solution)/shard_map/all_gather | solution.py:425
  5384.3 74.4 %all-gather.35.cloned.1.call-done = f32[768,1536]{1,0:T(8,128)} async-done(((f32[96,1536]{1,0:T(8,128)}), f32[768,1536]{1,0:T(8,128)}) %all-gather.35.cloned.1.call-update) | async-done | bytes 4718608 | tf_op jit(solution)/shard_map/all_gather | solution.py:423
  5458.7 136.6 %all-reduce.53.cloned.1.call-done = (f32[1,768,384]{2,1,0:T(8,128)}, f32[1,768,384]{2,1,0:T(8,128)}) async-done(((f32[1,768,384]{2,1,0:T(8,128)}, f32[1,768,384]{2,1,0:T(8,128)}), (f32[1,768,384]{2,1,0:T(8,128)}, f32[1,768,384]{2,1,0:T(8,128)})) %all-reduce.53.cloned.1.call-update) | async-done | bytes 2359312 | tf_op jit(solution)/shard_map/psum | solution.py:431
  (1507 shorter events, 1236.3 us)
Async XLA Ops:
  7.2 61.2 %reduce-scatter.30.cloned.1.call-start = ((), (), s32[]{:S(2)}) async-start(), calls=%async_computation.33 | async-start | bytes 1253376 | tf_op jit(solution)/shard_map/reduce_scatter | solution.py:72
  48.8 63.6 %reduce-scatter.32.cloned.1.call-start = ((), (), s32[]{:S(2)}) async-start(), calls=%async_computation.34 | async-start | bytes 1253376 | tf_op jit(solution)/shard_map/reduce_scatter | solution.py:72
  94.2 580.8 %all-gather.41.cloned.1.call-start = ((), (), s32[]{:S(2)}) async-start(), calls=%async_computation.64 | async-start | bytes 31850496 | tf_op jit(solution)/shard_map/all_gather | solution.py:19
  133.4 667.7 %reduce-scatter.34.cloned.1.call-start = ((), (), s32[]{:S(2)}) async-start(), calls=%async_computation.35 | async-start | bytes 1253376 | tf_op jit(solution)/shard_map/reduce_scatter | solution.py:72
  696.5 2.9 collective-permute-start
  733.1 114.6 %reduce-scatter.36.cloned.1.call-start = ((), (), s32[]{:S(2)}) async-start(), calls=%async_computation.36 | async-start | bytes 1253376 | tf_op jit(solution)/shard_map/reduce_scatter | solution.py:72
  829.6 580.9 %all-gather.43.cloned.1.call-start = ((), (), s32[]{:S(2)}) async-start(), calls=%async_computation.65 | async-start | bytes 31850496 | tf_op jit(solution)/shard_map/all_gather | solution.py:19
  869.6 673.1 %reduce-scatter.42.cloned.1.call-start = ((), (), s32[]{:S(2)}) async-start(), calls=%async_computation.39 | async-start | bytes 1253376 | tf_op jit(solution)/shard_map/reduce_scatter | solution.py:72
  1431.8 2.8 collective-permute-start.1
  1437.0 1676.6 %copy-start.38 = (f32[128,768]{1,0:T(8,128)}, f32[128,768]{1,0:T(8,128)S(1)}, u32[]{:S(2)}) copy-start(f32[128,768]{1,0:T(8,128)S(1)} %get-tuple-element.827) | copy-start | bytes 1179652
  1473.0 111.5 %reduce-scatter.38.cloned.1.call-start = ((), (), s32[]{:S(2)}) async-start(), calls=%async_computation.37 | async-start | bytes 1253376 | tf_op jit(solution)/shard_map/reduce_scatter | solution.py:72
  1509.5 136.4 %reduce-scatter.40.cloned.1.call-start = ((), (), s32[]{:S(2)}) async-start(), calls=%async_computation.38 | async-start | bytes 1253376 | tf_op jit(solution)/shard_map/reduce_scatter | solution.py:72
  1616.4 47.6 reduce-scatter.44.cloned.1.call-start
  1645.8 582.6 %all-gather.45.cloned.1.call-start = ((), (), s32[]{:S(2)}) async-start(), calls=%async_computation.66 | async-start | bytes 31850496 | tf_op jit(solution)/shard_map/all_gather | solution.py:19
  1691.1 543.6 %all-to-all-start = ((f32[128,2,384]{2,0,1:T(8,128)}), f32[128,2,384]{2,0,1:T(8,128)}, u32[]{:S(2)}, u32[]{:S(2)}) async-start(f32[128,2,384]{2,0,1:T(8,128)} %copy.134), calls=%async_computation | async-start | bytes 786432 | tf_op jit(solution)/shard_map/all_to_all | solution.py:222
  1695.3 1140.3 %all-gather.47.cloned.1.call-start = ((), (), s32[]{:S(2)}) async-start(), calls=%async_computation.67 | async-start | bytes 31850496 | tf_op jit(solution)/shard_map/all_gather | solution.py:19
  2242.3 667.5 %reduce-scatter.46.cloned.1.call-start = ((), (), s32[]{:S(2)}) async-start(), calls=%async_computation.41 | async-start | bytes 1253376 | tf_op jit(solution)/shard_map/reduce_scatter | solution.py:72
  2894.5 63.0 %reduce-scatter.48.cloned.1.call-start = ((), (), s32[]{:S(2)}) async-start(), calls=%async_computation.42 | async-start | bytes 1253376 | tf_op jit(solution)/shard_map/reduce_scatter | solution.py:72
  2939.4 76.4 %reduce-scatter.50.cloned.1.call-start = ((), (), s32[]{:S(2)}) async-start(), calls=%async_computation.43 | async-start | bytes 1253376 | tf_op jit(solution)/shard_map/reduce_scatter | solution.py:72
  2997.7 97.8 %reduce-scatter.62.cloned.1.call-start = ((), (), s32[]{:S(2)}) async-start(), calls=%async_computation.49 | async-start | bytes 1253376 | tf_op jit(solution)/shard_map/reduce_scatter | solution.py:72
  3054.3 59.3 %reduce-scatter.52.cloned.1.call-start = ((), (), s32[]{:S(2)}) async-start(), calls=%async_computation.44 | async-start | bytes 1253376 | tf_op jit(solution)/shard_map/reduce_scatter | solution.py:72
  3095.5 91.5 %reduce-scatter.64.cloned.1.call-start = ((), (), s32[]{:S(2)}) async-start(), calls=%async_computation.50 | async-start | bytes 1253376 | tf_op jit(solution)/shard_map/reduce_scatter | solution.py:72
  3144.7 50.9 reduce-scatter.54.cloned.1.call-start
  3176.5 3.6 collective-permute-start.2
  3182.7 35.3 all-to-all-start.3
  3186.9 580.2 %all-gather.49.cloned.1.call-start = ((), (), s32[]{:S(2)}) async-start(), calls=%async_computation.68 | async-start | bytes 31850496 | tf_op jit(solution)/shard_map/all_gather | solution.py:19
  3225.7 615.5 %reduce-scatter.56.cloned.1.call-start = ((), (), s32[]{:S(2)}) async-start(), calls=%async_computation.46 | async-start | bytes 1253376 | tf_op jit(solution)/shard_map/reduce_scatter | solution.py:72
  3825.9 63.0 %reduce-scatter.58.cloned.1.call-start = ((), (), s32[]{:S(2)}) async-start(), calls=%async_computation.47 | async-start | bytes 1253376 | tf_op jit(solution)/shard_map/reduce_scatter | solution.py:72
  3870.8 81.8 %reduce-scatter.60.cloned.1.call-start = ((), (), s32[]{:S(2)}) async-start(), calls=%async_computation.48 | async-start | bytes 1253376 | tf_op jit(solution)/shard_map/reduce_scatter | solution.py:72
  3957.1 5.1 collective-permute-start.3
  3963.8 11.3 all-to-all-start.4
  3967.3 555.4 %all-gather.51.cloned.1.call-start = ((), (), s32[]{:S(2)}) async-start(), calls=%async_computation.69 | async-start | bytes 31850496 | tf_op jit(solution)/shard_map/all_gather | solution.py:19
  3981.7 615.2 %reduce-scatter.66.cloned.1.call-start = ((), (), s32[]{:S(2)}) async-start(), calls=%async_computation.51 | async-start | bytes 1253376 | tf_op jit(solution)/shard_map/reduce_scatter | solution.py:72
  4581.6 61.9 %reduce-scatter.68.cloned.1.call-start = ((), (), s32[]{:S(2)}) async-start(), calls=%async_computation.52 | async-start | bytes 1253376 | tf_op jit(solution)/shard_map/reduce_scatter | solution.py:72
  4625.4 157.7 %reduce-scatter.80.cloned.1.call-start = ((), (), s32[]{:S(2)}) async-start(), calls=%async_computation.62 | async-start | bytes 1327104 | tf_op jit(solution)/shard_map/reduce_scatter | solution.py:418
  4632.5 151.1 %reduce-scatter.70.cloned.1.call-start = ((), (), s32[]{:S(2)}) async-start(), calls=%async_computation.53 | async-start | bytes 1253376 | tf_op jit(solution)/shard_map/reduce_scatter | solution.py:72
  4681.3 118.0 %reduce-scatter.74.cloned.1.call-start = ((), (), s32[]{:S(2)}) async-start(), calls=%async_computation.56 | async-start | bytes 1327104 | tf_op jit(solution)/shard_map/reduce_scatter | solution.py:413
  4692.0 189.9 %reduce-scatter.72.cloned.1.call-start = ((), (), s32[]{:S(2)}) async-start(), calls=%async_computation.54 | async-start | bytes 3981312 | tf_op jit(solution)/shard_map/reduce_scatter | solution.py:412
  4725.9 255.7 %reduce-scatter.78.cloned.1.call-start = ((), (), s32[]{:S(2)}) async-start(), calls=%async_computation.60 | async-start | bytes 5308416 | tf_op jit(solution)/shard_map/reduce_scatter | solution.py:416
  4754.9 326.6 %reduce-scatter.76.cloned.1.call-start = ((), (), s32[]{:S(2)}) async-start(), calls=%async_computation.58 | async-start | bytes 5308416 | tf_op jit(solution)/shard_map/reduce_scatter | solution.py:414
  4782.9 392.2 %all-gather.39.cloned.1.call-start = ((), (), s32[]{:S(2)}) async-start(), calls=%async_computation.63 | async-start | bytes 1327104 | tf_op jit(solution)/shard_map/all_gather | solution.py:427
  4783.5 465.2 %reduce-scatter.82.cloned.1.call-start = ((), (), s32[]{:S(2)}) async-start(), calls=%async_computation.70 | async-start | bytes 442368
  4788.4 492.8 %all-gather.33.cloned.1.call-start = ((), (), s32[]{:S(2)}) async-start(), calls=%async_computation.57 | async-start | bytes 1327104 | tf_op jit(solution)/shard_map/all_gather | solution.py:422
  4799.3 498.3 %all-gather.31.cloned.1.call-start = ((), (), s32[]{:S(2)}) async-start(), calls=%async_computation.55 | async-start | bytes 3981312 | tf_op jit(solution)/shard_map/all_gather | solution.py:421
  4882.0 496.2 %all-gather.37.cloned.1.call-start = ((), (), s32[]{:S(2)}) async-start(), calls=%async_computation.61 | async-start | bytes 5308416 | tf_op jit(solution)/shard_map/all_gather | solution.py:425
  4981.6 477.1 %all-gather.35.cloned.1.call-start = ((), (), s32[]{:S(2)}) async-start(), calls=%async_computation.59 | async-start | bytes 5308416 | tf_op jit(solution)/shard_map/all_gather | solution.py:423
  5081.5 513.8 %all-reduce.53.cloned.1.call-start = ((), (), s32[]{:S(2)}) async-start(), calls=%async_computation.71 | async-start | bytes 4718592 | tf_op jit(solution)/shard_map/psum | solution.py:431
  5109.3 10.4 all-to-all-start.5
  (367 other events, 11455.6 us)
Sparse Core Ops, SparseCore 0:
  48.9 19.4 reduce-scatter.29
  94.3 17.9 reduce-scatter.31
  133.6 541.4 all-gather.40
  733.3 67.8 reduce-scatter.33
  829.8 17.9 reduce-scatter.35
  869.7 540.7 all-gather.42
  1473.2 69.4 reduce-scatter.41
  1545.6 38.9 reduce-scatter.37
  1616.5 21.6 reduce-scatter.39
  1645.9 17.9 reduce-scatter.43
  1687.5 540.8 all-gather.44
  2242.4 593.1 all-gather.46
  2894.6 15.1 reduce-scatter.45
  2939.6 17.9 reduce-scatter.47
  2997.8 17.9 reduce-scatter.49
  3054.4 21.4 reduce-scatter.61
  3095.6 17.9 reduce-scatter.51
  3144.8 21.4 reduce-scatter.63
  3175.2 20.2 reduce-scatter.53
  3225.8 541.2 all-gather.48
  3826.0 15.1 reduce-scatter.55
  3870.9 17.9 reduce-scatter.57
  3928.9 21.6 reduce-scatter.59
  3981.9 540.7 all-gather.50
  4581.7 15.1 reduce-scatter.65
  4625.5 17.9 reduce-scatter.67
  4647.3 64.1 reduce-scatter.79
  4713.8 16.9 reduce-scatter.69
  4735.1 64.1 reduce-scatter.73
  4803.8 78.1 reduce-scatter.71
  4886.6 94.9 reduce-scatter.77
  4986.3 95.1 reduce-scatter.75
  5083.8 40.7 all-gather.38
  5128.2 60.1 reduce-scatter.81
  5190.9 40.2 all-gather.32
  5233.4 64.1 all-gather.30
  5299.9 78.3 all-gather.36
  5380.7 78.0 all-gather.34
  5465.8 129.4 all-reduce.52
where the time goes:
time: 5630 us; the launch traced here: 5610 us
  waiting for transfers between devices  3690 us (66%)
  blocking collectives  919 us (16%)
  matrix products  551 us (10%)
  other arithmetic  213 us (4%)
  local copies, waits for them, and re-layouts  171 us (3%)
    all_gather x6, waiting for transfers between devices, entering(): gathered = jax.tree.map(lambda a: lax.all_gather(a, axis), part)  2720 us
    dot_general x111, matrix products, matmul(): jnp.dot(left_mat, right_mat, precision=HIGHEST_PRECISION, preferred_eleme...  480 us
    all_gather x6, blocking collectives, entering(): gathered = jax.tree.map(lambda a: lax.all_gather(a, axis), part)  380 us
    reduce_scatter x21, waiting for transfers between devices, collect_rows(): lax.psum_scatter(term_rows(), 'head', scatter_dimension=0, tiled=True)  354 us
    all_gather x24, blocking collectives, spread_rows(): return lax.all_gather(local_rows, 'head', axis=0, tiled=True)  315 us
    psum x1, waiting for transfers between devices, shards(): lax.psum((grad_gains, grad_biases, grad_residual, grad_query_w, grad_key_...  137 us
  transfers between devices with their start and end apart: 47, of which 35 were waited for; matrix products, arithmetic and copies ran while one was open for 7% of the time, Pallas kernels for 0%

commit v1 on v0

v1 whole, which is shorter than its diff:
```python
import math

import jax
import jax.numpy as jnp
from jax import lax
from jax.sharding import PartitionSpec as P

HEAD_DIM = 64
EPSILON = 1e-05
SCALE = 1.0 / math.sqrt(HEAD_DIM)


def mm(left, right, dims=((1,), (0,))):
    return lax.dot_general(
        left, right, (dims, ((), ())), precision=lax.Precision.HIGH, preferred_element_type=jnp.float32
    )


def mm_nt(left, right):
    return mm(left, right, ((1,), (1,)))


def mm_tn(left, right):
    return mm(left, right, ((0,), (0,)))


def unit_rows(rows):
    centred = rows - jnp.mean(rows, axis=-1, keepdims=True)
    inverse = lax.rsqrt(jnp.mean(centred * centred, axis=-1, keepdims=True) + EPSILON)
    return centred * inverse, inverse


def unit_rows_back(d_unit, unit, inverse):
    return inverse * (
        d_unit
        - jnp.mean(d_unit, axis=-1, keepdims=True)
        - unit * jnp.mean(d_unit * unit, axis=-1, keepdims=True)
    )


def features(projected):
    halves = jnp.concatenate([jax.nn.softplus(projected), jax.nn.softplus(-projected)], axis=-1)
    return jnp.concatenate(
        [halves * jnp.roll(halves, rolled_by, axis=-1) for rolled_by in (1, 2, 3)], axis=-1
    )


def gelu_tanh(values_in):
    return jax.nn.gelu(values_in, approximate=True)


def swap(value):
    return lax.ppermute(value, "head", [(0, 1), (1, 0)])


def head_sum(value):
    if lax.axis_size("head") == 2:
        return value + swap(value)
    return lax.psum(value, "head")


def head_sum_rows(rows, share):
    count = lax.axis_size("head")
    segment = count * share
    if count == 2:
        other = swap(rows)
        return rows + jnp.concatenate(
            [other[share:segment], other[:share], other[segment:]], axis=0
        )
    turn = lax.axis_index("head") * share
    total = lax.psum(
        jnp.concatenate([jnp.roll(rows[:segment], turn, axis=0), rows[segment:]], axis=0), "head"
    )
    return jnp.concatenate([jnp.roll(total[:segment], -turn, axis=0), total[segment:]], axis=0)


def head_rows(local):
    count = lax.axis_size("head")
    if count == 2:
        return jnp.concatenate([local, swap(local)], axis=0)
    gathered = lax.all_gather(local, "head", axis=0, tiled=True)
    return jnp.roll(gathered, -lax.axis_index("head") * local.shape[0], axis=0)


def head_scatter(rows):
    count = lax.axis_size("head")
    share = rows.shape[0] // count
    if count == 2:
        return rows[:share] + swap(rows[share:])
    placed = jnp.roll(rows, lax.axis_index("head") * share, axis=0)
    return lax.psum_scatter(placed, "head", scatter_dimension=0, tiled=True)


def head_columns(values):
    count = lax.axis_size("head")
    share = values.shape[1] // count
    place = lax.axis_index("head")
    if count == 2:
        own = lax.dynamic_slice_in_dim(values, place * share, share, 1)
        other = lax.dynamic_slice_in_dim(values, (1 - place) * share, share, 1)
        return own + swap(other)
    return lax.psum_scatter(values, "head", scatter_dimension=1, tiled=True)


def heads_of(part):
    return part.reshape(part.shape[0], -1, HEAD_DIM).transpose(1, 0, 2)


def rows_of(part):
    return part.transpose(1, 0, 2).reshape(part.shape[1], -1)


def bmm(left, right, left_dim, right_dim):
    return lax.dot_general(
        left,
        right,
        (((left_dim,), (right_dim,)), ((0,), (0,))),
        precision=lax.Precision.HIGH,
        preferred_element_type=jnp.float32,
    )


def layer_forward(local, params, mask, allowed):
    width = local.shape[1]
    local_count = local.shape[0]
    segment = lax.axis_size("head") * local_count
    rows = jnp.concatenate([head_rows(local), params["memory"]], axis=0)
    unit_one, inverse_one = unit_rows(rows)
    normed = unit_one * params["gains"][0] + params["biases"][0]
    projected = mm(normed, params["proj_in"]) + params["in_bias"]
    share = projected.shape[1] // 3
    query, key, value = (heads_of(projected[:, i * share : (i + 1) * share]) for i in range(3))
    scores = jnp.where(allowed, bmm(query, key, 2, 2) * SCALE, -1e30)
    row_top = jnp.max(scores, axis=-1, keepdims=True)
    exponent = jnp.exp(scores - row_top)
    soft = exponent / jnp.sum(exponent, axis=-1, keepdims=True)
    attended = rows_of(bmm(soft, value, 2, 1))
    hidden = rows + head_sum_rows(mm(attended, params["proj_out"]), local_count) + params["residual"][0]
    unit_two, inverse_two = unit_rows(hidden)
    mixed = unit_two * params["gains"][1] + params["biases"][1]
    inner_pre = mm(mixed, params["up"]) + params["up_bias"]
    inner_act = gelu_tanh(inner_pre)
    partial = mm(inner_act, params["down"])
    out_local = head_scatter(partial[:segment]) + hidden[:local_count] + params["residual"][1]
    out_mem = head_sum(partial[segment:]) + hidden[segment:] + params["residual"][1]
    key_proj = mm(out_mem, params["key_mem"])
    values = mm(out_mem, params["value_mem"])
    gathered = lax.all_gather(jnp.concatenate([key_proj, values], axis=1), "seq", axis=0, tiled=True)
    dk = key_proj.shape[1]
    keys_all = gathered[:, :dk]
    values_all = lax.all_gather(gathered[:, dk:], "head", axis=1, tiled=True)
    key_feats = features(keys_all)
    query_proj = mm(out_local, params["query_mem"])
    query_feats = features(query_proj)
    weights = mask * mm_nt(query_feats, key_feats)
    denominator = jnp.sum(weights, axis=1, keepdims=True) + 1.0
    read = mm(weights, values_all) / denominator
    return dict(
        unit_one=unit_one,
        inverse_one=inverse_one,
        projected=projected,
        attended=attended,
        soft=soft,
        unit_two=unit_two,
        inverse_two=inverse_two,
        inner_pre=inner_pre,
        out_local=out_local,
        out_mem=out_mem,
        keys_all=keys_all,
        values_all=values_all,
        query_proj=query_proj,
        weights=weights,
        denominator=denominator,
        read=read,
        output=out_local + read,
    )


def layer_backward(grad, record, params, mask):
    head_count = lax.axis_size("head")
    seq_count = lax.axis_size("seq")
    width = grad.shape[1]
    local_count = grad.shape[0]
    segment = head_count * local_count
    denominator = record["denominator"]
    d_numer = grad / denominator
    d_denom = -jnp.sum(grad * record["read"], axis=1, keepdims=True) / denominator
    d_weights = mask * (mm_nt(d_numer, record["values_all"]) + d_denom)
    key_feats, keys_back = jax.vjp(features, record["keys_all"])
    query_feats, query_back = jax.vjp(features, record["query_proj"])
    d_query_proj = query_back(mm(d_weights, key_feats))[0]
    d_keys = keys_back(mm_tn(d_weights, query_feats))[0]
    d_values = mm_tn(record["weights"], d_numer)
    d_memory = lax.psum_scatter(
        jnp.concatenate([d_keys, d_values], axis=1), "seq", scatter_dimension=0, tiled=True
    )
    dk = d_keys.shape[1]
    d_key_proj = d_memory[:, :dk]
    d_value = head_columns(d_memory[:, dk:])
    d_mem = head_sum(mm_nt(d_key_proj, params["key_mem"]) + mm_nt(d_value, params["value_mem"]))
    d_local = grad + mm_nt(d_query_proj, params["query_mem"])
    d_result = jnp.concatenate([head_rows(d_local), d_mem], axis=0)
    inner_act, gelu_back = jax.vjp(gelu_tanh, record["inner_pre"])
    grad_down = mm_tn(inner_act, d_result)
    d_pre = gelu_back(mm_nt(d_result, params["down"]))[0]
    gains, biases = params["gains"], params["biases"]
    mixed = record["unit_two"] * gains[1] + biases[1]
    grad_up = mm_tn(mixed, d_pre)
    d_mixed = head_sum_rows(mm_nt(d_pre, params["up"]), local_count)
    d_hidden = d_result + unit_rows_back(d_mixed * gains[1], record["unit_two"], record["inverse_two"])
    grad_out = mm_tn(record["attended"], d_hidden)
    d_attended = mm_nt(d_hidden, params["proj_out"])
    share = d_attended.shape[1]
    query, key, value = (
        heads_of(record["projected"][:, i * share : (i + 1) * share]) for i in range(3)
    )
    soft = record["soft"]
    d_heads = heads_of(d_attended)
    inner_dot = jnp.sum(d_heads * heads_of(record["attended"]), axis=-1, keepdims=True)
    d_scores = soft * (bmm(d_heads, value, 2, 2) - inner_dot) * SCALE
    d_projected = jnp.concatenate(
        [
            rows_of(bmm(d_scores, key, 2, 1)),
            rows_of(bmm(d_scores, query, 1, 1)),
            rows_of(bmm(soft, d_heads, 1, 1)),
        ],
        axis=1,
    )
    normed = record["unit_one"] * gains[0] + biases[0]
    grad_in = mm_tn(normed, d_projected)
    columns = jnp.sum(d_projected, axis=0)
    grad_head_bias = jnp.stack([columns[:share], columns[2 * share :]])
    d_normed_all = mm_nt(d_projected, params["proj_in"])
    d_normed = head_scatter(d_normed_all[:segment])
    d_normed_mem = lax.psum_scatter(
        d_normed_all[segment:], "head", scatter_dimension=0, tiled=True
    )
    mem_count = d_normed_mem.shape[0]
    own_mem = segment + lax.axis_index("head") * mem_count

    def own(values):
        return jnp.concatenate(
            [values[:local_count], lax.dynamic_slice_in_dim(values, own_mem, mem_count, 0)], axis=0
        )

    d_normed_own = jnp.concatenate([d_normed, d_normed_mem], axis=0)
    unit_own = own(record["unit_one"])
    d_rows = own(d_hidden) + unit_rows_back(
        d_normed_own * gains[0], unit_own, own(record["inverse_one"])
    )
    part = 1.0 / head_count
    sharded = (
        grad_in,
        grad_head_bias,
        grad_out,
        grad_up,
        jnp.sum(d_pre, axis=0),
        grad_down,
        d_rows[local_count:],
        mm_tn(record["out_mem"], d_value),
    )
    shared = (
        jnp.stack(
            [
                jnp.sum(d_normed_own * unit_own, axis=0),
                part * jnp.sum(d_mixed * record["unit_two"], axis=0),
            ]
        ),
        jnp.stack([jnp.sum(d_normed_own, axis=0), part * jnp.sum(d_mixed, axis=0)]),
        part * jnp.stack([jnp.sum(d_hidden, axis=0), jnp.sum(d_result, axis=0)]),
        mm_tn(record["out_local"], d_query_proj),
        mm_tn(record["out_mem"], d_key_proj),
    )
    return (d_rows[:local_count], sharded, shared)


def passed_along(value, axis, steps):
    count = lax.axis_size(axis)
    first, last = (max(0, -steps), min(count, count - steps))
    return lax.ppermute(value, axis, [(source, source + steps) for source in range(first, last)])


def shards(
    boundary_in,
    short_items,
    norm_gains,
    norm_biases,
    projection_in,
    head_bias,
    projection_out,
    residual_bias,
    up_weight,
    up_bias,
    down_weight,
    memory_tokens,
    query_memory,
    key_memory,
    value_memory,
):
    section = lax.axis_index("section")
    sections = lax.axis_size("section")
    head_count = lax.axis_size("head")
    head_place = lax.axis_index("head")
    seq_count = lax.axis_size("seq")
    seq_place = lax.axis_index("seq")
    micro_total = boundary_in.shape[1]
    local_count = boundary_in.shape[2]
    width = boundary_in.shape[3]
    segment = head_count * local_count
    head_width = projection_in.shape[3]
    memory_all = lax.all_gather(memory_tokens[0], "head", axis=0, tiled=True)
    mem_count = memory_all.shape[0]
    params = dict(
        gains=norm_gains[0],
        biases=norm_biases[0],
        proj_in=projection_in[0].reshape(width, 3 * head_width),
        in_bias=jnp.concatenate(
            [head_bias[0, 0], jnp.zeros((head_width,), jnp.float32), head_bias[0, 1]]
        ),
        proj_out=projection_out[0],
        residual=residual_bias[0],
        up=up_weight[0],
        up_bias=up_bias[0],
        down=down_weight[0],
        memory=memory_all,
        query_mem=query_memory[0],
        key_mem=key_memory[0],
        value_mem=value_memory[0],
    )
    ordinal = jnp.arange(segment)
    places = jnp.concatenate(
        [(ordinal + head_place * local_count) % segment, segment + jnp.arange(mem_count)]
    )
    allowed = (places[:, None] >= places[None, :])[None]

    positions = jnp.arange(seq_count)
    masks = []
    for micro in range(micro_total):
        if micro == 0:
            item = jnp.zeros((seq_count,), jnp.int32)
        else:
            ends = jnp.cumsum(short_items[micro - 1])
            item = jnp.sum((positions[:, None] >= ends[None, :]).astype(jnp.int32), axis=1)
        own_item = jnp.sum(jnp.where(positions == seq_place, item, 0))
        seen = jnp.logical_and(positions < seq_place, item == own_item).astype(jnp.float32)
        masks.append(jnp.repeat(seen, mem_count)[None, :])
    masks = jnp.stack(masks)

    tick_total = micro_total + sections - 1
    received = jnp.zeros_like(boundary_in[0, 0])
    records = []
    for tick in range(tick_total):
        micro = jnp.clip(tick - section, 0, micro_total - 1)
        local = jnp.where(section == 0, boundary_in[0, min(tick, micro_total - 1)], received)
        records.append(layer_forward(local, params, masks[micro], allowed))
        if tick + 1 < tick_total:
            received = passed_along(records[-1]["output"], "section", 1)
    back_received = jnp.zeros_like(boundary_in[0, 0])
    grads_input = []
    total = None
    for tick in range(tick_total):
        raw = tick - (sections - 1 - section)
        valid = jnp.logical_and(raw >= 0, raw < micro_total)
        micro = jnp.clip(raw, 0, micro_total - 1)
        grad = jnp.where(
            section == sections - 1, boundary_in[0, min(tick, micro_total - 1)], back_received
        )
        record = jax.tree.map(
            lambda *kinds: lax.select_n(section, *kinds),
            *[
                records[min(max(tick - (sections - 1 - place), 0), micro_total - 1) + place]
                for place in range(sections)
            ],
        )
        grad_x, sharded, shared = layer_backward(grad, record, params, masks[micro])
        fresh = jax.tree.map(lambda part: jnp.where(valid, part, 0.0), (sharded, shared))
        total = fresh if total is None else jax.tree.map(jnp.add, total, fresh)
        grads_input.append(grad_x)
        if tick + 1 < tick_total:
            back_received = passed_along(grad_x, "section", -1)
    sharded, shared = total
    grad_in, grad_heads_bias, grad_out, grad_up, grad_up_b, grad_down, grad_mem, grad_value = lax.psum(
        sharded, "seq"
    )
    grad_gains, grad_biases, grad_residual, grad_query, grad_key = lax.psum(shared, ("seq", "head"))
    finished_grads = jnp.stack(
        [grads_input[micro + sections - 1] for micro in range(micro_total)]
    )
    finished_outputs = jnp.stack(
        [records[micro + sections - 1]["output"] for micro in range(micro_total)]
    )
    boundary_out = jnp.where(section == 0, finished_grads, finished_outputs)[None]
    return (
        boundary_out,
        grad_gains[None],
        grad_biases[None],
        grad_in.reshape(projection_in.shape),
        grad_heads_bias[None],
        grad_out[None],
        grad_residual[None],
        grad_up[None],
        grad_up_b[None],
        grad_down[None],
        grad_mem[None],
        grad_query[None],
        grad_key[None],
        grad_value[None],
    )


def solution(mesh):
    return jax.shard_map(
        shards,
        mesh=mesh,
        in_specs=(
            P("section", None, ("seq", "head"), None),
            P(),
            P("section", None, None),
            P("section", None, None),
            P("section", None, None, "head"),
            P("section", None, "head"),
            P("section", "head", None),
            P("section", None, None),
            P("section", None, "head"),
            P("section", "head"),
            P("section", "head", None),
            P("section", "head", None),
            P("section", None, None),
            P("section", None, None),
            P("section", None, "head"),
        ),
        out_specs=(
            P("section", None, ("seq", "head"), None),
            P("section", None, None),
            P("section", None, None),
            P("section", None, None, "head"),
            P("section", None, "head"),
            P("section", "head", None),
            P("section", None, None),
            P("section", None, "head"),
            P("section", "head"),
            P("section", "head", None),
            P("section", "head", None),
            P("section", None, None),
            P("section", None, None),
            P("section", None, "head"),
        ),
        check_vma=False,
    )
```

time: 5630 us -> 1460 us (0.26)
  waiting for transfers between devices: 3690 us -> 691 us
  blocking collectives: 919 us -> 234 us
  matrix products: 551 us -> 251 us
  other arithmetic: 213 us -> 80.4 us
    all_gather x11 -> x0, waiting for transfers between devices: 2890 us -> none  [the longest x6 2720 us: entering(): gathered = jax.tree.map(lambda a: lax.all_gather(a, axis), part)]
    all_gather x31 -> x7, blocking collectives: 727 us -> 119 us  [the longest x3 93.9 us: layer_forward(): lax.all_gather(jnp.concatenate([key_proj, values], axis=1), 'seq', axis=0...]
    reduce_scatter x26 -> x6, waiting for transfers between devices: 647 us -> 148 us  [the longest x3 142 us: layer_backward(): lax.psum_scatter(jnp.concatenate([d_keys, d_values], axis=1), 'seq', scat...]
    psum x1 -> x2, waiting for transfers between devices: 137 us -> 443 us  [the longest x1 311 us: shards(): lax.psum(sharded, 'seq')]
    dot_general x135 -> x99, matrix products: 551 us -> 251 us  [the longest x81 215 us: mm(): lax.dot_general(left, right, (dims, ((), ())), precision=lax.Precision.HI...]
    add x69 -> x14, other arithmetic: 123 us -> 3.87 us  [the longest x3 2.97 us: layer_backward(): own(d_hidden)]
    ppermute x0 -> x27, waiting for transfers between devices: none -> 96.3 us  [swap(): return lax.ppermute(value, 'head', [(0, 1), (1, 0)])]
    unnamed x2 -> x0, blocking collectives: 68.3 us -> none
  transfers between devices with their start and end apart: 47 -> 39, of which waited for: 35 -> 27; matrix products, arithmetic and copies ran while one was open for 7% -> 16% of each run, Pallas kernels for 0% -> 0%
where the time goes in v1:
time: 1460 us; the launch traced here: 1450 us
  waiting for transfers between devices  691 us (47%)
  matrix products  251 us (17%)
  blocking collectives  234 us (16%)
  local copies, waits for them, and re-layouts  137 us (9%)
  other arithmetic  80.4 us (6%)
  starting transfers between devices  37.5 us (3%)
  between operations  20.8 us (1%)
    psum x1, waiting for transfers between devices, shards(): lax.psum(sharded, 'seq')  311 us
    dot_general x81, matrix products, mm(): lax.dot_general(left, right, (dims, ((), ())), precision=lax.Precision.HI...  215 us
    reduce_scatter x3, waiting for transfers between devices, layer_backward(): lax.psum_scatter(jnp.concatenate([d_keys, d_values], axis=1), 'seq', scat...  142 us
    psum x1, waiting for transfers between devices, shards(): lax.psum(shared, ('seq', 'head'))  133 us
    ppermute x27, waiting for transfers between devices, swap(): return lax.ppermute(value, 'head', [(0, 1), (1, 0)])  96.3 us
    all_gather x3, blocking collectives, layer_forward(): lax.all_gather(jnp.concatenate([key_proj, values], axis=1), 'seq', axis=0...  93.9 us
    psum x1, blocking collectives, shards(): lax.psum(shared, ('seq', 'head'))  77 us
    unnamed x909, local copies, waits for them, and re-layouts  48.8 us
  transfers between devices with their start and end apart: 39, of which 27 were waited for; matrix products, arithmetic and copies ran while one was open for 16% of the time, Pallas kernels for 0%

profile of v1, /device:TPU:0, one launch (start us, length us, event | category | flops | bytes accessed | tf_op | source)
XLA Modules:
  0.0 1451.6 jit_solution(15375712908665711855)
XLA Ops:
  12.3 5.2 copy.99
  17.4 4.5 all-gather
  22.6 3.9 convolution_add_fusion.2
  42.2 16.9 %collective-permute-done.1 = f32[272,768]{1,0:T(8,128)} collective-permute-done((f32[272,768]{1,0:T(8,128)}, f32[272,768]{1,0:T(8,128)}, u32[]{:S(2)}, u32[]{:S(2)}) %collective-permute-start.1) | collective-permute-done | bytes 835616 | tf_op jit(solution)/shard_map/ppermute | solution.py:53
  62.9 5.2 fusion.26
  68.2 3.1 fusion.10
  76.9 31.5 %all_gather.22 = f32[128,768]{1,0:T(8,128)S(1)} all-gather(f32[16,768]{1,0:T(8,128)S(1)} %pad_maximum_fusion.60), channel_id=1, replica_groups=mesh['section'=2,'seq'=8,'head'=2] {'seq'}, dimensions={0}, use_global_device_ids=true | all-gather | bytes 442368 | tf_op jit(solution)/shard_map/all_gather | solution.py:148
  108.8 6.3 all_gather.23
  124.3 10.7 collective-permute-done.5
  153.6 19.3 %collective-permute-done.6 = f32[272,768]{1,0:T(8,128)S(1)} collective-permute-done((f32[272,768]{1,0:T(8,128)S(1)}, f32[272,768]{1,0:T(8,128)S(1)}, u32[]{:S(2)}, u32[]{:S(2)}) %collective-permute-start.6) | collective-permute-done | bytes 835616 | tf_op jit(solution)/shard_map/ppermute | solution.py:53
  177.1 15.2 %fusion.8 = f32[272,768]{1,0:T(8,128)S(1)} fusion(f32[1,1536,768]{2,1,0:T(8,128)S(1)} %bitcast.390, f32[272,1536]{1,0:T(8,128)S(1)} %fusion.29), kind=kOutput, calls=%fused_computation.8 | convolution fusion | flops 1928527872 | bytes 7225344 | tf_op jit(solution)/shard_map/dot_general | solution.py:14
  197.9 31.1 %all_gather.24 = f32[128,768]{1,0:T(8,128)S(1)} all-gather(f32[16,768]{1,0:T(8,128)S(1)} %pad_maximum_fusion.61), channel_id=1, replica_groups=mesh['section'=2,'seq'=8,'head'=2] {'seq'}, dimensions={0}, use_global_device_ids=true | all-gather | bytes 442368 | tf_op jit(solution)/shard_map/all_gather | solution.py:148
  229.3 6.3 all_gather.25
  248.9 7.4 collective-permute-done.16
  257.3 4.0 broadcast_select_fusion.12
  306.7 6.0 fusion.32
  320.5 31.3 %all_gather.26 = f32[128,768]{1,0:T(8,128)S(1)} all-gather(f32[16,768]{1,0:T(8,128)S(1)} %pad_maximum_fusion.62), channel_id=1, replica_groups=mesh['section'=2,'seq'=8,'head'=2] {'seq'}, dimensions={0}, use_global_device_ids=true | all-gather | bytes 442368 | tf_op jit(solution)/shard_map/all_gather | solution.py:148
  366.8 7.9 all_gather.27
  388.4 41.6 %reduce-scatter.7.cloned.1.call-done = f32[16,1152]{1,0:T(8,128)} async-done(((f32[128,1152]{1,0:T(8,128)}), f32[16,1152]{1,0:T(8,128)}) %reduce-scatter.7.cloned.1.call-update) | async-done | bytes 73744 | tf_op jit(solution)/shard_map/reduce_scatter | solution.py:194
  440.1 6.2 fusion.650
  452.9 12.0 collective-permute-done.12
  518.5 56.3 %reduce-scatter.11.cloned.1.call-done = f32[16,1152]{1,0:T(8,128)} async-done(((f32[128,1152]{1,0:T(8,128)}), f32[16,1152]{1,0:T(8,128)}) %reduce-scatter.11.cloned.1.call-update) | async-done | bytes 73744 | tf_op jit(solution)/shard_map/reduce_scatter | solution.py:194
  585.0 6.3 fusion.649
  597.2 7.7 fusion.89
  605.0 5.7 fusion.255
  640.7 4.5 reduce-scatter.13.cloned.1.call-done
  651.2 7.0 fusion.87
  658.3 6.6 convolution_select_fusion.1
  675.5 3.8 fusion.105
  679.3 5.7 fusion.252
  685.1 6.7 fusion.24
  694.3 43.7 %reduce-scatter.15.cloned.1.call-done = f32[16,1152]{1,0:T(8,128)} async-done(((f32[128,1152]{1,0:T(8,128)}), f32[16,1152]{1,0:T(8,128)}) %reduce-scatter.15.cloned.1.call-update) | async-done | bytes 73744 | tf_op jit(solution)/shard_map/reduce_scatter | solution.py:194
  745.6 3.1 fusion.111
  749.4 6.3 fusion.648
  758.9 7.9 add_bitcast_fusion
  766.8 8.7 collective-permute-done.29
  793.8 9.4 fusion.25
  803.3 8.1 add_bitcast_fusion.1
  813.5 5.2 copy.133
  832.5 3.1 convolution_select_fusion.4
  836.8 3.0 fusion.114
  856.7 5.4 collective-permute-done.30
  865.2 38.2 %all-reduce.38 = (f32[1,2,384]{2,1,0:T(2,128)}, f32[1,1536]{1,0:T(1,128)}, f32[1,8,768]{2,1,0:T(8,128)}) all-reduce(f32[1,2,384]{2,1,0:T(2,128)S(1)} %fusion.528, f32[1,1536]{1,0:T(1,128)S(1)} %broadcast_in_dim.199, f32[1,8,768]{2,1,0:T(8,128)S(1)} %fusion.500), channel_id=1, replica_groups=mesh['section'=2,'seq'=8,'head'=2] {'seq'}, use_global_device_ids=true, to_apply=%region_69.71 | all-reduce | flops 8448 | bytes 67584 | tf_op jit(solution)/shard_map/psum | solution.py:382
  903.6 77.0 %all-reduce.36 = (f32[1,2,768]{2,1,0:T(2,128)}, f32[1,2,768]{2,1,0:T(2,128)}, f32[1,2,768]{2,1,0:T(2,128)}) all-reduce(f32[1,2,768]{2,1,0:T(2,128)S(1)} %fusion.510, f32[1,2,768]{2,1,0:T(2,128)S(1)} %fusion.513, f32[1,2,768]{2,1,0:T(2,128)S(1)} %fusion.519), channel_id=1, replica_groups=mesh['section'=2,'seq'=8,'head'=2] {'seq','head'}, use_global_device_ids=true, to_apply=%region_54.56 | all-reduce | flops 4608 | bytes 36864 | tf_op jit(solution)/shard_map/psum | solution.py:385
  982.5 310.5 %all-reduce.45.cloned.1.call-done = (f32[1,768,3,384]{1,3,2,0:T(8,128)}, f32[1,384,768]{2,1,0:T(8,128)}, f32[1,768,1536]{2,1,0:T(8,128)}, f32[1,1536,768]{2,1,0:T(8,128)}, f32[1,768,384]{2,1,0:T(8,128)}) async-done(((f32[1,768,3,384]{1,3,2,0:T(8,128)}, f32[1,384,768]{2,1,0:T(8,128)}, f32[1,768,1536]{2,1,0:T(8,128)}, f32[1,1536,768]{2,1,0:T(8,128)}, f32[1,768,384]{2,1,0:T(8,128)}), ...) | async-done | bytes 15335440 | tf_op jit(solution)/shard_map/psum | solution.py:382
  1293.1 5.2 copy.134
  1298.3 132.8 %all-reduce.43.cloned.1.call-done = (f32[1,768,384]{2,1,0:T(8,128)}, f32[1,768,384]{2,1,0:T(8,128)}) async-done(((f32[1,768,384]{2,1,0:T(8,128)}, f32[1,768,384]{2,1,0:T(8,128)}), (f32[1,768,384]{2,1,0:T(8,128)}, f32[1,768,384]{2,1,0:T(8,128)})) %all-reduce.43.cloned.1.call-update) | async-done | bytes 2359312 | tf_op jit(solution)/shard_map/psum | solution.py:385
  1432.2 5.5 copy.159
  (1444 shorter events, 371.8 us)
Async XLA Ops:
  7.2 422.8 %reduce-scatter.7.cloned.1.call-start = ((), (), s32[]{:S(2)}) async-start(), calls=%async_computation.6 | async-start | bytes 663552 | tf_op jit(solution)/shard_map/reduce_scatter | solution.py:194
  8.4 52.7 %copy-start.37 = (f32[128,768]{1,0:T(8,128)}, f32[128,768]{1,0:T(8,128)S(1)}, u32[]{:S(2)}) copy-start(f32[128,768]{1,0:T(8,128)S(1)} %select_bitcast_fusion) | copy-start | bytes 1179652
  8.4 13.7 collective-permute-start
  39.4 19.7 %collective-permute-start.1 = (f32[272,768]{1,0:T(8,128)}, f32[272,768]{1,0:T(8,128)}, u32[]{:S(2)}, u32[]{:S(2)}) collective-permute-start(f32[272,768]{1,0:T(8,128)} %fusion.221), channel_id=1, source_target_pairs={{0,1},{1,0},{2,3},{3,2},{4,5},{5,4},{6,7},{7,6},{8,9},{9,8},{10,11... | collective-permute-start | bytes 2506760 | tf_op jit(solution)/shard_map/ppermute | solution.py:53
  62.6 53.3 %copy-start.31 = (f32[272,768]{1,0:T(8,128)}, f32[272,768]{1,0:T(8,128)S(1)}, u32[]{:S(2)}) copy-start(f32[272,768]{1,0:T(8,128)S(1)} %get-tuple-element.183) | copy-start | bytes 2506756
  71.3 4.7 collective-permute-start.3
  72.9 42.9 %collective-permute-start.2 = (f32[128,768]{1,0:T(8,128)S(1)}, f32[128,768]{1,0:T(8,128)S(1)}, u32[]{:S(2)}, u32[]{:S(2)}) collective-permute-start(f32[128,768]{1,0:T(8,128)S(1)} %slice.828), channel_id=1, source_target_pairs={{0,1},{1,0},{2,3},{3,2},{4,5},{5,4},{6,7},{7,6},{8,9},{9,8},{10,11... | collective-permute-start | bytes 1179656 | tf_op jit(solution)/shard_map/ppermute | solution.py:53
  120.7 2.7 collective-permute-start.4
  123.5 11.5 collective-permute-start.5
  152.8 20.1 %collective-permute-start.6 = (f32[272,768]{1,0:T(8,128)S(1)}, f32[272,768]{1,0:T(8,128)S(1)}, u32[]{:S(2)}, u32[]{:S(2)}) collective-permute-start(f32[272,768]{1,0:T(8,128)S(1)} %fusion.219), channel_id=1, source_target_pairs={{0,1},{1,0},{2,3},{3,2},{4,5},{5,4},{6,7},{7,6},{8,9},{9,8},{10,11... | collective-permute-start | bytes 2506760 | tf_op jit(solution)/shard_map/ppermute | solution.py:53
  173.3 63.0 %copy-start.28 = (f32[272,768]{1,0:T(8,128)}, f32[272,768]{1,0:T(8,128)S(1)}, u32[]{:S(2)}) copy-start(f32[272,768]{1,0:T(8,128)S(1)} %get-tuple-element.181) | copy-start | bytes 2506756
  192.3 4.7 collective-permute-start.8
  193.1 43.2 %collective-permute-start.7 = (f32[128,768]{1,0:T(8,128)S(1)}, f32[128,768]{1,0:T(8,128)S(1)}, u32[]{:S(2)}, u32[]{:S(2)}) collective-permute-start(f32[128,768]{1,0:T(8,128)S(1)} %slice.859), channel_id=1, source_target_pairs={{0,1},{1,0},{2,3},{3,2},{4,5},{5,4},{6,7},{7,6},{8,9},{9,8},{10,11... | collective-permute-start | bytes 1179656 | tf_op jit(solution)/shard_map/ppermute | solution.py:53
  240.6 2.8 collective-permute-start.15
  244.7 11.6 collective-permute-start.16
  275.3 26.8 %collective-permute-start.17 = (f32[272,768]{1,0:T(8,128)}, f32[272,768]{1,0:T(8,128)}, u32[]{:S(2)}, u32[]{:S(2)}) collective-permute-start(f32[272,768]{1,0:T(8,128)} %fusion.217), channel_id=1, source_target_pairs={{0,1},{1,0},{2,3},{3,2},{4,5},{5,4},{6,7},{7,6},{8,9},{9,8},{10,11... | collective-permute-start | bytes 2506760 | tf_op jit(solution)/shard_map/ppermute | solution.py:53
  305.8 52.0 %copy-start.34 = (f32[272,768]{1,0:T(8,128)}, f32[272,768]{1,0:T(8,128)S(1)}, u32[]{:S(2)}) copy-start(f32[272,768]{1,0:T(8,128)S(1)} %get-tuple-element.179) | copy-start | bytes 2506756
  315.5 4.2 collective-permute-start.19
  318.3 39.4 %collective-permute-start.18 = (f32[128,768]{1,0:T(8,128)S(1)}, f32[128,768]{1,0:T(8,128)S(1)}, u32[]{:S(2)}, u32[]{:S(2)}) collective-permute-start(f32[128,768]{1,0:T(8,128)S(1)} %slice.922), channel_id=1, source_target_pairs={{0,1},{1,0},{2,3},{3,2},{4,5},{5,4},{6,7},{7,6},{8,9},{9,8},{10,11... | collective-permute-start | bytes 1179656 | tf_op jit(solution)/shard_map/ppermute | solution.py:53
  366.7 128.8 %reduce-scatter.9.cloned.1.call-start = ((), (), s32[]{:S(2)}) async-start(), calls=%async_computation.7 | async-start | bytes 73728 | tf_op jit(solution)/shard_map/reduce_scatter | solution.py:235
  387.8 52.3 %collective-permute-start.9 = (f32[128,768]{1,0:T(8,128)}, f32[128,768]{1,0:T(8,128)}, u32[]{:S(2)}, u32[]{:S(2)}) collective-permute-start(f32[128,768]{1,0:T(8,128)} %get-tuple-element.355), channel_id=1, source_target_pairs={{0,1},{1,0},{2,3},{3,2},{4,5},{5,4},{6,7},{7,6},{8,9},{9,8},{10,11... | collective-permute-start | bytes 1179656 | tf_op jit(solution)/shard_map/ppermute | solution.py:53
  430.9 3.9 collective-permute-start.10
  435.4 4.2 collective-permute-start.11
  448.6 16.3 %collective-permute-start.12 = (f32[272,768]{1,0:T(8,128)S(1)}, f32[272,768]{1,0:T(8,128)S(1)}, u32[]{:S(2)}, u32[]{:S(2)}) collective-permute-start(f32[272,768]{1,0:T(8,128)S(1)} %fusion.18), channel_id=1, source_target_pairs={{0,1},{1,0},{2,3},{3,2},{4,5},{5,4},{6,7},{7,6},{8,9},{9,8},{10,11... | collective-permute-start | bytes 2506760 | tf_op jit(solution)/shard_map/ppermute | solution.py:53
  452.7 51.0 %copy-start.416 = (f32[128]{0:T(128)}, f32[128]{0:T(128)S(1)}, u32[]{:S(2)}) copy-start(f32[128]{0:T(128)S(1)} %get-tuple-element.341) | copy-start | bytes 1540
  483.1 8.1 collective-permute-start.13
  487.3 87.4 %reduce-scatter.11.cloned.1.call-start = ((), (), s32[]{:S(2)}) async-start(), calls=%async_computation.8 | async-start | bytes 663552 | tf_op jit(solution)/shard_map/reduce_scatter | solution.py:194
  499.8 3.7 collective-permute-start.14
  512.3 132.9 %reduce-scatter.13.cloned.1.call-start = ((), (), s32[]{:S(2)}) async-start(), calls=%async_computation.9 | async-start | bytes 73728 | tf_op jit(solution)/shard_map/reduce_scatter | solution.py:235
  516.0 75.3 %slice-start.4 = ((s8[4718592]{0:T(1024)(128)(4,1)}), s8[524288]{0:T(1024)(128)(4,1)S(1)}, s32[]{:S(2)}) async-start(s8[4718592]{0:T(1024)(128)(4,1)} %bitcast.383), calls=%async_computation.18 | async-start | bytes 1048576
  518.3 66.7 %collective-permute-start.20 = (f32[128,768]{1,0:T(8,128)}, f32[128,768]{1,0:T(8,128)}, u32[]{:S(2)}, u32[]{:S(2)}) collective-permute-start(f32[128,768]{1,0:T(8,128)} %get-tuple-element.353), channel_id=1, source_target_pairs={{0,1},{1,0},{2,3},{3,2},{4,5},{5,4},{6,7},{7,6},{8,9},{9,8},{10,11... | collective-permute-start | bytes 1179656 | tf_op jit(solution)/shard_map/ppermute | solution.py:53
  575.7 3.9 collective-permute-start.21
  580.2 4.2 collective-permute-start.22
  593.6 17.1 %collective-permute-start.23 = (f32[272,768]{1,0:T(8,128)S(1)}, f32[272,768]{1,0:T(8,128)S(1)}, u32[]{:S(2)}, u32[]{:S(2)}) collective-permute-start(f32[272,768]{1,0:T(8,128)S(1)} %fusion.14), channel_id=1, source_target_pairs={{0,1},{1,0},{2,3},{3,2},{4,5},{5,4},{6,7},{7,6},{8,9},{9,8},{10,11... | collective-permute-start | bytes 2506760 | tf_op jit(solution)/shard_map/ppermute | solution.py:53
  630.1 8.1 collective-permute-start.24
  636.1 101.9 %reduce-scatter.15.cloned.1.call-start = ((), (), s32[]{:S(2)}) async-start(), calls=%async_computation.10 | async-start | bytes 663552 | tf_op jit(solution)/shard_map/reduce_scatter | solution.py:194
  649.7 15.2 %collective-permute-start.25 = (f32[128,768]{1,0:T(8,128)S(1)}, f32[128,768]{1,0:T(8,128)S(1)}, u32[]{:S(2)}, u32[]{:S(2)}) collective-permute-start(f32[128,768]{1,0:T(8,128)S(1)} %get-tuple-element.247), channel_id=1, source_target_pairs={{16,0},{17,1},{18,2},{19,3},{20,4},{21,5},{22,6},{23,7},{24,8},{25... | collective-permute-start | bytes 1179656 | tf_op jit(solution)/shard_map/ppermute | solution.py:280
  675.0 180.8 %reduce-scatter.17.cloned.1.call-start = ((), (), s32[]{:S(2)}) async-start(), calls=%async_computation.11 | async-start | bytes 73728 | tf_op jit(solution)/shard_map/reduce_scatter | solution.py:235
  694.1 55.2 %collective-permute-start.26 = (f32[128,768]{1,0:T(8,128)}, f32[128,768]{1,0:T(8,128)}, u32[]{:S(2)}, u32[]{:S(2)}) collective-permute-start(f32[128,768]{1,0:T(8,128)} %get-tuple-element.351), channel_id=1, source_target_pairs={{0,1},{1,0},{2,3},{3,2},{4,5},{5,4},{6,7},{7,6},{8,9},{9,8},{10,11... | collective-permute-start | bytes 1179656 | tf_op jit(solution)/shard_map/ppermute | solution.py:53
  738.9 3.9 collective-permute-start.27
  743.3 5.4 collective-permute-start.28
  758.2 17.2 %collective-permute-start.29 = (f32[272,768]{1,0:T(8,128)S(1)}, f32[272,768]{1,0:T(8,128)S(1)}, u32[]{:S(2)}, u32[]{:S(2)}) collective-permute-start(f32[272,768]{1,0:T(8,128)S(1)} %fusion.12), channel_id=1, source_target_pairs={{0,1},{1,0},{2,3},{3,2},{4,5},{5,4},{6,7},{7,6},{8,9},{9,8},{10,11... | collective-permute-start | bytes 2506760 | tf_op jit(solution)/shard_map/ppermute | solution.py:53
  793.5 499.5 %all-reduce.45.cloned.1.call-start = ((), (), s32[]{:S(2)}) async-start(), calls=%async_computation.13 | async-start | bytes 30670848 | tf_op jit(solution)/shard_map/psum | solution.py:382
  818.8 612.4 %all-reduce.43.cloned.1.call-start = ((), (), s32[]{:S(2)}) async-start(), calls=%async_computation.12 | async-start | bytes 4718592 | tf_op jit(solution)/shard_map/psum | solution.py:385
  854.1 8.1 collective-permute-start.30
  863.2 117.3 %copy-start.222 = (f32[128,768]{1,0:T(8,128)S(1)}, f32[128,768]{1,0:T(8,128)}, u32[]{:S(2)}) copy-start(f32[128,768]{1,0:T(8,128)} %copy-done.221) | copy-start | bytes 1179652
  863.2 117.3 %copy-start.223 = (f32[1,1,128,768]{3,2,1,0:T(8,128)S(1)}, f32[1,1,128,768]{3,2,1,0:T(8,128)}, u32[]{:S(2)}) copy-start(f32[1,1,128,768]{3,2,1,0:T(8,128)} %get-tuple-element.246) | copy-start | bytes 1179652
  1293.1 138.1 %copy-start.248 = (f32[1,384,768]{2,1,0:T(8,128)S(1)}, f32[1,384,768]{2,1,0:T(8,128)}, u32[]{:S(2)}) copy-start(f32[1,384,768]{2,1,0:T(8,128)} %get-tuple-element.369) | copy-start | bytes 3538948
  (441 other events, 2834.0 us)
Sparse Core Ops, SparseCore 0:
  366.8 63.1 reduce-scatter.6
  487.5 8.0 reduce-scatter.8
  512.5 62.2 reduce-scatter.10
  636.3 8.8 reduce-scatter.12
  675.1 62.8 reduce-scatter.14
  793.7 8.0 reduce-scatter.16
  818.8 474.2 all-reduce.44
  1300.8 130.2 all-reduce.42

commit v2 on v1

--- a/solution.py
+++ b/solution.py
@@ -1,13 +1,19 @@
+import functools
 import math
 
 import jax
 import jax.numpy as jnp
 from jax import lax
+from jax.experimental import pallas as pl
+from jax.experimental.pallas import tpu as pltpu
 from jax.sharding import PartitionSpec as P
 
 HEAD_DIM = 64
 EPSILON = 1e-05
 SCALE = 1.0 / math.sqrt(HEAD_DIM)
+MESH = pl.DeviceIdType.MESH
+VMEM = pl.BlockSpec(memory_space=pltpu.VMEM)
+HBM = pl.BlockSpec(memory_space=pltpu.HBM)
 
 
 def mm(left, right, dims=((1,), (0,))):
@@ -49,21 +55,362 @@
     return jax.nn.gelu(values_in, approximate=True)
 
 
-def swap(value):
-    return lax.ppermute(value, "head", [(0, 1), (1, 0)])
-
-
-def head_sum(value):
+def barrier_with(pairs, wait_count):
+    barrier = pltpu.get_barrier_semaphore()
+    for condition, device in pairs:
+
+        @pl.when(condition)
+        def _(device=device):
+            pl.semaphore_signal(barrier, inc=1, device_id=device, device_id_type=MESH)
+
+    @pl.when(wait_count > 0)
+    def _():
+        pl.semaphore_wait(barrier, wait_count)
+
+
+def runs_in(active):
+    section = lax.axis_index("section")
+    if len(active) == 1:
+        return section == active[0]
+    return section >= 0
+
+
+def gather_kernel(active, block, keys, values, send_k, send_v, recv_k, recv_v):
+    seq = lax.axis_index("seq")
+    head = lax.axis_index("head")
+    seqs, heads = lax.axis_size("seq"), lax.axis_size("head")
+    mem = block.shape[0]
+    dk = keys.shape[1]
+    dv = values.shape[1] // heads
+    keys[...] = jnp.zeros_like(keys)
+    values[...] = jnp.zeros_like(values)
+
+    def key_copy(source, target):
+        return pltpu.make_async_remote_copy(
+            src_ref=block.at[:, pl.ds(0, dk)],
+            dst_ref=keys.at[pl.ds(pl.multiple_of(source * mem, mem), mem)],
+            send_sem=send_k.at[target],
+            recv_sem=recv_k.at[source],
+            device_id={"seq": target},
+            device_id_type=MESH,
+        )
+
+    def value_copy(source, source_head, target, target_head):
+        return pltpu.make_async_remote_copy(
+            src_ref=block.at[:, pl.ds(dk, dv)],
+            dst_ref=values.at[
+                pl.ds(pl.multiple_of(source * mem, mem), mem),
+                pl.ds(pl.multiple_of(source_head * dv, 128), dv),
+            ],
+            send_sem=send_v.at[target, target_head],
+            recv_sem=recv_v.at[source, source_head],
+            device_id={"seq": target, "head": target_head},
+            device_id_type=MESH,
+        )
+
+    @pl.when(runs_in(active))
+    def _():
+        barrier_with(
+            [
+                (other < seq, {"seq": other, "head": place})
+                for other in range(seqs)
+                for place in range(heads)
+            ],
+            (seqs - 1 - seq) * heads,
+        )
+        for other in range(seqs):
+
+            @pl.when(other > seq)
+            def _(other=other):
+                key_copy(seq, other).start()
+                for place in range(heads):
+                    value_copy(seq, head, other, place).start()
+
+        for other in range(seqs):
+
+            @pl.when(other < seq)
+            def _(other=other):
+                key_copy(other, other).wait_recv()
+                for place in range(heads):
+                    value_copy(other, place, other, place).wait_recv()
+
+        for other in range(seqs):
+
+            @pl.when(other > seq)
+            def _(other=other):
+                key_copy(seq, other).wait_send()
+                for place in range(heads):
+                    value_copy(seq, head, other, place).wait_send()
+
+
+def gather_memory(key_proj, values, active, number):
+    seqs, heads = lax.axis_size("seq"), lax.axis_size("head")
+    mem, dk = key_proj.shape
+    dv = values.shape[1]
+    if heads != 2:
+        return (
+            lax.all_gather(key_proj, "seq", axis=0, tiled=True),
+            lax.all_gather(
+                lax.all_gather(values, "seq", axis=0, tiled=True), "head", axis=1, tiled=True
+            ),
+        )
+    return pl.pallas_call(
+        functools.partial(gather_kernel, active),
+        out_shape=(
+            jax.ShapeDtypeStruct((seqs * mem, dk), jnp.float32),
+            jax.ShapeDtypeStruct((seqs * mem, heads * dv), jnp.float32),
+        ),
+        in_specs=[VMEM],
+        out_specs=(VMEM, VMEM),
+        scratch_shapes=[
+            pltpu.SemaphoreType.DMA((seqs,)),
+            pltpu.SemaphoreType.DMA((seqs, heads)),
+            pltpu.SemaphoreType.DMA((seqs,)),
+            pltpu.SemaphoreType.DMA((seqs, heads)),
+        ],
+        compiler_params=pltpu.CompilerParams(collective_id=number, has_side_effects=True),
+    )(jnp.concatenate([key_proj, values], axis=1))
+
+
+def scatter_kernel(active, d_keys, d_values, out_k, out_v, from_k, from_v, send_k, send_v, recv_k, recv_v):
+    seq = lax.axis_index("seq")
+    head = lax.axis_index("head")
+    seqs, heads = lax.axis_size("seq"), lax.axis_size("head")
+    mem, dk = out_k.shape
+    dv = out_v.shape[1]
+    from_k[...] = jnp.zeros_like(from_k)
+    from_v[...] = jnp.zeros_like(from_v)
+
+    def key_copy(source, target):
+        return pltpu.make_async_remote_copy(
+            src_ref=d_keys.at[pl.ds(pl.multiple_of(target * mem, mem), mem)],
+            dst_ref=from_k.at[source],
+            send_sem=send_k.at[target],
+            recv_sem=recv_k.at[source],
+            device_id={"seq": target},
+            device_id_type=MESH,
+        )
+
+    def value_copy(source, source_head, target, target_head):
+        return pltpu.make_async_remote_copy(
+            src_ref=d_values.at[
+                pl.ds(pl.multiple_of(target * mem, mem), mem),
+                pl.ds(pl.multiple_of(target_head * dv, 128), dv),
+            ],
+            dst_ref=from_v.at[source, source_head],
+            send_sem=send_v.at[target, target_head],
+            recv_sem=recv_v.at[source, source_head],
+            device_id={"seq": target, "head": target_head},
+            device_id_type=MESH,
+        )
+
+    @pl.when(runs_in(active))
+    def _():
+        barrier_with(
+            [
+                (other > seq, {"seq": other, "head": place})
+                for other in range(seqs)
+                for place in range(heads)
+            ],
+            seq * heads,
+        )
+        for other in range(seqs):
+
+            @pl.when(other < seq)
+            def _(other=other):
+                key_copy(seq, other).start()
+                for place in range(heads):
+                    value_copy(seq, head, other, place).start()
+
+        for other in range(seqs):
+
+            @pl.when(other > seq)
+            def _(other=other):
+                key_copy(other, other).wait_recv()
+                for place in range(heads):
+                    value_copy(other, place, other, place).wait_recv()
+
+        for other in range(seqs):
+
+            @pl.when(other < seq)
+            def _(other=other):
+                key_copy(seq, other).wait_send()
+                for place in range(heads):
+                    value_copy(seq, head, other, place).wait_send()
+
+    out_k[...] = jnp.sum(from_k[...], axis=0)
+    out_v[...] = jnp.sum(from_v[...], axis=(0, 1))
+
+
+def scatter_memory(d_keys, d_values, active, number):
+    seqs, heads = lax.axis_size("seq"), lax.axis_size("head")
+    mem = d_keys.shape[0] // seqs
+    dk = d_keys.shape[1]
+    dv = d_values.shape[1] // heads
+    if heads != 2:
+        d_values = lax.psum_scatter(d_values, "head", scatter_dimension=1, tiled=True)
+        return (
+            lax.psum_scatter(d_keys, "seq", scatter_dimension=0, tiled=True),
+            lax.psum_scatter(d_values, "seq", scatter_dimension=0, tiled=True),
+        )
+    return pl.pallas_call(
+        functools.partial(scatter_kernel, active),
+        out_shape=(
+            jax.ShapeDtypeStruct((mem, dk), jnp.float32),
+            jax.ShapeDtypeStruct((mem, dv), jnp.float32),
+        ),
+        in_specs=[VMEM, VMEM],
+        out_specs=(VMEM, VMEM),
+        scratch_shapes=[
+            pltpu.VMEM((seqs, mem, dk), jnp.float32),
+            pltpu.VMEM((seqs, heads, mem, dv), jnp.float32),
+            pltpu.SemaphoreType.DMA((seqs,)),
+            pltpu.SemaphoreType.DMA((seqs, heads)),
+            pltpu.SemaphoreType.DMA((seqs,)),
+            pltpu.SemaphoreType.DMA((seqs, heads)),
+        ],
+        compiler_params=pltpu.CompilerParams(collective_id=number, has_side_effects=True),
+    )(d_keys, d_values)
+
+
+def ring_kernel(active, lanes, count, aliased, *refs):
+    arrays = refs[:count]
+    refs = refs[count + (count if aliased else 0) :]
+    sums = refs[:count]
+    held = refs[count : 2 * count]
+    send, recv, local = refs[2 * count :]
+    seqs = lax.axis_size("seq")
+    along = seqs // lanes
+    seq = lax.axis_index("seq")
+    z, y = seq // lanes, lax.rem(seq, lanes)
+    place = y * along + jnp.where(lax.rem(y, 2) == 0, z, along - 1 - z)
+
+    def device(spot):
+        row = spot // along
+        column = lax.rem(spot, along)
+        column = jnp.where(lax.rem(row, 2) == 0, column, along - 1 - column)
+        return {"seq": column * lanes + row}
+
+    targets = (device(lax.rem(place + 1, seqs)), device(lax.rem(place + seqs - 1, seqs)))
+    signs = (1, -1)
+
+    def block(ref, way, spot):
+        rows = ref.shape[0] // seqs
+        half = rows // 2
+        spot = lax.rem(spot + 2 * seqs, seqs)
+        return ref.at[pl.ds(pl.multiple_of(spot * rows + way * half, half), half)]
+
+    def copy(source, target, way, index, step):
+        return pltpu.make_async_remote_copy(
+            src_ref=source,
+            dst_ref=target,
+            send_sem=send.at[step, way, index],
+            recv_sem=recv.at[step, way, index],
+            device_id=targets[way],
+            device_id_type=MESH,
+        )
+
+    ways = [(index, way) for index in range(count) for way in range(2)]
+    last = seqs - 2
+
+    @pl.when(runs_in(active))
+    def _():
+        barrier_with([(place >= 0, targets[0]), (place >= 0, targets[1])], place * 0 + 2)
+        for index, way in ways:
+            copy(block(arrays[index], way, place), held[index].at[way, 0], way, index, 0).start()
+
+        def forward(step, carry):
+            for index, way in ways:
+                got = held[index].at[way, step - 1]
+                copy(got, got, way, index, step - 1).wait_recv()
+                got[...] += block(arrays[index], way, place - signs[way] * step)[...]
+                copy(got, held[index].at[way, step], way, index, step).start()
+            return carry
+
+        lax.fori_loop(1, seqs - 1, forward, 0)
+        for index, way in ways:
+            got = held[index].at[way, last]
+            copy(got, got, way, index, last).wait_recv()
+            spot = place + signs[way]
+            got[...] += block(arrays[index], way, spot)[...]
+            home = block(sums[index], way, spot)
+            copy(got, home, way, index, seqs - 1).start()
+            pltpu.make_async_copy(got, home, local.at[way, index]).start()
+
+        def onward(step, carry):
+            for index, way in ways:
+                got = block(sums[index], way, place - signs[way] * (step - 1))
+                copy(got, got, way, index, seqs - 1 + step - 1).wait_recv()
+                copy(got, got, way, index, seqs - 1 + step).start()
+            return carry
+
+        lax.fori_loop(1, seqs - 1, onward, 0)
+        for index, way in ways:
+            got = block(sums[index], way, place - signs[way] * last)
+            copy(got, got, way, index, 2 * seqs - 3).wait_recv()
+            own = held[index].at[way, last]
+            pltpu.make_async_copy(
+                own, block(sums[index], way, place + signs[way]), local.at[way, index]
+            ).wait()
+
+        def sent(step, carry):
+            for index, way in ways:
+                own = held[index].at[way, 0]
+                copy(own, own, way, index, step).wait_send()
+            return carry
+
+        lax.fori_loop(0, 2 * seqs - 2, sent, 0)
+
+
+def ring_sum(arrays, before, active, lanes, number):
+    seqs = lax.axis_size("seq")
+    count = len(arrays)
+    aliased = before is not None
+    if lax.axis_size("head") != 2:
+        sums = tuple(lax.psum(a, "seq") for a in arrays)
+        if not aliased:
+            return sums
+        return tuple(jnp.where(runs_in(active), a, b) for a, b in zip(sums, before))
+    shapes = tuple(jax.ShapeDtypeStruct(a.shape, a.dtype) for a in arrays)
+    nbytes = sum(a.size * 4 for a in arrays)
+    return pl.pallas_call(
+        functools.partial(ring_kernel, active, lanes, count, aliased),
+        out_shape=shapes,
+        in_specs=[VMEM] * count + ([HBM] * count if aliased else []),
+        out_specs=(HBM,) * count,
+        input_output_aliases={count + i: i for i in range(count)} if aliased else {},
+        scratch_shapes=[
+            pltpu.VMEM((2, seqs - 1, a.shape[0] // (2 * seqs), a.shape[1]), jnp.float32)
+            for a in arrays
+        ]
+        + [
+            pltpu.SemaphoreType.DMA((2 * seqs - 2, 2, count)),
+            pltpu.SemaphoreType.DMA((2 * seqs - 2, 2, count)),
+            pltpu.SemaphoreType.DMA((2, count)),
+        ],
+        compiler_params=pltpu.CompilerParams(
+            collective_id=number, has_side_effects=True, vmem_limit_bytes=48 << 20
+        ),
+        cost_estimate=pl.CostEstimate(flops=0, bytes_accessed=20 * nbytes, transcendentals=0),
+    )(*arrays, *(before or ()))
+
+
+def swap(value, active):
+    pairs = [(2 * s + h, 2 * s + 1 - h) for s in active for h in range(2)]
+    return lax.ppermute(value, ("section", "head"), pairs)
+
+
+def head_sum(value, active):
     if lax.axis_size("head") == 2:
-        return value + swap(value)
+        return value + swap(value, active)
     return lax.psum(value, "head")
 
 
-def head_sum_rows(rows, share):
+def head_sum_rows(rows, share, active):
     count = lax.axis_size("head")
     segment = count * share
     if count == 2:
-        other = swap(rows)
+        other = swap(rows, active)
         return rows + jnp.concatenate(
             [other[share:segment], other[:share], other[segment:]], axis=0
         )
@@ -74,32 +421,21 @@
     return jnp.concatenate([jnp.roll(total[:segment], -turn, axis=0), total[segment:]], axis=0)
 
 
-def head_rows(local):
+def head_rows(local, active):
     count = lax.axis_size("head")
     if count == 2:
-        return jnp.concatenate([local, swap(local)], axis=0)
+        return jnp.concatenate([local, swap(local, active)], axis=0)
     gathered = lax.all_gather(local, "head", axis=0, tiled=True)
     return jnp.roll(gathered, -lax.axis_index("head") * local.shape[0], axis=0)
 
 
-def head_scatter(rows):
+def head_scatter(rows, active):
     count = lax.axis_size("head")
     share = rows.shape[0] // count
     if count == 2:
-        return rows[:share] + swap(rows[share:])
+        return rows[:share] + swap(rows[share:], active)
     placed = jnp.roll(rows, lax.axis_index("head") * share, axis=0)
     return lax.psum_scatter(placed, "head", scatter_dimension=0, tiled=True)
-
-
-def head_columns(values):
-    count = lax.axis_size("head")
-    share = values.shape[1] // count
-    place = lax.axis_index("head")
-    if count == 2:
-        own = lax.dynamic_slice_in_dim(values, place * share, share, 1)
-        other = lax.dynamic_slice_in_dim(values, (1 - place) * share, share, 1)
-        return own + swap(other)
-    return lax.psum_scatter(values, "head", scatter_dimension=1, tiled=True)
 
 
 def heads_of(part):
@@ -120,11 +456,11 @@
     )
 
 
-def layer_forward(local, params, mask, allowed):
+def layer_forward(local, params, mask, allowed, active, tick):
     width = local.shape[1]
     local_count = local.shape[0]
     segment = lax.axis_size("head") * local_count
-    rows = jnp.concatenate([head_rows(local), params["memory"]], axis=0)
+    rows = jnp.concatenate([head_rows(local, active), params["memory"]], axis=0)
     unit_one, inverse_one = unit_rows(rows)
     normed = unit_one * params["gains"][0] + params["biases"][0]
     projected = mm(normed, params["proj_in"]) + params["in_bias"]
@@ -135,20 +471,17 @@
     exponent = jnp.exp(scores - row_top)
     soft = exponent / jnp.sum(exponent, axis=-1, keepdims=True)
     attended = rows_of(bmm(soft, value, 2, 1))
-    hidden = rows + head_sum_rows(mm(attended, params["proj_out"]), local_count) + params["residual"][0]
+    hidden = rows + head_sum_rows(mm(attended, params["proj_out"]), local_count, active) + params["residual"][0]
     unit_two, inverse_two = unit_rows(hidden)
     mixed = unit_two * params["gains"][1] + params["biases"][1]
     inner_pre = mm(mixed, params["up"]) + params["up_bias"]
     inner_act = gelu_tanh(inner_pre)
     partial = mm(inner_act, params["down"])
-    out_local = head_scatter(partial[:segment]) + hidden[:local_count] + params["residual"][1]
-    out_mem = head_sum(partial[segment:]) + hidden[segment:] + params["residual"][1]
+    out_local = head_scatter(partial[:segment], active) + hidden[:local_count] + params["residual"][1]
+    out_mem = head_sum(partial[segment:], active) + hidden[segment:] + params["residual"][1]
     key_proj = mm(out_mem, params["key_mem"])
     values = mm(out_mem, params["value_mem"])
-    gathered = lax.all_gather(jnp.concatenate([key_proj, values], axis=1), "seq", axis=0, tiled=True)
-    dk = key_proj.shape[1]
-    keys_all = gathered[:, :dk]
-    values_all = lax.all_gather(gathered[:, dk:], "head", axis=1, tiled=True)
+    keys_all, values_all = gather_memory(key_proj, values, active, tick)
     key_feats = features(keys_all)
     query_proj = mm(out_local, params["query_mem"])
     query_feats = features(query_proj)
@@ -176,10 +509,9 @@
     )
 
 
-def layer_backward(grad, record, params, mask):
+def layer_backward(grad, record, params, mask, active, tick):
     head_count = lax.axis_size("head")
-    seq_count = lax.axis_size("seq")
-    width = grad.shape[1]
+    rows_total = record["unit_one"].shape[0]
     local_count = grad.shape[0]
     segment = head_count * local_count
     denominator = record["denominator"]
@@ -191,22 +523,17 @@
     d_query_proj = query_back(mm(d_weights, key_feats))[0]
     d_keys = keys_back(mm_tn(d_weights, query_feats))[0]
     d_values = mm_tn(record["weights"], d_numer)
-    d_memory = lax.psum_scatter(
-        jnp.concatenate([d_keys, d_values], axis=1), "seq", scatter_dimension=0, tiled=True
-    )
-    dk = d_keys.shape[1]
-    d_key_proj = d_memory[:, :dk]
-    d_value = head_columns(d_memory[:, dk:])
-    d_mem = head_sum(mm_nt(d_key_proj, params["key_mem"]) + mm_nt(d_value, params["value_mem"]))
+    d_key_proj, d_value = scatter_memory(d_keys, d_values, active, tick)
+    d_mem = head_sum(mm_nt(d_key_proj, params["key_mem"]) + mm_nt(d_value, params["value_mem"]), active)
     d_local = grad + mm_nt(d_query_proj, params["query_mem"])
-    d_result = jnp.concatenate([head_rows(d_local), d_mem], axis=0)
+    d_result = jnp.concatenate([head_rows(d_local, active), d_mem], axis=0)
     inner_act, gelu_back = jax.vjp(gelu_tanh, record["inner_pre"])
     grad_down = mm_tn(inner_act, d_result)
     d_pre = gelu_back(mm_nt(d_result, params["down"]))[0]
     gains, biases = params["gains"], params["biases"]
     mixed = record["unit_two"] * gains[1] + biases[1]
     grad_up = mm_tn(mixed, d_pre)
-    d_mixed = head_sum_rows(mm_nt(d_pre, params["up"]), local_count)
+    d_mixed = head_sum_rows(mm_nt(d_pre, params["up"]), local_count, active)
     d_hidden = d_result + unit_rows_back(d_mixed * gains[1], record["unit_two"], record["inverse_two"])
     grad_out = mm_tn(record["attended"], d_hidden)
     d_attended = mm_nt(d_hidden, params["proj_out"])
@@ -231,12 +558,13 @@
     columns = jnp.sum(d_projected, axis=0)
     grad_head_bias = jnp.stack([columns[:share], columns[2 * share :]])
     d_normed_all = mm_nt(d_projected, params["proj_in"])
-    d_normed = head_scatter(d_normed_all[:segment])
-    d_normed_mem = lax.psum_scatter(
-        d_normed_all[segment:], "head", scatter_dimension=0, tiled=True
-    )
-    mem_count = d_normed_mem.shape[0]
-    own_mem = segment + lax.axis_index("head") * mem_count
+    d_normed = head_scatter(d_normed_all[:segment], active)
+    mem_count = (rows_total - segment) // head_count
+    own_mem = lax.axis_index("head") * mem_count
+    d_normed_mem = lax.dynamic_slice_in_dim(
+        head_sum(d_normed_all[segment:], active), own_mem, mem_count, 0
+    )
+    own_mem = segment + own_mem
 
     def own(values):
         return jnp.concatenate(
@@ -278,6 +606,45 @@
     count = lax.axis_size(axis)
     first, last = (max(0, -steps), min(count, count - steps))
     return lax.ppermute(value, axis, [(source, source + steps) for source in range(first, last)])
+
+
+def pack_gradients(sharded, shared, active):
+    grad_in, grad_heads_bias, grad_out, grad_up, grad_up_b, grad_down, grad_mem, grad_value = sharded
+    gains, biases, residual, grad_query, grad_key = shared
+    first = lax.axis_index("head") == 0
+    few = (gains, biases, residual)
+    few_flat = jnp.concatenate([part.reshape(-1) for part in few]).reshape(-1, 128)
+    few_flat = head_sum(few_flat, active)
+    if lax.axis_size("head") == 2:
+        own_whole = jnp.where(first, grad_query, grad_key)
+        own_whole = own_whole + swap(jnp.where(first, grad_key, grad_query), active)
+    else:
+        own_whole = lax.psum(jnp.concatenate([grad_query, grad_key], axis=0), "head")
+    rest = (grad_heads_bias, grad_up_b, grad_mem)
+    small = jnp.concatenate([few_flat] + [part.reshape(-1, 128) for part in rest], axis=0)
+    unit = 16 * lax.axis_size("seq")
+    small_rows = small.shape[0]
+    small = jnp.pad(small, ((0, -small_rows % unit), (0, 0)))
+    arrays = (grad_down, grad_up, grad_out, grad_in, grad_value, own_whole, small)
+
+    def unpack(finished):
+        down, up, out, proj_in, value, whole, small = finished
+        if lax.axis_size("head") == 2:
+            other = swap(whole, range(lax.axis_size("section")))
+            query, key = jnp.where(first, whole, other), jnp.where(first, other, whole)
+        else:
+            query, key = jnp.split(whole, 2, axis=0)
+        parts, at = [], 0
+        for part in few + rest:
+            rows = part.size // 128
+            parts.append(small[at : at + rows].reshape(part.shape))
+            at += rows
+        gains, biases, residual, heads_bias, up_b, mem = parts
+        return (
+            proj_in, heads_bias, out, up, up_b, down, mem, value, gains, biases, residual, query, key
+        )
+
+    return arrays, unpack
 
 
 def shards(
@@ -352,12 +719,14 @@
     for tick in range(tick_total):
         micro = jnp.clip(tick - section, 0, micro_total - 1)
         local = jnp.where(section == 0, boundary_in[0, min(tick, micro_total - 1)], received)
-        records.append(layer_forward(local, params, masks[micro], allowed))
+        active = [place for place in range(sections) if 0 <= tick - place < micro_total]
+        records.append(layer_forward(local, params, masks[micro], allowed, active, tick))
         if tick + 1 < tick_total:
             received = passed_along(records[-1]["output"], "section", 1)
     back_received = jnp.zeros_like(boundary_in[0, 0])
     grads_input = []
     total = None
+    finished = None
     for tick in range(tick_total):
         raw = tick - (sections - 1 - section)
         valid = jnp.logical_and(raw >= 0, raw < micro_total)
@@ -372,17 +741,38 @@
                 for place in range(sections)
             ],
         )
-        grad_x, sharded, shared = layer_backward(grad, record, params, masks[micro])
+        active = [
+            place for place in range(sections) if 0 <= tick - (sections - 1 - place) < micro_total
+        ]
+        grad_x, sharded, shared = layer_backward(
+            grad, record, params, masks[micro], active, tick_total + tick
+        )
         fresh = jax.tree.map(lambda part: jnp.where(valid, part, 0.0), (sharded, shared))
         total = fresh if total is None else jax.tree.map(jnp.add, total, fresh)
         grads_input.append(grad_x)
         if tick + 1 < tick_total:
             back_received = passed_along(grad_x, "section", -1)
-    sharded, shared = total
-    grad_in, grad_heads_bias, grad_out, grad_up, grad_up_b, grad_down, grad_mem, grad_value = lax.psum(
-        sharded, "seq"
-    )
-    grad_gains, grad_biases, grad_residual, grad_query, grad_key = lax.psum(shared, ("seq", "head"))
+        if tick >= micro_total - 1:
+            done = sections - 1 - (tick - (micro_total - 1))
+            arrays, unpack = pack_gradients(*total, [done])
+            finished = ring_sum(arrays, finished, [done], head_count, 2 * tick_total + done)
+            if tick + 1 < tick_total:
+                back_received, finished = lax.optimization_barrier((back_received, finished))
+    (
+        grad_in,
+        grad_heads_bias,
+        grad_out,
+        grad_up,
+        grad_up_b,
+        grad_down,
+        grad_mem,
+        grad_value,
+        grad_gains,
+        grad_biases,
+        grad_residual,
+        grad_query,
+        grad_key,
+    ) = unpack(finished)
     finished_grads = jnp.stack(
         [grads_input[micro + sections - 1] for micro in range(micro_total)]
     )

time: 1460 us -> 937 us (0.64)
  waiting for transfers between devices: 691 us -> 80.7 us
  Pallas kernels: 0 us -> 255 us
  blocking collectives: 234 us -> 4.49 us
  other arithmetic: 80.4 us -> 113 us
  starting transfers between devices: 37.5 us -> 65.7 us
  local copies, waits for them, and re-layouts: 137 us -> 164 us
  matrix products: 251 us -> 235 us
    psum x2 -> x0, waiting for transfers between devices: 443 us -> none  [the longest x1 311 us: shards(): lax.psum(sharded, 'seq')]
    pallas_call x0 -> x8, Pallas kernels: none -> 255 us  [the longest x2 190 us: ring_sum(): pl.pallas_call(functools.partial(ring_kernel, active, lanes, count, alias...]
    reduce_scatter x6 -> x0, waiting for transfers between devices: 148 us -> none  [the longest x3 142 us: layer_backward(): lax.psum_scatter(jnp.concatenate([d_keys, d_values], axis=1), 'seq', scat...]
    psum x2 -> x0, blocking collectives: 115 us -> none  [the longest x1 77 us: shards(): lax.psum(shared, ('seq', 'head'))]
    all_gather x6 -> x0, blocking collectives: 115 us -> none  [the longest x3 93.9 us: layer_forward(): lax.all_gather(jnp.concatenate([key_proj, values], axis=1), 'seq', axis=0...]
    ppermute x27 -> x32, waiting for transfers between devices: 96.3 us -> 47 us  [swap(): return lax.ppermute(value, ('section', 'head'), pairs)]
    ppermute x4, waiting for transfers between devices: 3.38 us -> 33.7 us  [passed_along(): lax.ppermute(value, axis, [(source, source + steps) for source in range(f...]
    ppermute x27 -> x32, starting transfers between devices: 29.8 us -> 60 us  [swap(): return lax.ppermute(value, ('section', 'head'), pairs)]
  transfers between devices with their start and end apart: 39 -> 36, of which waited for: 27 -> 10; matrix products, arithmetic and copies ran while one was open for 16% -> 25% of each run, Pallas kernels for 0% -> 8%
where the time goes in v2:
time: 937 us; the launch traced here: 924 us
  Pallas kernels  255 us (27%)
  matrix products  235 us (25%)
  local copies, waits for them, and re-layouts  164 us (18%)
  other arithmetic  113 us (12%)
  waiting for transfers between devices  80.7 us (9%)
  starting transfers between devices  65.7 us (7%)
    dot_general x81, matrix products, mm(): lax.dot_general(left, right, (dims, ((), ())), precision=lax.Precision.HI...  199 us
    pallas_call x2, Pallas kernels, ring_sum(): pl.pallas_call(functools.partial(ring_kernel, active, lanes, count, alias...  190 us
    ppermute x32, starting transfers between devices, swap(): return lax.ppermute(value, ('section', 'head'), pairs)  60 us
    unnamed x909, local copies, waits for them, and re-layouts  51.1 us
    ppermute x32, waiting for transfers between devices, swap(): return lax.ppermute(value, ('section', 'head'), pairs)  47 us
    dot_general x18, matrix products, bmm(): lax.dot_general(left, right, (((left_dim,), (right_dim,)), ((0,), (0,))),...  35.1 us
    ppermute x4, waiting for transfers between devices, passed_along(): lax.ppermute(value, axis, [(source, source + steps) for source in range(f...  33.7 us
    pallas_call x3, Pallas kernels, scatter_memory(): pl.pallas_call(functools.partial(scatter_kernel, active), out_shape=(jax....  33.2 us
  transfers between devices with their start and end apart: 36, of which 10 were waited for; matrix products, arithmetic and copies ran while one was open for 25% of the time, Pallas kernels for 8%

profile of v2, /device:TPU:0, one launch (start us, length us, event | category | flops | bytes accessed | tf_op | source)
XLA Modules:
  0.0 924.1 jit_solution(8448085944518684992)
XLA Ops:
  1.8 4.8 collective-permute-start
  7.6 5.2 copy.106
  12.9 4.5 all-gather
  18.1 3.9 convolution_add_fusion.2
  38.0 10.6 %collective-permute-done.1 = f32[272,768]{1,0:T(8,128)} collective-permute-done((f32[272,768]{1,0:T(8,128)S(1)}, f32[272,768]{1,0:T(8,128)}, u32[]{:S(2)}, u32[]{:S(2)}) %collective-permute-start.1) | collective-permute-done | bytes 835616 | tf_op jit(solution)/shard_map/ppermute | solution.py:400
  51.7 4.8 fusion.26
  56.5 5.7 fusion.10
  65.7 3.9 collective-permute-start.2
  71.4 12.5 %shard_map.254 = (f32[128,384]{1,0:T(8,128)}, f32[128,768]{1,0:T(8,128)}) custom-call(f32[16,768]{1,0:T(8,128)} %pad_maximum_fusion.57.block), custom_call_target="tpu_custom_call" | custom-call | tf_op jit(solution)/shard_map/pallas_call | solution.py:157
  96.1 9.9 %collective-permute-done.5 = f32[128,768]{1,0:T(8,128)S(1)} collective-permute-done((f32[128,768]{1,0:T(8,128)S(1)}, f32[128,768]{1,0:T(8,128)S(1)}, u32[]{:S(2)}, u32[]{:S(2)}) %collective-permute-start.5) | collective-permute-done | bytes 393248 | tf_op jit(solution)/shard_map/ppermute | solution.py:400
  116.8 2.8 fusion.36
  125.3 18.6 %collective-permute-done.6 = f32[272,768]{1,0:T(8,128)S(1)} collective-permute-done((f32[272,768]{1,0:T(8,128)S(1)}, f32[272,768]{1,0:T(8,128)S(1)}, u32[]{:S(2)}, u32[]{:S(2)}) %collective-permute-start.6) | collective-permute-done | bytes 835616 | tf_op jit(solution)/shard_map/ppermute | solution.py:400
  145.2 2.8 fusion.29
  148.1 3.4 fusion.8
  159.3 16.3 %shard_map.255 = (f32[128,384]{1,0:T(8,128)}, f32[128,768]{1,0:T(8,128)}) custom-call(f32[16,768]{1,0:T(8,128)} %pad_maximum_fusion.58.block), custom_call_target="tpu_custom_call" | custom-call | tf_op jit(solution)/shard_map/pallas_call | solution.py:157
  193.9 4.0 broadcast_select_fusion.12
  205.1 2.8 fusion.37
  255.9 4.8 fusion.32
  260.7 5.7 fusion.4
  321.6 4.8 fusion.620
  326.4 3.2 fusion.18
  340.3 8.0 fusion.90
  376.8 5.7 fusion.255
  383.7 32.4 %collective-permute-done.14 = f32[128,768]{1,0:T(8,128)S(1)} collective-permute-done((f32[128,768]{1,0:T(8,128)S(1)}, f32[128,768]{1,0:T(8,128)S(1)}, u32[]{:S(2)}, u32[]{:S(2)}) %collective-permute-start.14) | collective-permute-done | bytes 393248 | tf_op jit(solution)/shard_map/ppermute | solution.py:608
  428.1 12.7 %shard_map.258 = (f32[16,384]{1,0:T(8,128)}, f32[16,384]{1,0:T(8,128)}) custom-call(f32[128,384]{1,0:T(8,128)} %fusion.446.d_keys, f32[128,768]{1,0:T(8,128)} %fusion.481.d_values), custom_call_target="tpu_custom_call" | custom-call | tf_op jit(solution)/shard_map/pallas_call | solution.py:256
  452.8 6.2 fusion.619
  458.9 3.2 fusion.14
  466.6 8.4 select_add_fusion.3.refs_0_
  477.5 6.5 collective-permute-done.22
  503.9 5.1 convolution_select_fusion.1
  511.2 6.7 fusion.24.refs_3_
  519.4 6.5 select_add_fusion.2.refs_1_
  555.0 8.8 shard_map.259
  575.8 2.9 collective-permute-start.28
  580.2 18.3 %shard_map.260 = (f32[16,384]{1,0:T(8,128)}, f32[16,384]{1,0:T(8,128)}) custom-call(f32[128,384]{1,0:T(8,128)} %fusion.462.d_keys, f32[128,768]{1,0:T(8,128)} %fusion.482.d_values), custom_call_target="tpu_custom_call" | custom-call | tf_op jit(solution)/shard_map/pallas_call | solution.py:256
  601.9 4.0 collective-permute-start.29
  614.2 5.6 fusion.623
  622.1 4.0 collective-permute-start.30
  627.9 9.8 %select_add_fusion.1.refs_0_ = f32[1536,768]{1,0:T(8,128)} fusion(f32[1536,768]{1,0:T(8,128)} %select_add_fusion.3.refs_0_, pred[]{:T(512)S(6)} %and.25, f32[272,1536]{1,0:T(8,128)} %copy-done.30, f32[272,1536]{1,0:T(8,128)} %copy-done.36, pred[]{:T(512)S(6)} %select_n.819, f32[16,768]{1,0:T(8,128)S(1)} %get-tuple-element.208, ...), kind=kOutput, calls=%fused_computation.25 | convolution fusion | flops 1931722752 | bytes 13615106 | tf_op jit(solution)/shard_map/dot_general | solution.py:20
  649.1 3.0 multiply_multiply_fusion
  659.3 6.7 fusion.25.refs_3_
  667.5 6.1 select_add_fusion.refs_1_
  675.8 3.8 collective-permute-start.32
  711.4 181.4 %shard_map.261 = (f32[1536,768]{1,0:T(8,128)}, f32[768,1536]{1,0:T(8,128)}, f32[384,768]{1,0:T(8,128)S(1)}, f32[768,1152]{1,0:T(8,128)}, f32[768,384]{1,0:T(8,12...) custom-call(f32[1536,768]{1,0:T(8,128)} %select_add_fusion.1.refs_0_, ...), custom_call_target="tpu_custom_call", output_to_operand_aliasing={{0}: (7, {}), {1}: (8, {}), {2}: (9, {}), {3}: (10, {}), {4... | custom-call | bytes 331612160 | tf_op jit(solution)/shard_map/pallas_call | solution.py:376
  897.2 5.2 copy.140
  902.3 5.2 copy.141
  911.2 2.9 select_bitcast_fusion
  915.1 5.5 copy.173
  (1454 shorter events, 406.8 us)
Async XLA Ops:
  1.8 48.8 %copy-start.48 = (f32[128,768]{1,0:T(8,128)}, f32[128,768]{1,0:T(8,128)S(1)}, u32[]{:S(2)}) copy-start(f32[128,768]{1,0:T(8,128)S(1)} %select_bitcast_fusion.2) | copy-start | bytes 1179652
  1.8 15.8 %collective-permute-start = (f32[128,768]{1,0:T(8,128)S(1)}, f32[128,768]{1,0:T(8,128)S(1)}, u32[]{:S(2)}, u32[]{:S(2)}) collective-permute-start(f32[128,768]{1,0:T(8,128)S(1)} %select_bitcast_fusion.2), channel_id=1, source_target_pairs={{0,1},{1,0},{2,3},{3,2},{4,5},{5,4},{6,7},{7,6},{8,9},{9,8},{10,11... | collective-permute-start | bytes 1179656 | tf_op jit(solution)/shard_map/ppermute | solution.py:400
  34.1 14.5 %collective-permute-start.1 = (f32[272,768]{1,0:T(8,128)S(1)}, f32[272,768]{1,0:T(8,128)}, u32[]{:S(2)}, u32[]{:S(2)}) collective-permute-start(f32[272,768]{1,0:T(8,128)S(1)} %fusion.216), channel_id=1, source_target_pairs={{0,1},{1,0},{2,3},{3,2},{4,5},{5,4},{6,7},{7,6},{8,9},{9,8},{10,11... | collective-permute-start | bytes 2506760 | tf_op jit(solution)/shard_map/ppermute | solution.py:400
  62.3 7.4 collective-permute-start.3
  65.7 20.1 %collective-permute-start.2 = (f32[128,768]{1,0:T(8,128)}, f32[128,768]{1,0:T(8,128)}, u32[]{:S(2)}, u32[]{:S(2)}) collective-permute-start(f32[128,768]{1,0:T(8,128)} %slice.804), channel_id=1, source_target_pairs={{0,1},{1,0},{2,3},{3,2},{4,5},{5,4},{6,7},{7,6},{8,9},{9,8},{10,11... | collective-permute-start | bytes 1179656 | tf_op jit(solution)/shard_map/ppermute | solution.py:400
  91.7 2.7 collective-permute-start.4
  94.5 11.5 %collective-permute-start.5 = (f32[128,768]{1,0:T(8,128)S(1)}, f32[128,768]{1,0:T(8,128)S(1)}, u32[]{:S(2)}, u32[]{:S(2)}) collective-permute-start(f32[128,768]{1,0:T(8,128)S(1)} %bitcast_select_fusion.3), channel_id=1, source_target_pairs={{0,1},{1,0},{16,17},{17,16},{2,3},{3,2},{18,19},{19,18},{4,5},{5,4... | collective-permute-start | bytes 1179656 | tf_op jit(solution)/shard_map/ppermute | solution.py:400
  123.8 20.1 %collective-permute-start.6 = (f32[272,768]{1,0:T(8,128)S(1)}, f32[272,768]{1,0:T(8,128)S(1)}, u32[]{:S(2)}, u32[]{:S(2)}) collective-permute-start(f32[272,768]{1,0:T(8,128)S(1)} %fusion.214), channel_id=1, source_target_pairs={{0,1},{1,0},{16,17},{17,16},{2,3},{3,2},{18,19},{19,18},{4,5},{5,4... | collective-permute-start | bytes 2506760 | tf_op jit(solution)/shard_map/ppermute | solution.py:400
  152.4 4.4 collective-permute-start.8
  155.6 22.3 %collective-permute-start.7 = (f32[128,768]{1,0:T(8,128)}, f32[128,768]{1,0:T(8,128)}, u32[]{:S(2)}, u32[]{:S(2)}) collective-permute-start(f32[128,768]{1,0:T(8,128)} %slice.833), channel_id=1, source_target_pairs={{0,1},{1,0},{16,17},{17,16},{2,3},{3,2},{18,19},{19,18},{4,5},{5,4... | collective-permute-start | bytes 1179656 | tf_op jit(solution)/shard_map/ppermute | solution.py:400
  183.0 2.6 collective-permute-start.15
  186.4 4.3 collective-permute-start.16
  213.0 38.1 %collective-permute-start.17 = (f32[272,768]{1,0:T(8,128)}, f32[272,768]{1,0:T(8,128)}, u32[]{:S(2)}, u32[]{:S(2)}) collective-permute-start(f32[272,768]{1,0:T(8,128)} %fusion.212), channel_id=1, source_target_pairs={{16,17},{17,16},{18,19},{19,18},{20,21},{21,20},{22,23},{23,22},{2... | collective-permute-start | bytes 2506760 | tf_op jit(solution)/shard_map/ppermute | solution.py:400
  266.4 4.4 collective-permute-start.19
  269.4 13.1 %collective-permute-start.18 = (f32[128,768]{1,0:T(8,128)}, f32[128,768]{1,0:T(8,128)}, u32[]{:S(2)}, u32[]{:S(2)}) collective-permute-start(f32[128,768]{1,0:T(8,128)} %slice.892), channel_id=1, source_target_pairs={{16,17},{17,16},{18,19},{19,18},{20,21},{21,20},{22,23},{23,22},{2... | collective-permute-start | bytes 1179656 | tf_op jit(solution)/shard_map/ppermute | solution.py:400
  298.9 22.6 %collective-permute-start.9 = (f32[128,768]{1,0:T(8,128)}, f32[128,768]{1,0:T(8,128)}, u32[]{:S(2)}, u32[]{:S(2)}) collective-permute-start(f32[128,768]{1,0:T(8,128)} %get-tuple-element.431), channel_id=1, source_target_pairs={{16,17},{17,16},{18,19},{19,18},{20,21},{21,20},{22,23},{23,22},{2... | collective-permute-start | bytes 1179656 | tf_op jit(solution)/shard_map/ppermute | solution.py:400
  312.1 8.8 collective-permute-start.10
  329.6 18.8 %collective-permute-start.11 = (f32[272,768]{1,0:T(8,128)}, f32[272,768]{1,0:T(8,128)}, u32[]{:S(2)}, u32[]{:S(2)}) collective-permute-start(f32[272,768]{1,0:T(8,128)} %fusion.18), channel_id=1, source_target_pairs={{16,17},{17,16},{18,19},{19,18},{20,21},{21,20},{22,23},{23,22},{2... | collective-permute-start | bytes 2506760 | tf_op jit(solution)/shard_map/ppermute | solution.py:400
  369.4 4.6 collective-permute-start.12
  370.2 3.7 collective-permute-start.13
  375.3 40.8 %copy-start.126 = (f32[1,2,128,768]{3,2,1,0:T(8,128)S(1)}, f32[1,2,128,768]{3,2,1,0:T(8,128)}, u32[]{:S(2)}) copy-start(f32[1,2,128,768]{3,2,1,0:T(8,128)} %param.16) | copy-start | bytes 2359300
  375.3 40.8 %copy-start.199 = (f32[128,768]{1,0:T(8,128)S(1)}, f32[128,768]{1,0:T(8,128)}, u32[]{:S(2)}) copy-start(f32[128,768]{1,0:T(8,128)} %get-tuple-element.407) | copy-start | bytes 1179652
  375.3 40.8 %copy-start.248 = (f32[128,768]{1,0:T(8,128)S(1)}, f32[128,768]{1,0:T(8,128)}, u32[]{:S(2)}) copy-start(f32[128,768]{1,0:T(8,128)} %convolution_divide_fusion) | copy-start | bytes 1179652
  375.3 40.8 %collective-permute-start.14 = (f32[128,768]{1,0:T(8,128)S(1)}, f32[128,768]{1,0:T(8,128)S(1)}, u32[]{:S(2)}, u32[]{:S(2)}) collective-permute-start(f32[128,768]{1,0:T(8,128)S(1)} %slice.884), channel_id=1, source_target_pairs={{16,0},{17,1},{18,2},{19,3},{20,4},{21,5},{22,6},{23,7},{24,8},{25... | collective-permute-start | bytes 1179656 | tf_op jit(solution)/shard_map/ppermute | solution.py:608
  382.5 33.8 %copy-start.418 = (f32[128]{0:T(128)S(1)}, f32[128]{0:T(128)}, u32[]{:S(2)}) copy-start(f32[128]{0:T(128)} %copy-done.417) | copy-start | bytes 1540
  382.5 33.8 %copy-start.292 = (f32[128,768]{1,0:T(8,128)S(1)}, f32[128,768]{1,0:T(8,128)}, u32[]{:S(2)}) copy-start(f32[128,768]{1,0:T(8,128)} %get-tuple-element.73) | copy-start | bytes 1179652
  382.5 33.8 %copy-start.421 = (f32[128]{0:T(128)S(1)}, f32[128]{0:T(128)}, u32[]{:S(2)}) copy-start(f32[128]{0:T(128)} %get-tuple-element.397) | copy-start | bytes 1540
  382.5 33.8 %copy-start.426 = (f32[128,768]{1,0:T(8,128)S(1)}, f32[128,768]{1,0:T(8,128)}, u32[]{:S(2)}) copy-start(f32[128,768]{1,0:T(8,128)} %get-tuple-element.87) | copy-start | bytes 1179652
  425.3 27.4 %collective-permute-start.20 = (f32[128,768]{1,0:T(8,128)}, f32[128,768]{1,0:T(8,128)}, u32[]{:S(2)}, u32[]{:S(2)}) collective-permute-start(f32[128,768]{1,0:T(8,128)} %get-tuple-element.433), channel_id=1, source_target_pairs={{0,1},{1,0},{16,17},{17,16},{2,3},{3,2},{18,19},{19,18},{4,5},{5,4... | collective-permute-start | bytes 1179656 | tf_op jit(solution)/shard_map/ppermute | solution.py:400
  443.7 8.4 collective-permute-start.21
  449.2 25.8 %collective-permute-start.26 = (f32[768,384]{1,0:T(8,128)}, f32[768,384]{1,0:T(8,128)}, u32[]{:S(2)}, u32[]{:S(2)}) collective-permute-start(f32[768,384]{1,0:T(8,128)} %get-tuple-element.424), channel_id=1, source_target_pairs={{16,17},{17,16},{18,19},{19,18},{20,21},{21,20},{22,23},{23,22},{2... | collective-permute-start | bytes 3538952 | tf_op jit(solution)/shard_map/ppermute | solution.py:400
  462.1 21.9 %collective-permute-start.22 = (f32[272,768]{1,0:T(8,128)}, f32[272,768]{1,0:T(8,128)}, u32[]{:S(2)}, u32[]{:S(2)}) collective-permute-start(f32[272,768]{1,0:T(8,128)} %fusion.14), channel_id=1, source_target_pairs={{0,1},{1,0},{16,17},{17,16},{2,3},{3,2},{18,19},{19,18},{4,5},{5,4... | collective-permute-start | bytes 2506760 | tf_op jit(solution)/shard_map/ppermute | solution.py:400
  509.1 24.6 %collective-permute-start.23 = (f32[128,768]{1,0:T(8,128)}, f32[128,768]{1,0:T(8,128)}, u32[]{:S(2)}, u32[]{:S(2)}) collective-permute-start(f32[128,768]{1,0:T(8,128)} %slice.940), channel_id=1, source_target_pairs={{0,1},{1,0},{16,17},{17,16},{2,3},{3,2},{18,19},{19,18},{4,5},{5,4... | collective-permute-start | bytes 1179656 | tf_op jit(solution)/shard_map/ppermute | solution.py:400
  510.0 22.3 %collective-permute-start.24 = (f32[16,768]{1,0:T(8,128)}, f32[16,768]{1,0:T(8,128)}, u32[]{:S(2)}, u32[]{:S(2)}) collective-permute-start(f32[16,768]{1,0:T(8,128)} %slice.941), channel_id=1, source_target_pairs={{0,1},{1,0},{16,17},{17,16},{2,3},{3,2},{18,19},{19,18},{4,5},{5,4... | collective-permute-start | bytes 147464 | tf_op jit(solution)/shard_map/ppermute | solution.py:400
  544.5 8.9 collective-permute-start.27
  549.5 14.5 %collective-permute-start.25 = (f32[128,768]{1,0:T(8,128)}, f32[128,768]{1,0:T(8,128)}, u32[]{:S(2)}, u32[]{:S(2)}) collective-permute-start(f32[128,768]{1,0:T(8,128)} %get-tuple-element.324), channel_id=1, source_target_pairs={{16,0},{17,1},{18,2},{19,3},{20,4},{21,5},{22,6},{23,7},{24,8},{25... | collective-permute-start | bytes 1179656 | tf_op jit(solution)/shard_map/ppermute | solution.py:608
  575.8 38.4 %collective-permute-start.28 = (f32[128,768]{1,0:T(8,128)}, f32[128,768]{1,0:T(8,128)}, u32[]{:S(2)}, u32[]{:S(2)}) collective-permute-start(f32[128,768]{1,0:T(8,128)} %get-tuple-element.441), channel_id=1, source_target_pairs={{0,1},{1,0},{2,3},{3,2},{4,5},{5,4},{6,7},{7,6},{8,9},{9,8},{10,11... | collective-permute-start | bytes 1179656 | tf_op jit(solution)/shard_map/ppermute | solution.py:400
  601.9 12.2 %collective-permute-start.29 = (f32[16,768]{1,0:T(8,128)S(1)}, f32[16,768]{1,0:T(8,128)S(1)}, u32[]{:S(2)}, u32[]{:S(2)}) collective-permute-start(f32[16,768]{1,0:T(8,128)S(1)} %fusion.227), channel_id=1, source_target_pairs={{0,1},{1,0},{2,3},{3,2},{4,5},{5,4},{6,7},{7,6},{8,9},{9,8},{10,11... | collective-permute-start | bytes 147464 | tf_op jit(solution)/shard_map/ppermute | solution.py:400
  612.1 25.6 %collective-permute-start.33 = (f32[768,384]{1,0:T(8,128)}, f32[768,384]{1,0:T(8,128)}, u32[]{:S(2)}, u32[]{:S(2)}) collective-permute-start(f32[768,384]{1,0:T(8,128)} %get-tuple-element.436), channel_id=1, source_target_pairs={{0,1},{1,0},{2,3},{3,2},{4,5},{5,4},{6,7},{7,6},{8,9},{9,8},{10,11... | collective-permute-start | bytes 3538952 | tf_op jit(solution)/shard_map/ppermute | solution.py:400
  622.1 18.0 %collective-permute-start.30 = (f32[272,768]{1,0:T(8,128)S(1)}, f32[272,768]{1,0:T(8,128)}, u32[]{:S(2)}, u32[]{:S(2)}) collective-permute-start(f32[272,768]{1,0:T(8,128)S(1)} %fusion.12), channel_id=1, source_target_pairs={{0,1},{1,0},{2,3},{3,2},{4,5},{5,4},{6,7},{7,6},{8,9},{9,8},{10,11... | collective-permute-start | bytes 2506760 | tf_op jit(solution)/shard_map/ppermute | solution.py:400
  673.6 11.9 %collective-permute-start.31 = (f32[128,768]{1,0:T(8,128)}, f32[128,768]{1,0:T(8,128)S(1)}, u32[]{:S(2)}, u32[]{:S(2)}) collective-permute-start(f32[128,768]{1,0:T(8,128)} %slice.976), channel_id=1, source_target_pairs={{0,1},{1,0},{2,3},{3,2},{4,5},{5,4},{6,7},{7,6},{8,9},{9,8},{10,11... | collective-permute-start | bytes 1179656 | tf_op jit(solution)/shard_map/ppermute | solution.py:400
  675.8 8.4 collective-permute-start.32
  697.7 7.5 collective-permute-start.34
  711.4 184.7 %copy-start.233 = (f32[136,768]{1,0:T(8,128)S(1)}, f32[136,768]{1,0:T(8,128)}, u32[]{:S(2)}) copy-start(f32[136,768]{1,0:T(8,128)} %copy-done.232) | copy-start | bytes 1253380
  711.4 184.7 %copy-start.235 = (f32[128,768]{1,0:T(8,128)S(1)}, f32[128,768]{1,0:T(8,128)}, u32[]{:S(2)}) copy-start(f32[128,768]{1,0:T(8,128)} %copy-done.234) | copy-start | bytes 1179652
  711.4 184.8 %copy-start.237 = (f32[1,1,128,768]{3,2,1,0:T(8,128)S(1)}, f32[1,1,128,768]{3,2,1,0:T(8,128)}, u32[]{:S(2)}) copy-start(f32[1,1,128,768]{3,2,1,0:T(8,128)} %get-tuple-element.323) | copy-start | bytes 1179652
  711.4 184.8 %copy-start.242 = (f32[1,1,128,768]{3,2,1,0:T(8,128)S(1)}, f32[1,1,128,768]{3,2,1,0:T(8,128)}, u32[]{:S(2)}) copy-start(f32[1,1,128,768]{3,2,1,0:T(8,128)} %get-tuple-element.325) | copy-start | bytes 1179652
  894.9 16.3 %collective-permute-start.35 = (f32[768,384]{1,0:T(8,128)S(1)}, f32[768,384]{1,0:T(8,128)}, u32[]{:S(2)}, u32[]{:S(2)}) collective-permute-start(f32[768,384]{1,0:T(8,128)S(1)} %get-tuple-element.128), channel_id=1, source_target_pairs={{0,1},{1,0},{16,17},{17,16},{2,3},{3,2},{18,19},{19,18},{4,5},{5,4... | collective-permute-start | bytes 3538952 | tf_op jit(solution)/shard_map/ppermute | solution.py:400
  (438 other events, 2311.2 us)

commit v3 on v1

--- a/solution.py
+++ b/solution.py
@@ -1,13 +1,21 @@
+import functools
 import math
 
 import jax
 import jax.numpy as jnp
 from jax import lax
+from jax.experimental import pallas as pl
+from jax.experimental.pallas import tpu as pltpu
 from jax.sharding import PartitionSpec as P
 
 HEAD_DIM = 64
 EPSILON = 1e-05
 SCALE = 1.0 / math.sqrt(HEAD_DIM)
+MESH = pl.DeviceIdType.MESH
+VMEM = pl.BlockSpec(memory_space=pltpu.VMEM)
+HBM = pl.BlockSpec(memory_space=pltpu.HBM)
+SMEM = pl.BlockSpec(memory_space=pltpu.SMEM)
+SHARED_ROWS = 36
 
 
 def mm(left, right, dims=((1,), (0,))):
@@ -49,24 +57,8 @@
     return jax.nn.gelu(values_in, approximate=True)
 
 
-def swap(value):
-    return lax.ppermute(value, "head", [(0, 1), (1, 0)])
-
-
-def head_sum(value):
-    if lax.axis_size("head") == 2:
-        return value + swap(value)
-    return lax.psum(value, "head")
-
-
 def head_sum_rows(rows, share):
-    count = lax.axis_size("head")
-    segment = count * share
-    if count == 2:
-        other = swap(rows)
-        return rows + jnp.concatenate(
-            [other[share:segment], other[:share], other[segment:]], axis=0
-        )
+    segment = lax.axis_size("head") * share
     turn = lax.axis_index("head") * share
     total = lax.psum(
         jnp.concatenate([jnp.roll(rows[:segment], turn, axis=0), rows[segment:]], axis=0), "head"
@@ -75,31 +67,14 @@
 
 
 def head_rows(local):
-    count = lax.axis_size("head")
-    if count == 2:
-        return jnp.concatenate([local, swap(local)], axis=0)
     gathered = lax.all_gather(local, "head", axis=0, tiled=True)
     return jnp.roll(gathered, -lax.axis_index("head") * local.shape[0], axis=0)
 
 
 def head_scatter(rows):
-    count = lax.axis_size("head")
-    share = rows.shape[0] // count
-    if count == 2:
-        return rows[:share] + swap(rows[share:])
+    share = rows.shape[0] // lax.axis_size("head")
     placed = jnp.roll(rows, lax.axis_index("head") * share, axis=0)
     return lax.psum_scatter(placed, "head", scatter_dimension=0, tiled=True)
-
-
-def head_columns(values):
-    count = lax.axis_size("head")
-    share = values.shape[1] // count
-    place = lax.axis_index("head")
-    if count == 2:
-        own = lax.dynamic_slice_in_dim(values, place * share, share, 1)
-        other = lax.dynamic_slice_in_dim(values, (1 - place) * share, share, 1)
-        return own + swap(other)
-    return lax.psum_scatter(values, "head", scatter_dimension=1, tiled=True)
 
 
 def heads_of(part):
@@ -142,7 +117,7 @@
     inner_act = gelu_tanh(inner_pre)
     partial = mm(inner_act, params["down"])
     out_local = head_scatter(partial[:segment]) + hidden[:local_count] + params["residual"][1]
-    out_mem = head_sum(partial[segment:]) + hidden[segment:] + params["residual"][1]
+    out_mem = lax.psum(partial[segment:], "head") + hidden[segment:] + params["residual"][1]
     key_proj = mm(out_mem, params["key_mem"])
     values = mm(out_mem, params["value_mem"])
     gathered = lax.all_gather(jnp.concatenate([key_proj, values], axis=1), "seq", axis=0, tiled=True)
@@ -196,8 +171,12 @@
     )
     dk = d_keys.shape[1]
     d_key_proj = d_memory[:, :dk]
-    d_value = head_columns(d_memory[:, dk:])
-    d_mem = head_sum(mm_nt(d_key_proj, params["key_mem"]) + mm_nt(d_value, params["value_mem"]))
+    d_value = lax.psum_scatter(
+        d_memory[:, dk:], "head", scatter_dimension=1, tiled=True
+    )
+    d_mem = lax.psum(
+        mm_nt(d_key_proj, params["key_mem"]) + mm_nt(d_value, params["value_mem"]), "head"
+    )
     d_local = grad + mm_nt(d_query_proj, params["query_mem"])
     d_result = jnp.concatenate([head_rows(d_local), d_mem], axis=0)
     inner_act, gelu_back = jax.vjp(gelu_tanh, record["inner_pre"])
@@ -408,9 +387,992 @@
     )
 
 
+def barrier_with(pairs, wait_count):
+    barrier = pltpu.get_barrier_semaphore()
+    for condition, device in pairs:
+
+        @pl.when(condition)
+        def _(device=device):
+            pl.semaphore_signal(barrier, inc=1, device_id=device, device_id_type=MESH)
+
+    @pl.when(wait_count > 0)
+    def _():
+        pl.semaphore_wait(barrier, wait_count)
+
+
+def nn(left, right):
+    return mm(left, right)
+
+
+def lane_tiles(width):
+    tile = 256 if width % 256 == 0 else width
+    return [(at, tile) for at in range(0, width, tile)]
+
+
+def rows_at(start, count):
+    return pl.ds(pl.multiple_of(start, count), count)
+
+
+def halves_of(projected):
+    small = jnp.log1p(jnp.exp(-jnp.abs(projected)))
+    return jnp.concatenate(
+        [jnp.maximum(projected, 0.0) + small, jnp.maximum(-projected, 0.0) + small], axis=1
+    )
+
+
+def halves_back(projected, d_halves):
+    width = projected.shape[1]
+    rising = 1.0 / (1.0 + jnp.exp(-projected))
+    falling = 1.0 / (1.0 + jnp.exp(projected))
+    return d_halves[:, :width] * rising - d_halves[:, width:] * falling
+
+
+def turned(values, by):
+    return pltpu.roll(values, by % values.shape[1], 1)
+
+
+GELU_IN = math.sqrt(2.0 / math.pi)
+
+
+def gelu_parts(pre):
+    cubic = 0.044715 * pre * pre
+    bent = jnp.tanh(GELU_IN * pre * (1.0 + cubic))
+    half = 0.5 * (1.0 + bent)
+    slope = half + 0.5 * pre * (1.0 - bent * bent) * GELU_IN * (1.0 + 3.0 * cubic)
+    return pre * half, slope
+
+
+def seen_mask(items, micro, seqs, mem):
+    seq = lax.axis_index("seq")
+    row_seq = lax.div(lax.broadcasted_iota(jnp.int32, (1, seqs * mem), 1), jnp.int32(mem))
+    end = jnp.int32(0)
+    own = jnp.int32(0)
+    item = jnp.zeros((1, seqs * mem), jnp.int32)
+    for piece in range(items.shape[1]):
+        end = end + items[jnp.maximum(micro - 1, 0), piece]
+        bound = jnp.where(micro == 0, seqs, end)
+        own = own + (seq >= bound).astype(jnp.int32)
+        item = item + (row_seq >= bound).astype(jnp.int32)
+    return jnp.logical_and(row_seq < seq, item == own)
+
+
+def sender(send, recv):
+    def copy(slot, source, target, device):
+        return pltpu.make_async_remote_copy(
+            src_ref=source,
+            dst_ref=target,
+            send_sem=send.at[slot],
+            recv_sem=recv.at[slot],
+            device_id=device,
+            device_id_type=MESH,
+        )
+
+    return copy
+
+
+def forward_kernel(
+    items, x, gains, biases, w_in, head_bias, w_out, residual, w_up, b_up, w_down, mem_tokens,
+    w_query, w_key, w_value,
+    rows, qkv, attended, lse, hidden, pre, out_local, out_mem, keys, values, query_proj, weights,
+    read, y,
+    normed, part, got_part, act, got_out, mem_all, key_block, value_block,
+    send, recv, send_k, recv_k, send_v, recv_v,
+):
+    section, seq, head = (lax.axis_index(name) for name in ("section", "seq", "head"))
+    seqs = lax.axis_size("seq")
+    micro_total, local, width = x.shape
+    segment = 2 * local
+    mem = out_mem.shape[1]
+    total = segment + mem
+    share = w_in.shape[2]
+    dv = w_value.shape[1]
+    other = 1 - head
+    partner = {"head": other}
+    copy = sender(send, recv)
+    own_rows, other_rows = rows_at(head * local, local), rows_at(other * local, local)
+    own_mem = rows_at(head * (mem // 2), mem // 2)
+    column_tiles = lane_tiles(width)
+
+    keys[...] = jnp.zeros_like(keys)
+    values[...] = jnp.zeros_like(values)
+    mem_all[own_mem] = mem_tokens[...]
+    barrier_with(
+        [(seq >= 0, partner)]
+        + [(t < seq, {"seq": t, "head": g}) for t in range(seqs) for g in range(2)]
+        + [(section == 1, {"section": 0, "head": g}) for g in range(2)],
+        1 + 2 * (seqs - 1 - seq) + 2 * (1 - section),
+    )
+    per_micro = 3 + 3 * len(column_tiles)
+
+    def slot(micro, number):
+        return 1 + micro * per_micro + number
+
+    tokens = copy(0, mem_tokens, mem_all.at[own_mem], partner)
+    tokens.start()
+
+    def x_copy(micro):
+        return copy(slot(micro, 0), x.at[micro], rows.at[micro, own_rows], partner)
+
+    def y_copy(micro, source_head, target_head):
+        return copy(
+            slot(micro, 1 + source_head),
+            y.at[micro],
+            rows.at[micro, rows_at(source_head * local, local)],
+            {"section": 1, "head": target_head},
+        )
+
+    def y_sent(micro, target_head):
+        return pltpu.make_async_remote_copy(
+            src_ref=y.at[micro],
+            dst_ref=rows.at[micro, own_rows],
+            send_sem=send.at[slot(micro, 1 + target_head)],
+            recv_sem=recv.at[slot(micro, 1 + head)],
+            device_id={"section": 1, "head": target_head},
+            device_id_type=MESH,
+        )
+
+    @pl.when(section == 0)
+    def _():
+        for micro in range(micro_total):
+            x_copy(micro).start()
+            rows[micro, own_rows] = x[micro]
+
+    tokens.wait_recv()
+    for micro in range(micro_total):
+        rows[micro, segment:] = mem_all[...]
+
+    def key_copy(micro, source, target):
+        return pltpu.make_async_remote_copy(
+            src_ref=key_block,
+            dst_ref=keys.at[micro, rows_at(source * mem, mem)],
+            send_sem=send_k.at[micro, target],
+            recv_sem=recv_k.at[micro, source],
+            device_id={"seq": target},
+            device_id_type=MESH,
+        )
+
+    def value_copy(micro, source, source_head, target, target_head):
+        return pltpu.make_async_remote_copy(
+            src_ref=value_block,
+            dst_ref=values.at[
+                micro, rows_at(source * mem, mem), pl.ds(pl.multiple_of(source_head * dv, 128), dv)
+            ],
+            send_sem=send_v.at[micro, target, target_head],
+            recv_sem=recv_v.at[micro, source, source_head],
+            device_id={"seq": target, "head": target_head},
+            device_id_type=MESH,
+        )
+
+    places = lax.broadcasted_iota(jnp.int32, (total, total), 0)
+    allowed = places >= lax.broadcasted_iota(jnp.int32, (total, total), 1)
+    lane = lax.broadcasted_iota(jnp.int32, (total, 128), 1)
+
+    def one_micro(micro, carry):
+        @pl.when(section == 0)
+        def _():
+            x_copy(micro).wait_recv()
+
+        @pl.when(section == 1)
+        def _():
+            for source in range(2):
+                y_copy(micro, source, source).wait_recv()
+
+        unit, _ = unit_rows(rows[micro])
+        normed[...] = unit * gains[0:1] + biases[0:1]
+        for kind in range(3):
+            made = nn(normed[...], w_in[kind])
+            if kind != 1:
+                made = made + head_bias[kind // 2 : kind // 2 + 1]
+            qkv[micro, :, kind * share : (kind + 1) * share] = made
+        tops = jnp.zeros((total, 128), jnp.float32)
+        for place in range(share // HEAD_DIM):
+            query, key, value = (
+                qkv[micro, :, kind * share + place * HEAD_DIM : kind * share + (place + 1) * HEAD_DIM]
+                for kind in range(3)
+            )
+            scores = jnp.where(allowed, mm_nt(query, key) * SCALE, -1e30)
+            top = jnp.max(scores, axis=1, keepdims=True)
+            exponent = jnp.exp(scores - top)
+            row_total = jnp.sum(exponent, axis=1, keepdims=True)
+            attended[micro, :, place * HEAD_DIM : (place + 1) * HEAD_DIM] = (
+                nn(exponent, value) / row_total
+            )
+            tops = jnp.where(lane == place, top + jnp.log(row_total), tops)
+        lse[micro] = tops
+
+        def part_copy(index):
+            at, tile = column_tiles[index]
+            return copy(
+                slot(micro, 3 + index),
+                part.at[:, at : at + tile],
+                got_part.at[micro, :, at : at + tile],
+                partner,
+            )
+
+        for index, (at, tile) in enumerate(column_tiles):
+            part[:, at : at + tile] = nn(attended[micro], w_out[:, at : at + tile])
+            part_copy(index).start()
+        for index, (at, tile) in enumerate(column_tiles):
+            part_copy(index).wait_recv()
+            cut = slice(at, at + tile)
+            hidden[micro, :, cut] = (
+                rows[micro, :, cut] + part[:, cut] + got_part[micro, :, cut] + residual[0:1, cut]
+            )
+        unit, _ = unit_rows(hidden[micro])
+        normed[...] = unit * gains[1:2] + biases[1:2]
+        for at, tile in lane_tiles(act.shape[1]):
+            cut = slice(at, at + tile)
+            made = nn(normed[...], w_up[:, cut]) + b_up[:, cut]
+            pre[micro, :, cut] = made
+            act[:, cut] = gelu_parts(made)[0]
+        for index in range(len(column_tiles)):
+            part_copy(index).wait_send()
+        count = len(column_tiles)
+
+        def out_copies(index):
+            at, tile = column_tiles[index]
+            return (
+                copy(
+                    slot(micro, 3 + count + index),
+                    part.at[other_rows, at : at + tile],
+                    got_out.at[micro, pl.ds(0, local), at : at + tile],
+                    partner,
+                ),
+                copy(
+                    slot(micro, 3 + 2 * count + index),
+                    part.at[pl.ds(segment, mem), at : at + tile],
+                    got_out.at[micro, pl.ds(local, mem), at : at + tile],
+                    partner,
+                ),
+            )
+
+        for index, (at, tile) in enumerate(column_tiles):
+            part[:, at : at + tile] = nn(act[...], w_down[:, at : at + tile])
+            for one in reversed(out_copies(index)):
+                one.start()
+        for index, (at, tile) in enumerate(column_tiles):
+            cut = slice(at, at + tile)
+            out_copies(index)[1].wait_recv()
+            out_mem[micro, :, cut] = (
+                part[segment:, cut]
+                + got_out[micro, local:, cut]
+                + hidden[micro, segment:, cut]
+                + residual[1:2, cut]
+            )
+        key_block[...] = nn(out_mem[micro], w_key[...])
+        value_block[...] = nn(out_mem[micro], w_value[...])
+        for t in range(seqs):
+
+            @pl.when(t > seq)
+            def _(t=t):
+                key_copy(micro, seq, t).start()
+                for g in range(2):
+                    value_copy(micro, seq, head, t, g).start()
+
+        for index, (at, tile) in enumerate(column_tiles):
+            cut = slice(at, at + tile)
+            out_copies(index)[0].wait_recv()
+            out_local[micro, :, cut] = (
+                part[own_rows, cut]
+                + got_out[micro, :local, cut]
+                + hidden[micro, own_rows, cut]
+                + residual[1:2, cut]
+            )
+        query_proj[micro] = nn(out_local[micro], w_query[...])
+        query_halves = halves_of(query_proj[micro])
+        for t in range(seqs):
+
+            @pl.when(t < seq)
+            def _(t=t):
+                key_copy(micro, t, t).wait_recv()
+
+        key_halves = halves_of(keys[micro])
+        scores = jnp.zeros((local, seqs * mem), jnp.float32)
+        for by in (1, 2, 3):
+            scores = scores + mm_nt(
+                query_halves * turned(query_halves, by), key_halves * turned(key_halves, by)
+            )
+        scores = jnp.where(seen_mask(items, micro, seqs, mem), scores, 0.0)
+        weights[micro] = scores
+        for t in range(seqs):
+
+            @pl.when(t < seq)
+            def _(t=t):
+                for g in range(2):
+                    value_copy(micro, t, g, t, g).wait_recv()
+
+        found = nn(scores, values[micro]) / (jnp.sum(scores, axis=1, keepdims=True) + 1.0)
+        read[micro] = found
+        y[micro] = out_local[micro] + found
+
+        @pl.when(section == 0)
+        def _():
+            for target in range(2):
+                y_sent(micro, target).start()
+
+        for index in range(count):
+            for one in out_copies(index):
+                one.wait_send()
+        for t in range(seqs):
+
+            @pl.when(t > seq)
+            def _(t=t):
+                key_copy(micro, seq, t).wait_send()
+                for g in range(2):
+                    value_copy(micro, seq, head, t, g).wait_send()
+
+        return carry
+
+    lax.fori_loop(0, micro_total, one_micro, 0)
+    tokens.wait_send()
+
+    @pl.when(section == 0)
+    def _():
+        for micro in range(micro_total):
+            x_copy(micro).wait_send()
+            for target in range(2):
+                y_sent(micro, target).wait_send()
+
+
+RECORDS = (
+    "rows", "qkv", "attended", "lse", "hidden", "pre", "out_local", "out_mem", "keys", "values",
+    "query_proj", "weights", "read",
+)
+
+
+def backward_kernel(
+    items, x, gains, biases, w_in, w_out, w_up, w_down, w_query, w_key, w_value, *refs
+):
+    count = len(RECORDS)
+    kept = refs[:count]
+    (g_in, g_out, g_up, g_down, g_value, g_whole, g_small, grad_x) = refs[count : count + 8]
+    record = dict(zip(RECORDS, refs[count + 8 : 2 * count + 8]))
+    (
+        d_out, normed, d_pre, d_part, got_mix, d_qkv, got_rows, from_k, from_v, d_keys, d_values,
+        mem_part, got_mem, grad_y,
+        load, send, recv, send_k, recv_k, send_v, recv_v,
+    ) = refs[2 * count + 8 :]
+    rows, qkv, attended, lse, hidden, pre = (record[name] for name in RECORDS[:6])
+    out_local, out_mem, keys, values = (record[name] for name in RECORDS[6:10])
+    query_proj, weights, read = (record[name] for name in RECORDS[10:])
+
+    section, seq, head = (lax.axis_index(name) for name in ("section", "seq", "head"))
+    seqs = lax.axis_size("seq")
+    micro_total, local, width = x.shape
+    segment = 2 * local
+    mem = out_mem.shape[0]
+    total = segment + mem
+    share = w_in.shape[2]
+    inner = w_up.shape[1]
+    dv = w_value.shape[1]
+    other = 1 - head
+    partner = {"head": other}
+    copy = sender(send, recv)
+    own_rows, other_rows = rows_at(head * local, local), rows_at(other * local, local)
+    own_mem_rows = rows_at(segment + head * (mem // 2), mem // 2)
+    own_mem = rows_at(head * (mem // 2), mem // 2)
+    column_tiles = lane_tiles(width)
+    inner_tiles = lane_tiles(inner)
+
+    def load_records(micro):
+        return [
+            pltpu.make_async_copy(kept[i].at[micro], record[RECORDS[i]], load.at[i])
+            for i in range(count)
+        ]
+
+    for one in load_records(0):
+        one.start()
+    for ref in (g_in, g_out, g_up, g_down, g_value, g_whole, g_small, from_k, from_v):
+        ref[...] = jnp.zeros_like(ref)
+    barrier_with(
+        [(seq >= 0, partner)]
+        + [(t > seq, {"seq": t, "head": g}) for t in range(seqs) for g in range(2)]
+        + [(section == 0, {"section": 1})],
+        1 + 2 * seq + section,
+    )
+    per_micro = 3 + 3 * len(column_tiles)
+
+    def slot(micro, number):
+        return micro * per_micro + number
+
+    def grad_copy(micro):
+        return copy(slot(micro, 0), grad_x.at[micro], grad_y.at[micro], {"section": 0})
+
+    def key_copy(micro, source, target):
+        return pltpu.make_async_remote_copy(
+            src_ref=d_keys.at[rows_at(target * mem, mem)],
+            dst_ref=from_k.at[micro, source],
+            send_sem=send_k.at[micro, target],
+            recv_sem=recv_k.at[micro, source],
+            device_id={"seq": target},
+            device_id_type=MESH,
+        )
+
+    def value_copy(micro, source, source_head, target, target_head):
+        return pltpu.make_async_remote_copy(
+            src_ref=d_values.at[
+                rows_at(target * mem, mem), pl.ds(pl.multiple_of(target_head * dv, 128), dv)
+            ],
+            dst_ref=from_v.at[micro, source, source_head],
+            send_sem=send_v.at[micro, target, target_head],
+            recv_sem=recv_v.at[micro, source, source_head],
+            device_id={"seq": target, "head": target_head},
+            device_id_type=MESH,
+        )
+
+    places = lax.broadcasted_iota(jnp.int32, (total, total), 0)
+    allowed = places >= lax.broadcasted_iota(jnp.int32, (total, total), 1)
+
+    def add_small(row, vector):
+        for at in range(0, vector.shape[1], 128):
+            g_small[row + at // 128 : row + at // 128 + 1] += vector[:, at : at + 128]
+
+    def column_sum(values_in):
+        return jnp.sum(values_in, axis=0, keepdims=True)
+
+    def one_micro(micro, carry):
+        @pl.when(micro > 0)
+        def _():
+            for one in load_records(micro):
+                one.start()
+
+        for one in load_records(micro):
+            one.wait()
+
+        @pl.when(section == 0)
+        def _():
+            grad_copy(micro).wait_recv()
+
+        @pl.when(section == 1)
+        def _():
+            grad_y[micro] = x[micro]
+
+        grad = grad_y[micro]
+        scores = weights[...]
+        denominator = jnp.sum(scores, axis=1, keepdims=True) + 1.0
+        d_numer = grad / denominator
+        d_denom = -jnp.sum(grad * read[...], axis=1, keepdims=True) / denominator
+        d_values[...] = mm_tn(scores, d_numer)
+        for t in range(seqs):
+
+            @pl.when(t < seq)
+            def _(t=t):
+                for g in range(2):
+                    value_copy(micro, seq, head, t, g).start()
+
+        d_scores = jnp.where(
+            seen_mask(items, micro, seqs, mem), mm_nt(d_numer, values[...]) + d_denom, 0.0
+        )
+        query_halves, key_halves = halves_of(query_proj[...]), halves_of(keys[...])
+        d_key_halves = jnp.zeros_like(key_halves)
+        for by in (1, 2, 3):
+            d_feats = mm_tn(d_scores, query_halves * turned(query_halves, by))
+            d_key_halves += d_feats * turned(key_halves, by) + turned(d_feats * key_halves, -by)
+        d_keys[...] = halves_back(keys[...], d_key_halves)
+        for t in range(seqs):
+
+            @pl.when(t < seq)
+            def _(t=t):
+                key_copy(micro, seq, t).start()
+
+        d_query_halves = jnp.zeros_like(query_halves)
+        for by in (1, 2, 3):
+            d_feats = nn(d_scores, key_halves * turned(key_halves, by))
+            d_query_halves += d_feats * turned(query_halves, by) + turned(d_feats * query_halves, -by)
+        d_query = halves_back(query_proj[...], d_query_halves)
+        d_out[micro, own_rows] = grad + mm_nt(d_query, w_query[...])
+        local_copy = copy(
+            slot(micro, 1), d_out.at[micro, own_rows], d_out.at[micro, own_rows], partner
+        )
+        local_copy.start()
+        g_whole[0] += mm_tn(out_local[...], d_query)
+        for t in range(seqs):
+
+            @pl.when(t > seq)
+            def _(t=t):
+                key_copy(micro, t, t).wait_recv()
+                for g in range(2):
+                    value_copy(micro, t, g, t, g).wait_recv()
+
+        d_key_proj = jnp.sum(from_k[micro], axis=0)
+        d_value = jnp.sum(from_v[micro], axis=(0, 1))
+        mem_part[...] = mm_nt(d_key_proj, w_key[...]) + mm_nt(d_value, w_value[...])
+        mem_copy = copy(slot(micro, 2), mem_part, got_mem.at[micro], partner)
+        mem_copy.start()
+        g_whole[1] += mm_tn(out_mem[...], d_key_proj)
+        g_value[...] += mm_tn(out_mem[...], d_value)
+        mem_copy.wait_recv()
+        d_out[micro, segment:] = mem_part[...] + got_mem[micro]
+        local_copy.wait_recv()
+
+        add_small(30, 0.5 * column_sum(d_out[micro]))
+        for at, tile in inner_tiles:
+            cut = slice(at, at + tile)
+            activated, slope = gelu_parts(pre[:, cut])
+            made = slope * mm_nt(d_out[micro], w_down[cut])
+            pre[:, cut] = activated
+            d_pre[:, cut] = made
+            add_small(36 + at // 128, column_sum(made))
+
+        def mix_copy(index):
+            at, tile = column_tiles[index]
+            return copy(
+                slot(micro, 3 + index),
+                d_part.at[:, at : at + tile],
+                got_mix.at[micro, :, at : at + tile],
+                partner,
+            )
+
+        for index, (at, tile) in enumerate(column_tiles):
+            d_part[:, at : at + tile] = mm_nt(d_pre[...], w_up[at : at + tile])
+            mix_copy(index).start()
+        unit, inverse = unit_rows(hidden[...])
+        normed[...] = unit * gains[1:2] + biases[1:2]
+        for at, tile in inner_tiles:
+            cut = slice(at, at + tile)
+            g_down[cut] += mm_tn(pre[:, cut], d_out[micro])
+            g_up[:, cut] += mm_tn(normed[...], d_pre[:, cut])
+        for index, (at, tile) in enumerate(column_tiles):
+            cut = slice(at, at + tile)
+            mix_copy(index).wait_recv()
+            got_mix[micro, :, cut] += d_part[:, cut]
+        unit, inverse = unit_rows(hidden[...])
+        d_mixed = got_mix[micro]
+        add_small(6, 0.5 * column_sum(d_mixed * unit))
+        add_small(18, 0.5 * column_sum(d_mixed))
+        hidden[...] = d_out[micro] + unit_rows_back(d_mixed * gains[1:2], unit, inverse)
+        add_small(24, 0.5 * column_sum(hidden[...]))
+        for index in range(len(column_tiles)):
+            mix_copy(index).wait_send()
+
+        d_attended = mm_nt(hidden[...], w_out[...])
+        tops = lse[...]
+        for place in range(share // HEAD_DIM):
+            cut = slice(place * HEAD_DIM, (place + 1) * HEAD_DIM)
+            query, key, value = (
+                qkv[:, kind * share + place * HEAD_DIM : kind * share + (place + 1) * HEAD_DIM]
+                for kind in range(3)
+            )
+            scores = jnp.where(allowed, mm_nt(query, key) * SCALE, -1e30)
+            soft = jnp.exp(scores - tops[:, place : place + 1])
+            d_head = d_attended[:, cut]
+            inner_dot = jnp.sum(d_head * attended[:, cut], axis=1, keepdims=True)
+            d_scores = soft * (mm_nt(d_head, value) - inner_dot) * SCALE
+            for kind, made in enumerate(
+                (nn(d_scores, key), mm_tn(d_scores, query), mm_tn(soft, d_head))
+            ):
+                d_qkv[:, kind * share + place * HEAD_DIM : kind * share + (place + 1) * HEAD_DIM] = made
+        add_small(48, column_sum(d_qkv[:, :share]))
+        add_small(51, column_sum(d_qkv[:, 2 * share :]))
+
+        def rows_copies(index):
+            at, tile = column_tiles[index]
+            return (
+                copy(
+                    slot(micro, 3 + len(column_tiles) + index),
+                    d_part.at[other_rows, at : at + tile],
+                    got_rows.at[micro, pl.ds(0, local), at : at + tile],
+                    partner,
+                ),
+                copy(
+                    slot(micro, 3 + 2 * len(column_tiles) + index),
+                    d_part.at[pl.ds(segment, mem), at : at + tile],
+                    got_rows.at[micro, pl.ds(local, mem), at : at + tile],
+                    partner,
+                ),
+            )
+
+        for index, (at, tile) in enumerate(column_tiles):
+            made = mm_nt(d_qkv[:, :share], w_in[0, at : at + tile])
+            for kind in (1, 2):
+                made = made + mm_nt(
+                    d_qkv[:, kind * share : (kind + 1) * share], w_in[kind, at : at + tile]
+                )
+            d_part[:, at : at + tile] = made
+            for one in rows_copies(index):
+                one.start()
+        unit, inverse = unit_rows(rows[...])
+        normed[...] = unit * gains[0:1] + biases[0:1]
+        g_out[...] += mm_tn(attended[...], hidden[...])
+        for kind in range(3):
+            g_in[kind] += mm_tn(normed[...], d_qkv[:, kind * share : (kind + 1) * share])
+        for index in range(len(column_tiles)):
+            for one in rows_copies(index):
+                one.wait_recv()
+
+        def finish(d_normed, at_rows):
+            unit, inverse = unit_rows(rows[at_rows])
+            add_small(0, column_sum(d_normed * unit))
+            add_small(12, column_sum(d_normed))
+            return hidden[at_rows] + unit_rows_back(d_normed * gains[0:1], unit, inverse)
+
+        grad_x[micro] = finish(d_part[own_rows] + got_rows[micro, :local], own_rows)
+
+        @pl.when(section == 1)
+        def _():
+            grad_copy(micro).start()
+
+        mem_rows = rows_at(local + head * (mem // 2), mem // 2)
+        d_tokens = finish(d_part[own_mem_rows] + got_rows[micro, mem_rows], own_mem_rows)
+        for at in range(0, width, 128):
+            row = 56 + (at // 128) * (mem // 2)
+            g_small[row : row + mem // 2] += d_tokens[:, at : at + 128]
+
+        for index in range(len(column_tiles)):
+            for one in rows_copies(index):
+                one.wait_send()
+        local_copy.wait_send()
+        mem_copy.wait_send()
+        for t in range(seqs):
+
+            @pl.when(t < seq)
+            def _(t=t):
+                key_copy(micro, seq, t).wait_send()
+                for g in range(2):
+                    value_copy(micro, seq, head, t, g).wait_send()
+
+        return carry
+
+    lax.fori_loop(0, micro_total, one_micro, 0)
+
+    @pl.when(section == 1)
+    def _():
+        for micro in range(micro_total):
+            grad_copy(micro).wait_send()
+
+
+def ring_kernel(lanes, count, *refs):
+    arrays = refs[:count]
+    whole = refs[count]
+    small_index = count - 1
+    sums = refs[count + 1 : 2 * count + 1]
+    whole_sum = refs[2 * count + 1]
+    held = refs[2 * count + 2 : 3 * count + 3]
+    got_whole, got_small, send, recv, local, send_x, recv_x = refs[3 * count + 3 :]
+    seqs = lax.axis_size("seq")
+    along = seqs // lanes
+    seq, head = lax.axis_index("seq"), lax.axis_index("head")
+    other = 1 - head
+    z, y = seq // lanes, lax.rem(seq, lanes)
+    place = y * along + jnp.where(lax.rem(y, 2) == 0, z, along - 1 - z)
+
+    def device(spot):
+        row = spot // along
+        column = lax.rem(spot, along)
+        column = jnp.where(lax.rem(row, 2) == 0, column, along - 1 - column)
+        return {"seq": column * lanes + row}
+
+    targets = (device(lax.rem(place + 1, seqs)), device(lax.rem(place + seqs - 1, seqs)))
+    partner = {"head": other}
+    signs = (1, -1)
+    sources = [*arrays[:small_index], got_small, got_whole]
+    results = [*sums, whole_sum.at[head]]
+
+    def block(ref, way, spot):
+        rows = ref.shape[0] // seqs
+        half = rows // 2
+        spot = lax.rem(spot + 2 * seqs, seqs)
+        return ref.at[pl.ds(pl.multiple_of(spot * rows + way * half, half), half)]
+
+    def copy(source, target, way, index, step):
+        return pltpu.make_async_remote_copy(
+            src_ref=source,
+            dst_ref=target,
+            send_sem=send.at[step, way, index],
+            recv_sem=recv.at[step, way, index],
+            device_id=targets[way],
+            device_id_type=MESH,
+        )
+
+    def across(source, target, number):
+        return pltpu.make_async_remote_copy(
+            src_ref=source,
+            dst_ref=target,
+            send_sem=send_x.at[number],
+            recv_sem=recv_x.at[number],
+            device_id=partner,
+            device_id_type=MESH,
+        )
+
+    def hand_over(way, spot, step):
+        mine = block(whole_sum.at[head], way, spot)
+        return across(mine, mine, 2 + way * seqs + step)
+
+    ways = [(index, way) for index in range(count + 1) for way in range(2)]
+    last = seqs - 2
+    barrier_with([(place >= 0, target) for target in (*targets, partner)], place * 0 + 3)
+    whole_copy = across(whole.at[other], got_whole, 0)
+    whole_copy.start()
+    small_copy = across(arrays[small_index], got_small, 1)
+    small_copy.start()
+    for index, way in ways:
+        if index == small_index and way == 0:
+            small_copy.wait()
+            got_small[0:SHARED_ROWS] += arrays[small_index][0:SHARED_ROWS]
+            got_small[SHARED_ROWS:] = arrays[small_index][SHARED_ROWS:]
+        if index == count and way == 0:
+            whole_copy.wait()
+            got_whole[...] += whole[head]
+        copy(block(sources[index], way, place), held[index].at[way, 0], way, index, 0).start()
+
+    def forward(step, carry):
+        for index, way in ways:
+            got = held[index].at[way, step - 1]
+            copy(got, got, way, index, step - 1).wait_recv()
+            got[...] += block(sources[index], way, place - signs[way] * step)[...]
+            copy(got, held[index].at[way, step], way, index, step).start()
+        return carry
+
+    lax.fori_loop(1, seqs - 1, forward, 0)
+    for index, way in ways:
+        got = held[index].at[way, last]
+        copy(got, got, way, index, last).wait_recv()
+        spot = place + signs[way]
+        got[...] += block(sources[index], way, spot)[...]
+        home = block(results[index], way, spot)
+        copy(got, home, way, index, seqs - 1).start()
+        pltpu.make_async_copy(got, home, local.at[way, index]).start()
+        if index == count:
+            across(got, home, 2 + way * seqs).start()
+
+    def onward(step, carry):
+        for index, way in ways:
+            spot = place - signs[way] * (step - 1)
+            got = block(results[index], way, spot)
+            copy(got, got, way, index, seqs - 1 + step - 1).wait_recv()
+            copy(got, got, way, index, seqs - 1 + step).start()
+            if index == count:
+                hand_over(way, spot, step).start()
+        return carry
+
+    lax.fori_loop(1, seqs - 1, onward, 0)
+    for index, way in ways:
+        spot = place - signs[way] * last
+        got = block(results[index], way, spot)
+        copy(got, got, way, index, 2 * seqs - 3).wait_recv()
+        if index == count:
+            hand_over(way, spot, seqs - 1).start()
+        own = held[index].at[way, last]
+        home = block(results[index], way, place + signs[way])
+        pltpu.make_async_copy(own, home, local.at[way, index]).wait()
+
+    def sent(step, carry):
+        for index, way in ways:
+            own = held[index].at[way, 0]
+            copy(own, own, way, index, step).wait_send()
+        return carry
+
+    lax.fori_loop(0, 2 * seqs - 2, sent, 0)
+
+    def crossed(step, carry):
+        for way in range(2):
+            spot = place - signs[way] * (step - 1)
+            theirs = block(whole_sum.at[other], way, spot)
+            across(theirs, theirs, 2 + way * seqs + step).wait()
+        return carry
+
+    lax.fori_loop(0, seqs, crossed, 0)
+
+
+def shapes_of(*shapes):
+    return tuple(jax.ShapeDtypeStruct(shape, jnp.float32) for shape in shapes)
+
+
+def buffers(*shapes):
+    return [pltpu.VMEM(shape, jnp.float32) for shape in shapes]
+
+
+def dma(*shape):
+    return pltpu.SemaphoreType.DMA(shape)
+
+
+def params_of(number):
+    return pltpu.CompilerParams(
+        collective_id=number, has_side_effects=True, vmem_limit_bytes=62 << 20
+    )
+
+
+def shards_of_two(
+    boundary_in,
+    short_items,
+    norm_gains,
+    norm_biases,
+    projection_in,
+    head_bias,
+    projection_out,
+    residual_bias,
+    up_weight,
+    up_bias,
+    down_weight,
+    memory_tokens,
+    query_memory,
+    key_memory,
+    value_memory,
+):
+    seqs = lax.axis_size("seq")
+    x = boundary_in[0]
+    micros, local, width = x.shape
+    w_in = projection_in[0].transpose(1, 0, 2)
+    share = w_in.shape[2]
+    inner = up_weight.shape[2]
+    half_mem = memory_tokens.shape[1]
+    mem = 2 * half_mem
+    segment = 2 * local
+    total = segment + mem
+    dk, dv = key_memory.shape[2], value_memory.shape[2]
+    stored = seqs * mem
+    tiles = len(lane_tiles(width))
+    slots = 3 + 3 * tiles
+    record_shapes = dict(
+        rows=(total, width),
+        qkv=(total, 3 * share),
+        attended=(total, share),
+        lse=(total, 128),
+        hidden=(total, width),
+        pre=(total, inner),
+        out_local=(local, width),
+        out_mem=(mem, width),
+        keys=(stored, dk),
+        values=(stored, 2 * dv),
+        query_proj=(local, dk),
+        weights=(local, stored),
+        read=(local, width),
+    )
+    memory_sems = [dma(micros, seqs), dma(micros, seqs), dma(micros, seqs, 2), dma(micros, seqs, 2)]
+    weights = (
+        norm_gains[0],
+        norm_biases[0],
+        w_in,
+        head_bias[0],
+        projection_out[0],
+        residual_bias[0],
+        up_weight[0],
+        up_bias,
+        down_weight[0],
+        memory_tokens[0],
+        query_memory[0],
+        key_memory[0],
+        value_memory[0],
+    )
+    *records, y = pl.pallas_call(
+        forward_kernel,
+        out_shape=shapes_of(
+            *((micros, *record_shapes[name]) for name in RECORDS), (micros, local, width)
+        ),
+        in_specs=[SMEM] + [VMEM] * (1 + len(weights)),
+        out_specs=(VMEM,) * (len(RECORDS) + 1),
+        scratch_shapes=buffers(
+            (total, width),
+            (total, width),
+            (micros, total, width),
+            (total, inner),
+            (micros, local + mem, width),
+            (mem, width),
+            (mem, dk),
+            (mem, dv),
+        )
+        + [dma(1 + micros * slots), dma(1 + micros * slots), *memory_sems],
+        compiler_params=params_of(0),
+        name="forward",
+    )(short_items, x, *weights)
+    gradient_shapes = (
+        (3, width, share),
+        (share, width),
+        (width, inner),
+        (inner, width),
+        (width, dv),
+        (2, width, dk),
+        (16 * seqs, 128),
+    )
+    *gradients, grad_x = pl.pallas_call(
+        backward_kernel,
+        out_shape=shapes_of(*gradient_shapes, (micros, local, width)),
+        in_specs=[SMEM] + [VMEM] * 10 + [HBM] * len(RECORDS),
+        out_specs=(VMEM,) * 8,
+        scratch_shapes=buffers(
+            *(record_shapes[name] for name in RECORDS),
+            (micros, total, width),
+            (total, width),
+            (total, inner),
+            (total, width),
+            (micros, total, width),
+            (total, 3 * share),
+            (micros, local + mem, width),
+            (micros, seqs, mem, dk),
+            (micros, seqs, 2, mem, dv),
+            (stored, dk),
+            (stored, 2 * dv),
+            (mem, width),
+            (micros, mem, width),
+            (micros, local, width),
+        )
+        + [dma(len(RECORDS)), dma(micros * slots), dma(micros * slots), *memory_sems],
+        compiler_params=params_of(1),
+        name="backward",
+    )(
+        short_items,
+        x,
+        norm_gains[0],
+        norm_biases[0],
+        w_in,
+        projection_out[0],
+        up_weight[0],
+        down_weight[0],
+        query_memory[0],
+        key_memory[0],
+        value_memory[0],
+        *records,
+    )
+    g_in, g_out, g_up, g_down, g_value, g_whole, g_small = gradients
+    arrays = (g_down, g_up, g_in.reshape(3 * width, share), g_out, g_value, g_small)
+    count = len(arrays)
+    held = [(a.shape[0], a.shape[1]) for a in (*arrays, g_whole[0])]
+    g_down, g_up, g_in, g_out, g_value, small, whole = pl.pallas_call(
+        functools.partial(ring_kernel, 2, count),
+        out_shape=shapes_of(*(a.shape for a in arrays), g_whole.shape),
+        in_specs=[VMEM] * (count + 1),
+        out_specs=(HBM,) * (count + 1),
+        scratch_shapes=buffers(
+            *((2, seqs - 1, rows // (2 * seqs), columns) for rows, columns in held),
+            (width, dk),
+            g_small.shape,
+        )
+        + [
+            dma(2 * seqs - 2, 2, count + 1),
+            dma(2 * seqs - 2, 2, count + 1),
+            dma(2, count + 1),
+            dma(2 + 2 * seqs),
+            dma(2 + 2 * seqs),
+        ],
+        compiler_params=params_of(2),
+        name="ring",
+    )(*arrays, g_whole)
+    section = lax.axis_index("section")
+    vectors = small[:36].reshape(3, 1, 2, width)
+    return (
+        jnp.where(section == 0, grad_x, y)[None],
+        vectors[0],
+        vectors[1],
+        g_in.reshape(3, width, share).transpose(1, 0, 2)[None],
+        small[48:54].reshape(1, 2, share),
+        g_out[None],
+        vectors[2],
+        g_up[None],
+        small[36:48].reshape(1, inner),
+        g_down[None],
+        small[56 : 56 + 6 * half_mem]
+        .reshape(6, half_mem, 128)
+        .transpose(1, 0, 2)
+        .reshape(1, half_mem, width),
+        whole[0][None],
+        whole[1][None],
+        g_value[None],
+    )
+
+
 def solution(mesh):
     return jax.shard_map(
-        shards,
+        shards_of_two if mesh.shape["head"] == 2 else shards,
         mesh=mesh,
         in_specs=(
             P("section", None, ("seq", "head"), None),

time: 1460 us -> 674 us (0.46)
  waiting for transfers between devices: 691 us -> 0 us
  Pallas kernels: 0 us -> 639 us
  matrix products: 251 us -> 0 us
  blocking collectives: 234 us -> 0 us
  local copies, waits for them, and re-layouts: 137 us -> 19.1 us
  other arithmetic: 80.4 us -> 2.11 us
  starting transfers between devices: 37.5 us -> 0 us
  between operations: 20.8 us -> 0.91 us
    pallas_call x0 -> x3, Pallas kernels: none -> 639 us  [the longest x1 283 us: shards_of_two(): pl.pallas_call(functools.partial(ring_kernel, 2, count), out_shape=shapes...]
    psum x2 -> x0, waiting for transfers between devices: 443 us -> none  [the longest x1 311 us: shards(): lax.psum(sharded, 'seq')]
    dot_general x99 -> x0, matrix products: 251 us -> none  [the longest x81 215 us: mm(): lax.dot_general(left, right, (dims, ((), ())), precision=lax.Precision.HI...]
    reduce_scatter x6 -> x0, waiting for transfers between devices: 148 us -> none  [the longest x3 142 us: layer_backward(): lax.psum_scatter(jnp.concatenate([d_keys, d_values], axis=1), 'seq', scat...]
    all_gather x7 -> x0, blocking collectives: 119 us -> none  [the longest x3 93.9 us: layer_forward(): lax.all_gather(jnp.concatenate([key_proj, values], axis=1), 'seq', axis=0...]
    psum x2 -> x0, blocking collectives: 115 us -> none  [the longest x1 77 us: shards(): lax.psum(shared, ('seq', 'head'))]
    ppermute x31 -> x0, waiting for transfers between devices: 99.7 us -> none  [the longest x27 96.3 us: swap(): return lax.ppermute(value, 'head', [(0, 1), (1, 0)])]
    slice x103 -> x2, local copies, waits for them, and re-layouts: 66.3 us -> 4.15 us  [the longest x1 3.48 us: shards_of_two(): whole[1][None]]
  transfers between devices with their start and end apart: 39 -> 0, of which waited for: 27 -> 0; matrix products, arithmetic and copies ran while one was open for 16% -> 0% of each run, Pallas kernels for 0% -> 0%
where the time goes in v3:
time: 674 us; the launch traced here: 662 us
  Pallas kernels  639 us (95%)
  local copies, waits for them, and re-layouts  19.1 us (3%)
    pallas_call x1, Pallas kernels, shards_of_two(): pl.pallas_call(functools.partial(ring_kernel, 2, count), out_shape=shapes...  283 us
    pallas_call x1, Pallas kernels, shards_of_two(): pl.pallas_call(backward_kernel, out_shape=shapes_of(*gradient_shapes, (mi...  250 us
    pallas_call x1, Pallas kernels, shards_of_two(): pl.pallas_call(forward_kernel, out_shape=shapes_of(*((micros, *record_sha...  106 us

profile of v3, /device:TPU:0, one launch (start us, length us, event | category | flops | bytes accessed | tf_op | source)
XLA Modules:
  0.0 661.6 jit_solution(9669339516283239227)
XLA Ops:
  0.7 106.4 %forward.1 = (f32[2,272,768]{2,1,0:T(8,128)}, f32[2,272,1152]{2,1,0:T(8,128)}, f32[2,272,384]{2,1,0:T(8,128)}, f32[2,272,128]{2,1,0:T(8,128)}, f32[2,272,768]{2,...) custom-call(s32[1,3]{1,0:T(1,128)} %items.3, ...), custom_call_target="tpu_custom_call" | custom-call | tf_op jit(solution)/shard_map/forward/pallas_call | solution.py:1257
  107.0 0.0 copy-start.3
  107.0 249.8 %backward.1 = (f32[3,768,384]{2,1,0:T(8,128)}, f32[384,768]{1,0:T(8,128)}, f32[768,1536]{1,0:T(8,128)}, f32[1536,768]{1,0:T(8,128)}, f32[768,384]{1,0:T(8,128)},...) custom-call(s32[1,3]{1,0:T(1,128)} %items.3, f32[2,128,768]{2,1,0:T(8,128)} %bitcast.62, ...), custom_call_target="tpu_custom_call" | custom-call | tf_op jit(solution)/shard_map/backward/pallas_call | solution.py:1287
  356.9 0.0 copy-done.3
  356.9 2.1 select_bitcast_fusion
  359.0 283.3 %ring.1 = (f32[1536,768]{1,0:T(8,128)}, f32[768,1536]{1,0:T(8,128)}, f32[2304,384]{1,0:T(8,128)}, f32[384,768]{1,0:T(8,128)}, f32[768,384]{1,0:T(8,128)}, /*index=5*/f32[128,128]{1,0:T(8,128)}, f32[2,768,384]{2,1,0:T(8,128)}) custom-call(f32[1536,768]{1,0:T(8,128)} %get-tuple-element.58.refs_0_, f32[768,1536]{1,0:T(8,128)} %get-tuple-element.59.refs_1_, ...), custom_call_target="tpu_custom_call" | custom-call | tf_op jit(solution)/shard_map/ring/pallas_call | solution.py:1330
  642.3 0.7 slice.33
  643.0 0.6 reshape.55
  643.6 1.3 slice_bitcast_fusion
  644.9 0.8 slice_bitcast_fusion.1
  645.7 0.6 copy.31
  646.3 0.6 squeeze.71
  646.9 0.6 squeeze.70
  647.5 0.0 copy-start
  647.5 0.6 squeeze.69
  648.1 0.0 slice-start.2
  648.1 3.5 fusion
  651.6 0.0 copy-done
  651.6 0.0 copy-start.2
  651.6 0.0 slice-start.3
  651.6 1.8 copy.37
  653.4 0.3 copy-done.2
  653.7 0.0 slice-start
  653.7 1.0 copy.38
  654.7 0.0 slice-done.2
  654.7 0.0 slice-done.3
  654.7 0.0 slice-start.1
  654.7 2.4 copy.39
  657.1 0.8 slice-done
  657.9 0.3 slice-done.1
  658.2 0.0 copy-start.1
  658.2 2.2 copy.40
  660.4 0.0 copy-done.1
  660.4 1.0 copy.41
  (2 shorter events, 0.0 us)
Async XLA Ops:
  107.0 249.9 %copy-start.3 = (f32[2,128,768]{2,1,0:T(8,128)S(1)}, f32[2,128,768]{2,1,0:T(8,128)}, u32[]{:S(2)}) copy-start(f32[2,128,768]{2,1,0:T(8,128)} %get-tuple-element.57) | copy-start | bytes 2359300
  647.5 4.1 copy-start
  648.1 6.6 slice-start.2
  651.6 2.1 copy-start.2
  651.6 3.1 slice-start.3
  653.7 4.3 slice-start
  654.7 3.5 slice-start.1
  658.2 2.2 copy-start.1

commit v4 on v1

v4 whole, which is shorter than its diff:
```python
import functools
import math
from types import SimpleNamespace

import jax
import jax.numpy as jnp
from jax import lax
from jax.experimental import pallas as pl
from jax.experimental.pallas import tpu as pltpu
from jax.sharding import PartitionSpec as P

SECTION, SEQ, HEAD = "section", "seq", "head"
HEAD_DIM = 64
EPSILON = 1e-05
SCALE = 1.0 / math.sqrt(HEAD_DIM)
MESH = pl.DeviceIdType.MESH
VMEM = pl.BlockSpec(memory_space=pltpu.VMEM)
HBM = pl.BlockSpec(memory_space=pltpu.HBM)
SMEM = pl.BlockSpec(memory_space=pltpu.SMEM)
SHARED_ROWS = 36


def mm(left, right, dims=((1,), (0,))):
    return lax.dot_general(
        left, right, (dims, ((), ())), precision=lax.Precision.HIGH, preferred_element_type=jnp.float32
    )


def mm_nt(left, right):
    return mm(left, right, ((1,), (1,)))


def mm_tn(left, right):
    return mm(left, right, ((0,), (0,)))


def unit_rows(rows):
    centred = rows - jnp.mean(rows, axis=-1, keepdims=True)
    inverse = lax.rsqrt(jnp.mean(centred * centred, axis=-1, keepdims=True) + EPSILON)
    return centred * inverse, inverse


def unit_rows_back(d_unit, unit, inverse):
    return inverse * (
        d_unit
        - jnp.mean(d_unit, axis=-1, keepdims=True)
        - unit * jnp.mean(d_unit * unit, axis=-1, keepdims=True)
    )


def features(projected):
    halves = jnp.concatenate([jax.nn.softplus(projected), jax.nn.softplus(-projected)], axis=-1)
    return jnp.concatenate(
        [halves * jnp.roll(halves, rolled_by, axis=-1) for rolled_by in (1, 2, 3)], axis=-1
    )


def gelu_tanh(values_in):
    return jax.nn.gelu(values_in, approximate=True)


def head_sum_rows(rows, share):
    segment = lax.axis_size(HEAD) * share
    turn = lax.axis_index(HEAD) * share
    total = lax.psum(
        jnp.concatenate([jnp.roll(rows[:segment], turn, axis=0), rows[segment:]], axis=0), HEAD
    )
    return jnp.concatenate([jnp.roll(total[:segment], -turn, axis=0), total[segment:]], axis=0)


def head_rows(local):
    gathered = lax.all_gather(local, HEAD, axis=0, tiled=True)
    return jnp.roll(gathered, -lax.axis_index(HEAD) * local.shape[0], axis=0)


def head_scatter(rows):
    share = rows.shape[0] // lax.axis_size(HEAD)
    placed = jnp.roll(rows, lax.axis_index(HEAD) * share, axis=0)
    return lax.psum_scatter(placed, HEAD, scatter_dimension=0, tiled=True)


def heads_of(part):
    return part.reshape(part.shape[0], -1, HEAD_DIM).transpose(1, 0, 2)


def rows_of(part):
    return part.transpose(1, 0, 2).reshape(part.shape[1], -1)


def bmm(left, right, left_dim, right_dim):
    return lax.dot_general(
        left,
        right,
        (((left_dim,), (right_dim,)), ((0,), (0,))),
        precision=lax.Precision.HIGH,
        preferred_element_type=jnp.float32,
    )


def layer_forward(local, params, mask, allowed):
    width = local.shape[1]
    local_count = local.shape[0]
    segment = lax.axis_size(HEAD) * local_count
    rows = jnp.concatenate([head_rows(local), params.memory], axis=0)
    unit_one, inverse_one = unit_rows(rows)
    normed = unit_one * params.gains[0] + params.biases[0]
    projected = mm(normed, params.proj_in) + params.in_bias
    share = projected.shape[1] // 3
    query, key, value = (heads_of(projected[:, i * share : (i + 1) * share]) for i in range(3))
    scores = jnp.where(allowed, bmm(query, key, 2, 2) * SCALE, -1e30)
    row_top = jnp.max(scores, axis=-1, keepdims=True)
    exponent = jnp.exp(scores - row_top)
    soft = exponent / jnp.sum(exponent, axis=-1, keepdims=True)
    attended = rows_of(bmm(soft, value, 2, 1))
    hidden = rows + head_sum_rows(mm(attended, params.proj_out), local_count) + params.residual[0]
    unit_two, inverse_two = unit_rows(hidden)
    mixed = unit_two * params.gains[1] + params.biases[1]
    inner_pre = mm(mixed, params.up) + params.up_bias
    inner_act = gelu_tanh(inner_pre)
    partial = mm(inner_act, params.down)
    out_local = head_scatter(partial[:segment]) + hidden[:local_count] + params.residual[1]
    out_mem = lax.psum(partial[segment:], HEAD) + hidden[segment:] + params.residual[1]
    key_proj = mm(out_mem, params.key_mem)
    values = mm(out_mem, params.value_mem)
    gathered = lax.all_gather(jnp.concatenate([key_proj, values], axis=1), SEQ, axis=0, tiled=True)
    dk = key_proj.shape[1]
    keys_all = gathered[:, :dk]
    values_all = lax.all_gather(gathered[:, dk:], HEAD, axis=1, tiled=True)
    key_feats = features(keys_all)
    query_proj = mm(out_local, params.query_mem)
    query_feats = features(query_proj)
    weights = mask * mm_nt(query_feats, key_feats)
    denominator = jnp.sum(weights, axis=1, keepdims=True) + 1.0
    read = mm(weights, values_all) / denominator
    return SimpleNamespace(
        unit_one=unit_one,
        inverse_one=inverse_one,
        projected=projected,
        attended=attended,
        soft=soft,
        unit_two=unit_two,
        inverse_two=inverse_two,
        inner_pre=inner_pre,
        out_local=out_local,
        out_mem=out_mem,
        keys_all=keys_all,
        values_all=values_all,
        query_proj=query_proj,
        weights=weights,
        denominator=denominator,
        read=read,
        output=out_local + read,
    )


def layer_backward(grad, record, params, mask):
    head_count = lax.axis_size(HEAD)
    seq_count = lax.axis_size(SEQ)
    width = grad.shape[1]
    local_count = grad.shape[0]
    segment = head_count * local_count
    denominator = record.denominator
    d_numer = grad / denominator
    d_denom = -jnp.sum(grad * record.read, axis=1, keepdims=True) / denominator
    d_weights = mask * (mm_nt(d_numer, record.values_all) + d_denom)
    key_feats, keys_back = jax.vjp(features, record.keys_all)
    query_feats, query_back = jax.vjp(features, record.query_proj)
    d_query_proj = query_back(mm(d_weights, key_feats))[0]
    d_keys = keys_back(mm_tn(d_weights, query_feats))[0]
    d_values = mm_tn(record.weights, d_numer)
    d_memory = lax.psum_scatter(
        jnp.concatenate([d_keys, d_values], axis=1), SEQ, scatter_dimension=0, tiled=True
    )
    dk = d_keys.shape[1]
    d_key_proj = d_memory[:, :dk]
    d_value = lax.psum_scatter(
        d_memory[:, dk:], HEAD, scatter_dimension=1, tiled=True
    )
    d_mem = lax.psum(
        mm_nt(d_key_proj, params.key_mem) + mm_nt(d_value, params.value_mem), HEAD
    )
    d_local = grad + mm_nt(d_query_proj, params.query_mem)
    d_result = jnp.concatenate([head_rows(d_local), d_mem], axis=0)
    inner_act, gelu_back = jax.vjp(gelu_tanh, record.inner_pre)
    grad_down = mm_tn(inner_act, d_result)
    d_pre = gelu_back(mm_nt(d_result, params.down))[0]
    gains, biases = params.gains, params.biases
    mixed = record.unit_two * gains[1] + biases[1]
    grad_up = mm_tn(mixed, d_pre)
    d_mixed = head_sum_rows(mm_nt(d_pre, params.up), local_count)
    d_hidden = d_result + unit_rows_back(d_mixed * gains[1], record.unit_two, record.inverse_two)
    grad_out = mm_tn(record.attended, d_hidden)
    d_attended = mm_nt(d_hidden, params.proj_out)
    share = d_attended.shape[1]
    query, key, value = (
        heads_of(record.projected[:, i * share : (i + 1) * share]) for i in range(3)
    )
    soft = record.soft
    d_heads = heads_of(d_attended)
    inner_dot = jnp.sum(d_heads * heads_of(record.attended), axis=-1, keepdims=True)
    d_scores = soft * (bmm(d_heads, value, 2, 2) - inner_dot) * SCALE
    d_projected = jnp.concatenate(
        [
            rows_of(bmm(d_scores, key, 2, 1)),
            rows_of(bmm(d_scores, query, 1, 1)),
            rows_of(bmm(soft, d_heads, 1, 1)),
        ],
        axis=1,
    )
    normed = record.unit_one * gains[0] + biases[0]
    grad_in = mm_tn(normed, d_projected)
    columns = jnp.sum(d_projected, axis=0)
    grad_head_bias = jnp.stack([columns[:share], columns[2 * share :]])
    d_normed_all = mm_nt(d_projected, params.proj_in)
    d_normed = head_scatter(d_normed_all[:segment])
    d_normed_mem = lax.psum_scatter(
        d_normed_all[segment:], HEAD, scatter_dimension=0, tiled=True
    )
    mem_count = d_normed_mem.shape[0]
    own_mem = segment + lax.axis_index(HEAD) * mem_count

    def own(values):
        return jnp.concatenate(
            [values[:local_count], lax.dynamic_slice_in_dim(values, own_mem, mem_count, 0)], axis=0
        )

    d_normed_own = jnp.concatenate([d_normed, d_normed_mem], axis=0)
    unit_own = own(record.unit_one)
    d_rows = own(d_hidden) + unit_rows_back(
        d_normed_own * gains[0], unit_own, own(record.inverse_one)
    )
    part = 1.0 / head_count
    sharded = (
        grad_in,
        grad_head_bias,
        grad_out,
        grad_up,
        jnp.sum(d_pre, axis=0),
        grad_down,
        d_rows[local_count:],
        mm_tn(record.out_mem, d_value),
    )
    shared = (
        jnp.stack(
            [
                jnp.sum(d_normed_own * unit_own, axis=0),
                part * jnp.sum(d_mixed * record.unit_two, axis=0),
            ]
        ),
        jnp.stack([jnp.sum(d_normed_own, axis=0), part * jnp.sum(d_mixed, axis=0)]),
        part * jnp.stack([jnp.sum(d_hidden, axis=0), jnp.sum(d_result, axis=0)]),
        mm_tn(record.out_local, d_query_proj),
        mm_tn(record.out_mem, d_key_proj),
    )
    return (d_rows[:local_count], sharded, shared)


def passed_along(value, axis, steps):
    count = lax.axis_size(axis)
    first, last = (max(0, -steps), min(count, count - steps))
    return lax.ppermute(value, axis, [(source, source + steps) for source in range(first, last)])


def shards(
    boundary_in,
    short_items,
    norm_gains,
    norm_biases,
    projection_in,
    head_bias,
    projection_out,
    residual_bias,
    up_weight,
    up_bias,
    down_weight,
    memory_tokens,
    query_memory,
    key_memory,
    value_memory,
):
    section = lax.axis_index(SECTION)
    sections = lax.axis_size(SECTION)
    head_count = lax.axis_size(HEAD)
    head_place = lax.axis_index(HEAD)
    seq_count = lax.axis_size(SEQ)
    seq_place = lax.axis_index(SEQ)
    micro_total = boundary_in.shape[1]
    local_count = boundary_in.shape[2]
    width = boundary_in.shape[3]
    segment = head_count * local_count
    head_width = projection_in.shape[3]
    memory_all = lax.all_gather(memory_tokens[0], HEAD, axis=0, tiled=True)
    mem_count = memory_all.shape[0]
    params = SimpleNamespace(
        gains=norm_gains[0],
        biases=norm_biases[0],
        proj_in=projection_in[0].reshape(width, 3 * head_width),
        in_bias=jnp.concatenate(
            [head_bias[0, 0], jnp.zeros((head_width,), jnp.float32), head_bias[0, 1]]
        ),
        proj_out=projection_out[0],
        residual=residual_bias[0],
        up=up_weight[0],
        up_bias=up_bias[0],
        down=down_weight[0],
        memory=memory_all,
        query_mem=query_memory[0],
        key_mem=key_memory[0],
        value_mem=value_memory[0],
    )
    ordinal = jnp.arange(segment)
    places = jnp.concatenate(
        [(ordinal + head_place * local_count) % segment, segment + jnp.arange(mem_count)]
    )
    allowed = (places[:, None] >= places[None, :])[None]

    positions = jnp.arange(seq_count)
    masks = []
    for micro in range(micro_total):
        if micro == 0:
            item = jnp.zeros((seq_count,), jnp.int32)
        else:
            ends = jnp.cumsum(short_items[micro - 1])
            item = jnp.sum((positions[:, None] >= ends[None, :]).astype(jnp.int32), axis=1)
        own_item = jnp.sum(jnp.where(positions == seq_place, item, 0))
        seen = jnp.logical_and(positions < seq_place, item == own_item).astype(jnp.float32)
        masks.append(jnp.repeat(seen, mem_count)[None, :])
    masks = jnp.stack(masks)

    tick_total = micro_total + sections - 1
    received = jnp.zeros_like(boundary_in[0, 0])
    records = []
    for tick in range(tick_total):
        micro = jnp.clip(tick - section, 0, micro_total - 1)
        local = jnp.where(section == 0, boundary_in[0, min(tick, micro_total - 1)], received)
        records.append(layer_forward(local, params, masks[micro], allowed))
        if tick + 1 < tick_total:
            received = passed_along(records[-1].output, SECTION, 1)
    back_received = jnp.zeros_like(boundary_in[0, 0])
    grads_input = []
    total = None
    for tick in range(tick_total):
        raw = tick - (sections - 1 - section)
        valid = jnp.logical_and(raw >= 0, raw < micro_total)
        micro = jnp.clip(raw, 0, micro_total - 1)
        grad = jnp.where(
            section == sections - 1, boundary_in[0, min(tick, micro_total - 1)], back_received
        )
        kept = [
            vars(records[min(max(tick - (sections - 1 - place), 0), micro_total - 1) + place])
            for place in range(sections)
        ]
        record = SimpleNamespace(
            **jax.tree.map(lambda *kinds: lax.select_n(section, *kinds), *kept)
        )
        grad_x, sharded, shared = layer_backward(grad, record, params, masks[micro])
        fresh = jax.tree.map(lambda part: jnp.where(valid, part, 0.0), (sharded, shared))
        total = fresh if total is None else jax.tree.map(jnp.add, total, fresh)
        grads_input.append(grad_x)
        if tick + 1 < tick_total:
            back_received = passed_along(grad_x, SECTION, -1)
    sharded, shared = total
    grad_in, grad_heads_bias, grad_out, grad_up, grad_up_b, grad_down, grad_mem, grad_value = lax.psum(
        sharded, SEQ
    )
    grad_gains, grad_biases, grad_residual, grad_query, grad_key = lax.psum(shared, (SEQ, HEAD))
    finished_grads = jnp.stack(
        [grads_input[micro + sections - 1] for micro in range(micro_total)]
    )
    finished_outputs = jnp.stack(
        [records[micro + sections - 1].output for micro in range(micro_total)]
    )
    boundary_out = jnp.where(section == 0, finished_grads, finished_outputs)[None]
    return (
        boundary_out,
        grad_gains[None],
        grad_biases[None],
        grad_in.reshape(projection_in.shape),
        grad_heads_bias[None],
        grad_out[None],
        grad_residual[None],
        grad_up[None],
        grad_up_b[None],
        grad_down[None],
        grad_mem[None],
        grad_query[None],
        grad_key[None],
        grad_value[None],
    )


def barrier_with(pairs, wait_count):
    barrier = pltpu.get_barrier_semaphore()
    for condition, device in pairs:

        @pl.when(condition)
        def _(device=device):
            pl.semaphore_signal(barrier, inc=1, device_id=device, device_id_type=MESH)

    @pl.when(wait_count > 0)
    def _():
        pl.semaphore_wait(barrier, wait_count)


def nn(left, right):
    return mm(left, right)


def lane_tiles(width):
    tile = 256 if width % 256 == 0 else width
    return [(at, tile) for at in range(0, width, tile)]


def rows_at(start, count):
    return pl.ds(pl.multiple_of(start, count), count)


def halves_of(projected):
    small = jnp.log1p(jnp.exp(-jnp.abs(projected)))
    return jnp.concatenate(
        [jnp.maximum(projected, 0.0) + small, jnp.maximum(-projected, 0.0) + small], axis=1
    )


def halves_back(projected, d_halves):
    width = projected.shape[1]
    rising = 1.0 / (1.0 + jnp.exp(-projected))
    falling = 1.0 / (1.0 + jnp.exp(projected))
    return d_halves[:, :width] * rising - d_halves[:, width:] * falling


def turned(values, by):
    return pltpu.roll(values, by % values.shape[1], 1)


GELU_IN = math.sqrt(2.0 / math.pi)


def gelu_parts(pre):
    cubic = 0.044715 * pre * pre
    bent = jnp.tanh(GELU_IN * pre * (1.0 + cubic))
    half = 0.5 * (1.0 + bent)
    slope = half + 0.5 * pre * (1.0 - bent * bent) * GELU_IN * (1.0 + 3.0 * cubic)
    return pre * half, slope


def seen_mask(items, micro, seqs, mem):
    seq = lax.axis_index(SEQ)
    row_seq = lax.div(lax.broadcasted_iota(jnp.int32, (1, seqs * mem), 1), jnp.int32(mem))
    end = jnp.int32(0)
    own = jnp.int32(0)
    item = jnp.zeros((1, seqs * mem), jnp.int32)
    for piece in range(items.shape[1]):
        end = end + items[jnp.maximum(micro - 1, 0), piece]
        bound = jnp.where(micro == 0, seqs, end)
        own = own + (seq >= bound).astype(jnp.int32)
        item = item + (row_seq >= bound).astype(jnp.int32)
    return jnp.logical_and(row_seq < seq, item == own)


WEIGHTS = IN, UP, DOWN, VALUE, QUERY, KEY = tuple(range(6))
COPIES = (1, 2, 3, 3, 3, 1, 1, 1, 3, 3, 3)
(X_IN, Y_OUT, PART, LOCAL, MEMORY, GRAD, D_LOCAL, D_MEMORY, MIX, ROWS, ROWS_MEMORY) = range(11)
COPY_SLOTS = sum(COPIES)
TOKENS, OUT_SHARE = range(2)


def copy_slot(micro, kind, index=0):
    return 2 + micro * COPY_SLOTS + sum(COPIES[:kind]) + index


def column_sum(values_in):
    return jnp.sum(values_in, axis=0, keepdims=True)


SLOTS = 3


def layers_kernel(lanes, *refs):
    refs = list(refs)

    def take(count):
        taken, refs[:] = refs[:count], refs[count:]
        return taken

    items, x, gains, biases, head_bias, residual, b_up, mem_tokens = take(8)
    weights_in = take(len(WEIGHTS))
    (w_out_in,) = take(1)
    down_sum, up_sum, in_sum, out_sum, value_sum, small_sum, whole_sum = take(7)
    y, grad_x = take(2)
    held = take(len(WEIGHTS))
    w_in, w_up, w_down, w_value, w_query, w_key = held
    rows, qkv, attended, lse, hidden, pre = take(6)
    out_local, out_mem, keys, values, query_proj, weights, read = take(7)
    w_out_all, got_attended = take(2)
    (
        normed, d_pre, d_out, part, got_part, got_out, mem_all, key_block, value_block, from_k, from_v,
        mem_part, got_mem, grad_y, wide_scores, wide_soft, wide_query, wide_grad,
        g_small, got_small, got_whole,
    ) = take(21)
    d_keys, d_values = keys, read
    slots = take(9)
    load, store, send, recv, send_k, recv_k, send_v, recv_v = take(8)
    back_sk, back_rk, back_sv, back_rv, send_w, recv_w = take(6)
    send_up, recv_up, send_on, recv_on, send_x, recv_x, free = refs

    section, seq, head = (lax.axis_index(name) for name in (SECTION, SEQ, HEAD))
    seqs = lax.axis_size(SEQ)
    micros, local, width = x.shape
    segment = 2 * local
    mem = out_mem.shape[1]
    half_mem = mem // 2
    total = segment + mem
    share = w_in.shape[2]
    inner = w_up.shape[1]
    heads = share // HEAD_DIM
    dv = w_value.shape[1]
    other = 1 - head
    partner = {HEAD: other}
    own_rows, other_rows = rows_at(head * local, local), rows_at(other * local, local)
    own_mem = rows_at(head * half_mem, half_mem)
    own_mem_rows = rows_at(segment + head * half_mem, half_mem)
    seg_rows, mem_rows = pl.ds(0, segment), pl.ds(segment, mem)
    column_tiles = [(at, width // 3) for at in range(0, width, width // 3)]
    inner_tiles = lane_tiles(inner)

    def copy(slot, source, target, device):
        return pltpu.make_async_remote_copy(
            src_ref=source,
            dst_ref=target,
            send_sem=send.at[slot],
            recv_sem=recv.at[slot],
            device_id=device,
            device_id_type=MESH,
        )

    def weight_copy(name):
        return pltpu.make_async_copy(
            weights_in[name], held[name], load.at[name]
        )

    out_copy = pltpu.make_async_copy(w_out_in, w_out_all.at[head], load.at[len(WEIGHTS)])
    w_out = w_out_all.at[head]

    def each_micro(stage):
        def body(micro, carry):
            stage(micro)
            return carry

        lax.fori_loop(0, micros, body, 0)

    def each_seq(condition, act):
        for t in range(seqs):

            @pl.when(condition(t))
            def _(t=t):
                act(t)

    def later(t):
        return t > seq

    def earlier(t):
        return t < seq

    out_copy.start()
    for name in WEIGHTS:
        weight_copy(name).start()
    keys[...] = jnp.zeros_like(keys)
    values[...] = jnp.zeros_like(values)
    from_k[...] = jnp.zeros_like(from_k)
    from_v[...] = jnp.zeros_like(from_v)
    g_small[...] = jnp.zeros_like(g_small)
    mem_all[own_mem] = mem_tokens[...]
    barrier_with(
        [(seq >= 0, partner)]
        + [(t != seq, {SEQ: t, HEAD: g}) for t in range(seqs) for g in range(2)]
        + [(section == 1, {SECTION: 0, HEAD: g}) for g in range(2)]
        + [(section == 0, {SECTION: 1})],
        1 + 2 * (seqs - 1) + 2 - section,
    )

    tokens = copy(TOKENS, mem_tokens, mem_all.at[own_mem], partner)

    def x_load(micro, target):
        return pltpu.make_async_copy(x.at[micro], target, load.at[len(WEIGHTS) + 1 + micro])

    def x_copy(micro):
        return copy(copy_slot(micro, X_IN), x.at[micro], rows.at[micro, own_rows], partner)

    def y_sent(micro, target_head):
        return pltpu.make_async_remote_copy(
            src_ref=y.at[micro],
            dst_ref=rows.at[micro, own_rows],
            send_sem=send.at[copy_slot(micro, Y_OUT, target_head)],
            recv_sem=recv.at[copy_slot(micro, Y_OUT, head)],
            device_id={SECTION: 1, HEAD: target_head},
            device_id_type=MESH,
        )

    def y_got(micro, source_head):
        here = rows.at[micro, rows_at(source_head * local, local)]
        return copy(copy_slot(micro, Y_OUT, source_head), here, here, partner)

    def tile_copy(kind, micro, index):
        at, tile = column_tiles[index]
        return copy(
            copy_slot(micro, kind, index),
            part.at[micro, :, at : at + tile],
            got_part.at[micro, :, at : at + tile],
            partner,
        )

    def attended_copy(micro, index):
        cut = slice(index * 2 * HEAD_DIM, (index + 1) * 2 * HEAD_DIM)
        return copy(
            copy_slot(micro, PART, index),
            attended.at[micro, :, cut],
            got_attended.at[micro, :, cut],
            partner,
        )

    def local_tile(kind, micro, index):
        at, tile = column_tiles[index]
        return copy(
            copy_slot(micro, kind, index),
            part.at[micro, other_rows, at : at + tile],
            got_out.at[micro, pl.ds(0, local), at : at + tile],
            partner,
        )

    def memory_tile(kind, micro, index):
        at, tile = column_tiles[index]
        return copy(
            copy_slot(micro, kind, index),
            part.at[micro, mem_rows, at : at + tile],
            got_out.at[micro, pl.ds(local, mem), at : at + tile],
            partner,
        )

    def key_copy(micro, source, target):
        return pltpu.make_async_remote_copy(
            src_ref=key_block.at[micro],
            dst_ref=keys.at[micro, rows_at(source * mem, mem)],
            send_sem=send_k.at[micro, target],
            recv_sem=recv_k.at[micro, source],
            device_id={SEQ: target},
            device_id_type=MESH,
        )

    def value_copy(micro, source, source_head, target, target_head):
        return pltpu.make_async_remote_copy(
            src_ref=value_block.at[micro],
            dst_ref=values.at[
                micro, rows_at(source * mem, mem), pl.ds(pl.multiple_of(source_head * dv, 128), dv)
            ],
            send_sem=send_v.at[micro, target, target_head],
            recv_sem=recv_v.at[micro, source, source_head],
            device_id={SEQ: target, HEAD: target_head},
            device_id_type=MESH,
        )

    tokens.start()

    out_share = share // seqs

    def out_piece(half, piece):
        return w_out_all.at[half, rows_at(piece * out_share, out_share)]

    def over_out():
        mine = w_out_in.at[rows_at(seq * out_share, out_share)]
        return copy(OUT_SHARE, mine, out_piece(head, seq), partner)

    def hand_out(source, target):
        return pltpu.make_async_remote_copy(
            src_ref=out_piece(other, source),
            dst_ref=out_piece(other, source),
            send_sem=send_w.at[target],
            recv_sem=recv_w.at[source],
            device_id={SEQ: target},
            device_id_type=MESH,
        )

    over_out().start()

    @pl.when(section == 0)
    def _():
        for micro in range(micros):
            x_copy(micro).start()
            x_load(micro, rows.at[micro, own_rows]).start()

    @pl.when(section == 1)
    def _():
        for micro in range(micros):
            x_load(micro, grad_y.at[micro]).start()

    tokens.wait_recv()
    for micro in range(micros):
        rows[micro, mem_rows] = mem_all[...]
    over_out().wait_recv()
    each_seq(lambda t: t != seq, lambda t: hand_out(seq, t).start())

    causal = lax.broadcasted_iota(jnp.int32, (segment, segment), 0) >= (
        lax.broadcasted_iota(jnp.int32, (segment, segment), 1)
    )
    mem_causal = segment + lax.broadcasted_iota(jnp.int32, (mem, total), 0) >= (
        lax.broadcasted_iota(jnp.int32, (mem, total), 1)
    )
    lane = lax.broadcasted_iota(jnp.int32, (total, 128), 1)

    def lanes_of(kind, place):
        return slice(kind * share + place * HEAD_DIM, kind * share + (place + 1) * HEAD_DIM)

    def attention(micro):
        @pl.when(section == 0)
        def _():
            x_load(micro, rows.at[micro, own_rows]).wait()
            x_copy(micro).wait_recv()

        @pl.when(section == 1)
        def _():
            for source in range(2):
                y_got(micro, source).wait_recv()

        unit, _ = unit_rows(rows[micro])
        normed[micro] = unit * gains[0:1] + biases[0:1]

        @pl.when(micro == 0)
        def _():
            weight_copy(IN).wait()

        for kind in range(3):
            made = nn(normed[micro], w_in[kind])
            if kind != 1:
                made = made + head_bias[kind // 2 : kind // 2 + 1]
            qkv[micro, :, kind * share : (kind + 1) * share] = made
        tops = jnp.zeros((total, 128), jnp.float32)
        for place in range(heads):
            query, key, value = (lanes_of(kind, place) for kind in range(3))
            made_top = []
            for at, allowed, seen in ((seg_rows, causal, seg_rows), (mem_rows, mem_causal, pl.ds(0, total))):
                scores = mm_nt(qkv[micro, at, query], qkv[micro, seen, key]) * SCALE
                scores = jnp.where(allowed, scores, -1e30)
                top = jnp.max(scores, axis=1, keepdims=True)
                exponent = jnp.exp(scores - top)
                row_total = jnp.sum(exponent, axis=1, keepdims=True)
                attended[micro, at, place * HEAD_DIM : (place + 1) * HEAD_DIM] = (
                    nn(exponent, qkv[micro, seen, value]) / row_total
                )
                made_top.append(top + jnp.log(row_total))
            tops = jnp.where(lane == place, jnp.concatenate(made_top, axis=0), tops)
            if place % 2 == 1:
                attended_copy(micro, place // 2).start()
        lse[micro] = tops

    each_micro(attention)
    weight_copy(UP).wait()
    weight_copy(DOWN).wait()
    out_copy.wait()
    each_seq(lambda t: t != seq, lambda t: hand_out(t, t).wait_recv())

    def feed_forward(micro):
        for index in range(heads // 2):
            attended_copy(micro, index).wait()
        for at, tile in column_tiles:
            cut = slice(at, at + tile)
            hidden[micro, :, cut] = (
                rows[micro, :, cut]
                + nn(attended[micro], w_out_all[head, :, cut])
                + nn(got_attended[micro], w_out_all[other, :, cut])
                + residual[0:1, cut]
            )
        unit, _ = unit_rows(hidden[micro])
        normed[micro] = unit * gains[1:2] + biases[1:2]
        for at, tile in inner_tiles:
            cut = slice(at, at + tile)
            made = nn(normed[micro], w_up[:, cut]) + b_up[:, cut]
            pre[micro, :, cut] = made
            d_pre[micro, :, cut] = gelu_parts(made)[0]
        for index, (at, tile) in enumerate(column_tiles):
            part[micro, :, at : at + tile] = nn(d_pre[micro], w_down[:, at : at + tile])
            memory_tile(MEMORY, micro, index).start()
            local_tile(LOCAL, micro, index).start()

    each_micro(feed_forward)
    for name in (KEY, VALUE, QUERY):
        weight_copy(name).wait()

    def memory_write(micro):
        for index, (at, tile) in enumerate(column_tiles):
            cut = slice(at, at + tile)
            memory_tile(MEMORY, micro, index).wait()
            out_mem[micro, :, cut] = (
                part[micro, mem_rows, cut]
                + got_out[micro, local:, cut]
                + hidden[micro, mem_rows, cut]
                + residual[1:2, cut]
            )
        key_block[micro] = nn(out_mem[micro], w_key[...])
        value_block[micro] = nn(out_mem[micro], w_value[...])

        def share_block(t):
            key_copy(micro, seq, t).start()
            for g in range(2):
                value_copy(micro, seq, head, t, g).start()

        each_seq(later, share_block)

    each_micro(memory_write)

    def read_query(micro):
        for index, (at, tile) in enumerate(column_tiles):
            cut = slice(at, at + tile)
            local_tile(LOCAL, micro, index).wait()
            out_local[micro, :, cut] = (
                part[micro, own_rows, cut]
                + got_out[micro, :local, cut]
                + hidden[micro, own_rows, cut]
                + residual[1:2, cut]
            )
        query_proj[micro] = nn(out_local[micro], w_query[...])

    def memory_read(micro):
        read_query(micro)

        def got(t):
            key_copy(micro, t, t).wait_recv()
            for g in range(2):
                value_copy(micro, t, g, t, g).wait_recv()

        query_halves = halves_of(query_proj[micro])
        each_seq(earlier, got)
        key_halves = halves_of(keys[micro])
        scores = jnp.zeros((local, seqs * mem), jnp.float32)
        for by in (1, 2, 3):
            scores = scores + mm_nt(
                query_halves * turned(query_halves, by), key_halves * turned(key_halves, by)
            )
        scores = jnp.where(seen_mask(items, micro, seqs, mem), scores, 0.0)
        weights[micro] = scores
        found = nn(scores, values[micro]) / (jnp.sum(scores, axis=1, keepdims=True) + 1.0)
        read[micro] = found
        y[micro] = out_local[micro] + found

        @pl.when(section == 0)
        def _():
            for target in range(2):
                y_sent(micro, target).start()

    each_micro(memory_read)

    def grad_copy(micro):
        return copy(
            copy_slot(micro, GRAD), grad_x.at[micro], grad_y.at[micro], {SECTION: 0}
        )

    def rows_copy(micro):
        here = d_out.at[micro, own_rows]
        return copy(copy_slot(micro, D_LOCAL), here, here, partner)

    def mem_copy(micro):
        return copy(copy_slot(micro, D_MEMORY), mem_part.at[micro], got_mem.at[micro], partner)

    def back_key(micro, source, target):
        return pltpu.make_async_remote_copy(
            src_ref=d_keys.at[micro, rows_at(target * mem, mem)],
            dst_ref=from_k.at[micro, source],
            send_sem=back_sk.at[micro, target],
            recv_sem=back_rk.at[micro, source],
            device_id={SEQ: target},
            device_id_type=MESH,
        )

    def back_value(micro, source, source_head, target, target_head):
        return pltpu.make_async_remote_copy(
            src_ref=d_values.at[
                micro, rows_at(target * mem, mem), pl.ds(pl.multiple_of(target_head * dv, 128), dv)
            ],
            dst_ref=from_v.at[micro, source, source_head],
            send_sem=back_sv.at[micro, target, target_head],
            recv_sem=back_rv.at[micro, source, source_head],
            device_id={SEQ: target, HEAD: target_head},
            device_id_type=MESH,
        )

    def add_small(row, vector):
        for at in range(0, vector.shape[1], 128):
            g_small[row + at // 128 : row + at // 128 + 1] += vector[:, at : at + 128]

    def read_back(micro):
        @pl.when(section == 0)
        def _():
            grad_copy(micro).wait_recv()

        @pl.when(section == 1)
        def _():
            x_load(micro, grad_y.at[micro]).wait()

        grad = grad_y[micro]
        scores = weights[micro]
        denominator = jnp.sum(scores, axis=1, keepdims=True) + 1.0
        d_numer = grad / denominator
        d_denom = -jnp.sum(grad * read[micro], axis=1, keepdims=True) / denominator
        d_values[micro] = mm_tn(scores, d_numer)

        def send_values(t):
            for g in range(2):
                back_value(micro, seq, head, t, g).start()

        each_seq(earlier, send_values)
        d_scores = jnp.where(
            seen_mask(items, micro, seqs, mem), mm_nt(d_numer, values[micro]) + d_denom, 0.0
        )
        query_halves, key_halves = halves_of(query_proj[micro]), halves_of(keys[micro])
        d_key_halves = jnp.zeros_like(key_halves)
        for by in (1, 2, 3):
            d_feats = mm_tn(d_scores, query_halves * turned(query_halves, by))
            d_key_halves += d_feats * turned(key_halves, by) + turned(d_feats * key_halves, -by)
        d_keys[micro] = halves_back(keys[micro], d_key_halves)
        each_seq(earlier, lambda t: back_key(micro, seq, t).start())
        d_query_halves = jnp.zeros_like(query_halves)
        for by in (1, 2, 3):
            d_feats = nn(d_scores, key_halves * turned(key_halves, by))
            d_query_halves += d_feats * turned(query_halves, by) + turned(d_feats * query_halves, -by)
        query_proj[micro] = halves_back(query_proj[micro], d_query_halves)
        d_out[micro, own_rows] = grad + mm_nt(query_proj[micro], w_query[...])
        rows_copy(micro).start()

    each_micro(read_back)

    def write_back(micro):
        def got(t):
            back_key(micro, t, t).wait_recv()
            for g in range(2):
                back_value(micro, t, g, t, g).wait_recv()

        each_seq(later, got)
        key_block[micro] = jnp.sum(from_k[micro], axis=0)
        value_block[micro] = jnp.sum(from_v[micro], axis=(0, 1))
        mem_part[micro] = mm_nt(key_block[micro], w_key[...]) + mm_nt(
            value_block[micro], w_value[...]
        )
        mem_copy(micro).start()

    def forward_sent(micro):
        def sent(t):
            key_copy(micro, seq, t).wait_send()
            for g in range(2):
                value_copy(micro, seq, head, t, g).wait_send()

        each_seq(later, sent)

    each_micro(forward_sent)
    each_micro(write_back)

    def both(ref):
        return ref[...].reshape(micros * ref.shape[1], ref.shape[2])

    w_query[...] = mm_tn(both(out_local), both(query_proj))
    w_key[...] = mm_tn(both(out_mem), both(key_block))
    w_value[...] = mm_tn(both(out_mem), both(value_block))
    def feed_forward_back(micro):
        mem_copy(micro).wait()
        d_out[micro, mem_rows] = mem_part[micro] + got_mem[micro]
        rows_copy(micro).wait()
        for at, tile in inner_tiles:
            cut = slice(at, at + tile)
            activated, slope = gelu_parts(pre[micro, :, cut])
            made = slope * mm_nt(d_out[micro], w_down[cut])
            pre[micro, :, cut] = activated
            d_pre[micro, :, cut] = made
            add_small(36 + at // 128, column_sum(made))
        for index, (at, tile) in enumerate(column_tiles):
            part[micro, :, at : at + tile] = mm_nt(d_pre[micro], w_up[at : at + tile])
            tile_copy(MIX, micro, index).start()
        add_small(30, 0.5 * column_sum(d_out[micro]))

    each_micro(feed_forward_back)

    def attention_back(micro):
        unit, inverse = unit_rows(hidden[micro])
        for index, (at, tile) in enumerate(column_tiles):
            cut = slice(at, at + tile)
            tile_copy(MIX, micro, index).wait()
            got_part[micro, :, cut] += part[micro, :, cut]
        d_mixed = got_part[micro]
        normed[micro] = unit * gains[1:2] + biases[1:2]
        hidden[micro] = d_out[micro] + unit_rows_back(d_mixed * gains[1:2], unit, inverse)
        add_small(6, 0.5 * column_sum(d_mixed * unit))
        add_small(18, 0.5 * column_sum(d_mixed))
        add_small(24, 0.5 * column_sum(hidden[micro]))
        part[micro, :, :share] = mm_nt(hidden[micro], w_out[...])
        block_rows = lax.div(
            lax.broadcasted_iota(jnp.int32, (mem, share), 1), jnp.int32(HEAD_DIM)
        )
        for place in range(heads):
            query, key, value = (lanes_of(kind, place) for kind in range(3))
            cut = slice(place * HEAD_DIM, (place + 1) * HEAD_DIM)
            wide = pl.ds(place * mem, mem)
            grads = []
            for at, allowed, seen in ((seg_rows, causal, seg_rows), (mem_rows, mem_causal, pl.ds(0, total))):
                scores = mm_nt(qkv[micro, at, query], qkv[micro, seen, key]) * SCALE
                soft = jnp.exp(
                    jnp.where(allowed, scores, -1e30) - lse[micro, at, place : place + 1]
                )
                d_head = part[micro, at, cut]
                inner_dot = jnp.sum(d_head * attended[micro, at, cut], axis=1, keepdims=True)
                d_scores = soft * (mm_nt(d_head, qkv[micro, seen, value]) - inner_dot) * SCALE
                grads.append((soft, d_scores, d_head, nn(d_scores, qkv[micro, seen, key])))
            (soft, d_scores, d_head, d_query), (mem_soft, mem_scores, _, mem_query) = grads
            wide_soft[wide] = mem_soft
            wide_scores[wide] = mem_scores
            mine = block_rows == place
            wide_query[wide] = jnp.where(mine, qkv[micro, mem_rows, :share], 0.0)
            wide_grad[wide] = jnp.where(mine, part[micro, mem_rows, :share], 0.0)
            d_key = mm_tn(d_scores, qkv[micro, seg_rows, query])
            d_value = mm_tn(soft, d_head)
            qkv[micro, seg_rows, query] = d_query
            qkv[micro, mem_rows, query] = mem_query
            qkv[micro, seg_rows, key] = d_key
            qkv[micro, seg_rows, value] = d_value
        qkv[micro, mem_rows, share:] = jnp.zeros((mem, 2 * share), jnp.float32)
        qkv[micro, :, share : 2 * share] += mm_tn(wide_scores[...], wide_query[...])
        qkv[micro, :, 2 * share :] += mm_tn(wide_soft[...], wide_grad[...])
        for index, (at, tile) in enumerate(column_tiles):
            made = mm_nt(qkv[micro, :, :share], w_in[0, at : at + tile])
            for kind in (1, 2):
                made = made + mm_nt(
                    qkv[micro, :, kind * share : (kind + 1) * share], w_in[kind, at : at + tile]
                )
            part[micro, :, at : at + tile] = made
            local_tile(ROWS, micro, index).start()
            memory_tile(ROWS_MEMORY, micro, index).start()
        add_small(48, column_sum(qkv[micro, :, :share]))
        add_small(51, column_sum(qkv[micro, :, 2 * share :]))

    each_micro(attention_back)

    def finish(micro, d_normed, at_rows):
        unit, inverse = unit_rows(rows[micro, at_rows])
        add_small(0, column_sum(d_normed * unit))
        add_small(12, column_sum(d_normed))
        return hidden[micro, at_rows] + unit_rows_back(d_normed * gains[0:1], unit, inverse)

    def rows_back(micro):
        for index in range(len(column_tiles)):
            local_tile(ROWS, micro, index).wait()
            memory_tile(ROWS_MEMORY, micro, index).wait()
        grad_x[micro] = finish(micro, part[micro, own_rows] + got_out[micro, :local], own_rows)

        @pl.when(section == 1)
        def _():
            grad_copy(micro).start()

        mem_half = rows_at(local + head * half_mem, half_mem)
        d_tokens = finish(micro, part[micro, own_mem_rows] + got_out[micro, mem_half], own_mem_rows)
        for at in range(0, width, 128):
            row = 56 + (at // 128) * half_mem
            g_small[row : row + half_mem] += d_tokens[:, at : at + 128]

    along = seqs // lanes
    z, lane_y = seq // lanes, lax.rem(seq, lanes)
    place = lane_y * along + jnp.where(lax.rem(lane_y, 2) == 0, z, along - 1 - z)

    def device(spot):
        row = spot // along
        column = lax.rem(spot, along)
        column = jnp.where(lax.rem(row, 2) == 0, column, along - 1 - column)
        return {SEQ: column * lanes + row}

    targets = (device(lax.rem(place + 1, seqs)), device(lax.rem(place + seqs - 1, seqs)))
    signs = (1, -1)
    kinds = range(w_in.shape[0])
    sources = [w_down, w_value, w_up, w_out, *(w_in.at[kind] for kind in kinds), g_small, got_whole]
    results = [down_sum, value_sum, up_sum, out_sum, *(in_sum.at[kind] for kind in kinds)]
    results += [small_sum, whole_sum.at[head]]
    count = len(sources)
    ways = [(index, way) for index in range(count) for way in range(2)]
    last = seqs - 2

    def block(ref, way, spot):
        size = ref.shape[0] // seqs
        half = size // 2
        spot = lax.rem(spot + 2 * seqs, seqs)
        return ref.at[pl.ds(pl.multiple_of(spot * size + way * half, half), half)]

    def slot_of(index, way, step):
        return slots[index].at[way, lax.rem(step, SLOTS)]

    def up_copy(index, way, step, source):
        turn = lax.rem(step, SLOTS)
        return pltpu.make_async_remote_copy(
            src_ref=source,
            dst_ref=slot_of(index, way, step),
            send_sem=send_up.at[turn, way, index],
            recv_sem=recv_up.at[turn, way, index],
            device_id=targets[way],
            device_id_type=MESH,
        )

    def on_copy(index, way, step, source, target):
        return pltpu.make_async_remote_copy(
            src_ref=source,
            dst_ref=target,
            send_sem=send_on.at[step, way, index],
            recv_sem=recv_on.at[step, way, index],
            device_id=targets[way],
            device_id_type=MESH,
        )

    def over(source, target, number):
        return pltpu.make_async_remote_copy(
            src_ref=source,
            dst_ref=target,
            send_sem=send_x.at[number],
            recv_sem=recv_x.at[number],
            device_id=partner,
            device_id_type=MESH,
        )

    def begin(*indices):
        for index in indices:
            for way in range(2):
                up_copy(index, way, 0, block(sources[index], way, place)).start()

    for at, tile in inner_tiles:
        cut = slice(at, at + tile)
        w_down[cut] = mm_tn(both(pre.at[:, :, cut]), both(d_out))
    begin(0, 1)
    each_micro(rows_back)
    small_copy = over(g_small, got_small, 0)
    small_copy.start()

    def whole_copy(matrix):
        return over((w_query, w_key)[matrix], got_whole, 1)

    for matrix in range(2):

        @pl.when(head == matrix)
        def _(matrix=matrix):
            whole_copy(1 - matrix).start()

    for at, tile in inner_tiles:
        cut = slice(at, at + tile)
        w_up[:, cut] = mm_tn(both(normed), both(d_pre.at[:, :, cut]))
    begin(2)
    w_out_all[head] = mm_tn(both(attended), both(hidden))
    begin(3)
    for micro in range(micros):
        unit, _ = unit_rows(rows[micro])
        normed[micro] = unit * gains[0:1] + biases[0:1]
    for kind in kinds:
        w_in[kind] = mm_tn(both(normed), both(qkv.at[:, :, kind * share : (kind + 1) * share]))
        begin(4 + kind)
    small_copy.wait()
    g_small[0:SHARED_ROWS] += got_small[0:SHARED_ROWS]
    begin(count - 2)
    whole_copy(0).wait()
    for matrix in range(2):

        @pl.when(head == matrix)
        def _(matrix=matrix):
            got_whole[...] += (w_query, w_key)[matrix][...]

    begin(count - 1)

    def sum_up(step, carry):
        @pl.when(step >= SLOTS)
        def _():
            for way in range(2):
                pl.semaphore_wait(free.at[way], 1)

        for index, way in ways:
            got = slot_of(index, way, step - 1)
            up_copy(index, way, step - 1, got).wait_recv()
            got[...] += block(sources[index], way, place - signs[way] * step)[...]
            up_copy(index, way, step, got).start()
        for index, way in ways:
            up_copy(index, way, step - 1, slot_of(index, way, step)).wait_send()

        @pl.when(jnp.logical_and(step >= 2, step + 1 < seqs - 1))
        def _():
            for way in range(2):
                pl.semaphore_signal(
                    free.at[way], inc=1, device_id=targets[1 - way], device_id_type=MESH
                )

        return carry

    lax.fori_loop(1, seqs - 1, sum_up, 0)

    def hand_over(way, spot, step):
        mine = block(whole_sum.at[head], way, spot)
        return over(mine, mine, 2 + way * seqs + step)

    def home(index, way):
        return pltpu.make_async_copy(
            slot_of(index, way, last),
            block(results[index], way, place + signs[way]),
            store.at[way, index],
        )

    for index, way in ways:
        got = slot_of(index, way, last)
        up_copy(index, way, last, got).wait_recv()
        spot = place + signs[way]
        got[...] += block(sources[index], way, spot)[...]
        target = block(results[index], way, spot)
        on_copy(index, way, 0, got, target).start()
        home(index, way).start()
        if index == count - 1:
            over(got, target, 2 + way * seqs).start()

    def pass_on(step, carry):
        for index, way in ways:
            spot = place - signs[way] * (step - 1)
            here = block(results[index], way, spot)
            on_copy(index, way, step - 1, here, here).wait_recv()
            on_copy(index, way, step, here, here).start()
            if index == count - 1:
                hand_over(way, spot, step).start()
        return carry

    lax.fori_loop(1, seqs - 1, pass_on, 0)
    for index, way in ways:
        spot = place - signs[way] * last
        here = block(results[index], way, spot)
        on_copy(index, way, last, here, here).wait_recv()
        if index == count - 1:
            hand_over(way, spot, seqs - 1).start()
        home(index, way).wait()
        up_copy(index, way, last, slot_of(index, way, last)).wait_send()

    def passed(step, carry):
        for index, way in ways:
            own = slot_of(index, way, 0)
            on_copy(index, way, step, own, own).wait_send()
        return carry

    lax.fori_loop(0, seqs - 1, passed, 0)

    def crossed(step, carry):
        for way in range(2):
            theirs = block(whole_sum.at[other], way, place - signs[way] * (step - 1))
            over(theirs, theirs, 2 + way * seqs + step).wait()
        return carry

    lax.fori_loop(0, seqs, crossed, 0)

    tokens.wait_send()
    over_out().wait_send()
    each_seq(lambda t: t != seq, lambda t: hand_out(seq, t).wait_send())

    def all_sent(micro):
        @pl.when(section == 0)
        def _():
            x_copy(micro).wait_send()
            for target in range(2):
                y_sent(micro, target).wait_send()

        @pl.when(section == 1)
        def _():
            grad_copy(micro).wait_send()

        def sent(t):
            back_key(micro, seq, t).wait_send()
            for g in range(2):
                back_value(micro, seq, head, t, g).wait_send()

        each_seq(earlier, sent)

    each_micro(all_sent)


def shapes_of(*shapes):
    return tuple(jax.ShapeDtypeStruct(shape, jnp.float32) for shape in shapes)


def buffers(*shapes):
    return [pltpu.VMEM(shape, jnp.float32) for shape in shapes]


def dma(*shape):
    return pltpu.SemaphoreType.DMA(shape)


def params_of(number):
    return pltpu.CompilerParams(
        collective_id=number, has_side_effects=True, vmem_limit_bytes=62 << 20
    )


def shards_of_two(
    boundary_in,
    short_items,
    norm_gains,
    norm_biases,
    projection_in,
    head_bias,
    projection_out,
    residual_bias,
    up_weight,
    up_bias,
    down_weight,
    memory_tokens,
    query_memory,
    key_memory,
    value_memory,
):
    seqs = lax.axis_size(SEQ)
    x = boundary_in[0]
    micros, local, width = x.shape
    w_in = projection_in[0].transpose(1, 0, 2)
    share = w_in.shape[2]
    inner = up_weight.shape[2]
    half_mem = memory_tokens.shape[1]
    mem = 2 * half_mem
    segment = 2 * local
    total = segment + mem
    dk, dv = key_memory.shape[2], value_memory.shape[2]
    stored = seqs * mem
    records = (
        (total, width),
        (total, 3 * share),
        (total, share),
        (total, 128),
        (total, width),
        (total, inner),
        (local, width),
        (mem, width),
        (stored, dk),
        (stored, 2 * dv),
        (local, dk),
        (local, stored),
        (local, width),
    )
    weights = (
        w_in,
        up_weight[0],
        down_weight[0],
        value_memory[0],
        query_memory[0],
        key_memory[0],
    )
    w_out = projection_out[0]
    few = (norm_gains[0], norm_biases[0], head_bias[0], residual_bias[0], up_bias, memory_tokens[0])
    slots = 2 + micros * COPY_SLOTS
    ring = [w.shape for w in (down_weight[0], value_memory[0], up_weight[0], w_out)]
    ring += [w_in.shape[1:]] * 3 + [(16 * seqs, 128), (width, dk)]
    g_down, g_up, g_in, g_out, g_value, small, whole, y, grad_x = pl.pallas_call(
        functools.partial(layers_kernel, 2),
        out_shape=shapes_of(
            down_weight[0].shape,
            up_weight[0].shape,
            w_in.shape,
            w_out.shape,
            value_memory[0].shape,
            (16 * seqs, 128),
            (2, width, dk),
            (micros, local, width),
            (micros, local, width),
        ),
        in_specs=[SMEM, HBM] + [VMEM] * len(few) + [HBM] * (len(weights) + 1),
        out_specs=(HBM,) * 7 + (VMEM,) * 2,
        scratch_shapes=buffers(
            *(w.shape for w in weights),
            *((micros, *record) for record in records),
            (2, *w_out.shape),
            (micros, total, share),
            (micros, total, width),
            (micros, total, inner),
            (micros, total, width),
            (micros, total, width),
            (micros, total, width),
            (micros, local + mem, width),
            (mem, width),
            (micros, mem, dk),
            (micros, mem, dv),
            (micros, seqs, mem, dk),
            (micros, seqs, 2, mem, dv),
            (micros, mem, width),
            (micros, mem, width),
            (micros, local, width),
            (mem * (share // HEAD_DIM), total),
            (mem * (share // HEAD_DIM), total),
            (mem * (share // HEAD_DIM), share),
            (mem * (share // HEAD_DIM), share),
            (16 * seqs, 128),
            (16 * seqs, 128),
            (width, dk),
            *((2, SLOTS, height // (2 * seqs), columns) for height, columns in ring),
        )
        + [dma(len(weights) + 1 + micros), dma(2, len(ring)), dma(slots), dma(slots)]
        + [dma(micros, seqs), dma(micros, seqs), dma(micros, seqs, 2), dma(micros, seqs, 2)] * 2
        + [dma(seqs), dma(seqs)]
        + [dma(SLOTS, 2, len(ring)), dma(SLOTS, 2, len(ring))]
        + [dma(seqs - 1, 2, len(ring)), dma(seqs - 1, 2, len(ring))]
        + [dma(2 + 2 * seqs), dma(2 + 2 * seqs), pltpu.SemaphoreType.REGULAR((2,))],
        compiler_params=params_of(0),
        name="layers",
    )(short_items, x, *few, *weights, w_out)
    section = lax.axis_index(SECTION)
    vectors = small[:36].reshape(3, 1, 2, width)
    return (
        jnp.where(section == 0, grad_x, y)[None],
        vectors[0],
        vectors[1],
        g_in.transpose(1, 0, 2)[None],
        small[48:54].reshape(1, 2, share),
        g_out[None],
        vectors[2],
        g_up[None],
        small[36:48].reshape(1, inner),
        g_down[None],
        small[56 : 56 + 6 * half_mem]
        .reshape(6, half_mem, 128)
        .transpose(1, 0, 2)
        .reshape(1, half_mem, width),
        whole[0][None],
        whole[1][None],
        g_value[None],
    )


def solution(mesh):
    return jax.shard_map(
        shards_of_two if mesh.shape[HEAD] == 2 else shards,
        mesh=mesh,
        in_specs=(
            P(SECTION, None, (SEQ, HEAD), None),
            P(),
            P(SECTION, None, None),
            P(SECTION, None, None),
            P(SECTION, None, None, HEAD),
            P(SECTION, None, HEAD),
            P(SECTION, HEAD, None),
            P(SECTION, None, None),
            P(SECTION, None, HEAD),
            P(SECTION, HEAD),
            P(SECTION, HEAD, None),
            P(SECTION, HEAD, None),
            P(SECTION, None, None),
            P(SECTION, None, None),
            P(SECTION, None, HEAD),
        ),
        out_specs=(
            P(SECTION, None, (SEQ, HEAD), None),
            P(SECTION, None, None),
            P(SECTION, None, None),
            P(SECTION, None, None, HEAD),
            P(SECTION, None, HEAD),
            P(SECTION, HEAD, None),
            P(SECTION, None, None),
            P(SECTION, None, HEAD),
            P(SECTION, HEAD),
            P(SECTION, HEAD, None),
            P(SECTION, HEAD, None),
            P(SECTION, None, None),
            P(SECTION, None, None),
            P(SECTION, None, HEAD),
        ),
        check_vma=False,
    )
```

time: 1460 us -> 544 us (0.37)
  waiting for transfers between devices: 691 us -> 0 us
  Pallas kernels: 0 us -> 518 us
  matrix products: 251 us -> 0 us
  blocking collectives: 234 us -> 0 us
  local copies, waits for them, and re-layouts: 137 us -> 16.9 us
  other arithmetic: 80.4 us -> 2.15 us
  starting transfers between devices: 37.5 us -> 0 us
  between operations: 20.8 us -> 1.14 us
    pallas_call x0 -> x1, Pallas kernels: none -> 518 us  [shards_of_two(): pl.pallas_call(functools.partial(layers_kernel, 2), out_shape=shapes_of(d...]
    psum x2 -> x0, waiting for transfers between devices: 443 us -> none  [the longest x1 311 us: shards(): lax.psum(sharded, 'seq')]
    dot_general x99 -> x0, matrix products: 251 us -> none  [the longest x81 215 us: mm(): lax.dot_general(left, right, (dims, ((), ())), precision=lax.Precision.HI...]
    reduce_scatter x6 -> x0, waiting for transfers between devices: 148 us -> none  [the longest x3 142 us: layer_backward(): lax.psum_scatter(jnp.concatenate([d_keys, d_values], axis=1), 'seq', scat...]
    all_gather x7 -> x0, blocking collectives: 119 us -> none  [the longest x3 93.9 us: layer_forward(): lax.all_gather(jnp.concatenate([key_proj, values], axis=1), 'seq', axis=0...]
    psum x2 -> x0, blocking collectives: 115 us -> none  [the longest x1 77 us: shards(): lax.psum(shared, ('seq', 'head'))]
    ppermute x31 -> x0, waiting for transfers between devices: 99.7 us -> none  [the longest x27 96.3 us: swap(): return lax.ppermute(value, 'head', [(0, 1), (1, 0)])]
    slice x103 -> x2, local copies, waits for them, and re-layouts: 66.3 us -> 3.48 us  [the longest x1 3.48 us: shards_of_two(): whole[1][None]]
  transfers between devices with their start and end apart: 39 -> 0, of which waited for: 27 -> 0; matrix products, arithmetic and copies ran while one was open for 16% -> 0% of each run, Pallas kernels for 0% -> 0%
where the time goes in v4:
time: 544 us; the launch traced here: 539 us
  Pallas kernels  518 us (95%)
  local copies, waits for them, and re-layouts  16.9 us (3%)
    pallas_call x1, Pallas kernels, shards_of_two(): pl.pallas_call(functools.partial(layers_kernel, 2), out_shape=shapes_of(d...  518 us

profile of v4, /device:TPU:0, one launch (start us, length us, event | category | flops | bytes accessed | tf_op | source)
XLA Modules:
  0.0 538.6 jit_solution(4665227281549702662)
XLA Ops:
  0.7 518.3 %layers.1 = (f32[1536,768]{1,0:T(8,128)}, f32[768,1536]{1,0:T(8,128)}, f32[3,768,384]{2,1,0:T(8,128)}, f32[384,768]{1,0:T(8,128)}, f32[768,384]{1,0:T(8,128)}, /...) custom-call(s32[1,3]{1,0:T(1,128)} %refs_0_.1, ...), custom_call_target="tpu_custom_call" | custom-call | tf_op jit(solution)/shard_map/layers/pallas_call | solution.py:1349
  519.0 0.0 copy-start.3
  519.0 2.1 select_bitcast_fusion
  521.1 0.0 copy-done.3
  521.2 0.6 reshape.47
  521.7 0.6 slice_bitcast_fusion
  522.4 0.6 copy.31
  523.0 0.6 squeeze.63
  523.6 0.6 squeeze.62
  524.2 0.0 copy-start
  524.2 0.6 squeeze.61
  524.8 0.0 slice-start.2
  524.8 3.5 fusion
  528.2 0.0 copy-done
  528.2 0.0 copy-start.2
  528.3 0.0 slice-start.3
  528.3 1.8 copy.37
  530.1 0.3 copy-done.2
  530.4 0.0 slice-start
  530.4 1.0 copy.38
  531.4 0.0 slice-done.2
  531.4 0.0 slice-done.3
  531.4 0.0 slice-start.1
  531.4 2.4 copy.39
  533.8 0.8 slice-done
  534.6 0.3 slice-done.1
  534.9 0.0 copy-start.1
  534.9 2.2 copy.40
  537.1 0.0 copy-done.1
  537.1 1.0 copy.41
  (4 shorter events, 0.0 us)
Async XLA Ops:
  519.0 2.2 copy-start.3
  524.2 4.1 copy-start
  524.8 6.6 %slice-start.2 = ((s8[4718592]{0:T(1024)(128)(4,1)}), s8[4194304]{0:T(1024)(128)(4,1)S(1)}, s32[]{:S(2)}) async-start(s8[4718592]{0:T(1024)(128)(4,1)} %bitcast.41), calls=%async_computation.2 | async-start | bytes 8388608
  528.2 2.1 copy-start.2
  528.3 3.1 slice-start.3
  530.4 4.3 slice-start
  531.4 3.5 slice-start.1
  534.9 2.2 copy-start.1

commit v5 on v4

--- a/solution.py
+++ b/solution.py
@@ -474,6 +474,7 @@
 
 
 SLOTS = 3
+AHEAD = 4
 
 
 def layers_kernel(lanes, *refs):
@@ -502,7 +503,7 @@
     slots = take(9)
     load, store, send, recv, send_k, recv_k, send_v, recv_v = take(8)
     back_sk, back_rk, back_sv, back_rv, send_w, recv_w = take(6)
-    send_up, recv_up, send_on, recv_on, send_x, recv_x, free = refs
+    send_up, recv_up, send_on, recv_on, send_x, recv_x, free, go = refs
 
     section, seq, head = (lax.axis_index(name) for name in (SECTION, SEQ, HEAD))
     seqs = lax.axis_size(SEQ)
@@ -680,12 +681,14 @@
             device_id_type=MESH,
         )
 
-    over_out().start()
-
     @pl.when(section == 0)
     def _():
+        over_out().start()
+
+    @pl.when(section == 0)
+    def _():
+        x_copy(0).start()
         for micro in range(micros):
-            x_copy(micro).start()
             x_load(micro, rows.at[micro, own_rows]).start()
 
     @pl.when(section == 1)
@@ -696,6 +699,11 @@
     tokens.wait_recv()
     for micro in range(micros):
         rows[micro, mem_rows] = mem_all[...]
+    @pl.when(section == 1)
+    def _():
+        pl.semaphore_wait(go, 1)
+        over_out().start()
+
     over_out().wait_recv()
     each_seq(lambda t: t != seq, lambda t: hand_out(seq, t).start())
 
@@ -715,6 +723,10 @@
         def _():
             x_load(micro, rows.at[micro, own_rows]).wait()
             x_copy(micro).wait_recv()
+
+            @pl.when(micro + 1 < micros)
+            def _():
+                x_copy(micro + 1).start()
 
         @pl.when(section == 1)
         def _():
@@ -758,6 +770,11 @@
     out_copy.wait()
     each_seq(lambda t: t != seq, lambda t: hand_out(t, t).wait_recv())
 
+    @pl.when(section == 0)
+    def _():
+        pl.semaphore_signal(go, inc=1, device_id={SECTION: 1}, device_id_type=MESH)
+
+
     def feed_forward(micro):
         for index in range(heads // 2):
             attended_copy(micro, index).wait()
@@ -975,6 +992,152 @@
         add_small(30, 0.5 * column_sum(d_out[micro]))
 
     each_micro(feed_forward_back)
+    along = seqs // lanes
+    z, lane_y = seq // lanes, lax.rem(seq, lanes)
+    place = lane_y * along + jnp.where(lax.rem(lane_y, 2) == 0, z, along - 1 - z)
+
+    def device(spot):
+        row = spot // along
+        column = lax.rem(spot, along)
+        column = jnp.where(lax.rem(row, 2) == 0, column, along - 1 - column)
+        return {SEQ: column * lanes + row}
+
+    targets = (device(lax.rem(place + 1, seqs)), device(lax.rem(place + seqs - 1, seqs)))
+    signs = (1, -1)
+    kinds = range(w_in.shape[0])
+    sources = [w_down, w_up, w_value, w_out, *(w_in.at[kind] for kind in kinds), g_small, got_whole]
+    results = [down_sum, up_sum, value_sum, out_sum, *(in_sum.at[kind] for kind in kinds)]
+    results += [small_sum, whole_sum.at[head]]
+    count = len(sources)
+    ways = [[(index, way) for index in group for way in range(2)] for group in (range(2), range(2, count))]
+    last = seqs - 2
+
+    def block(ref, way, spot):
+        size = ref.shape[0] // seqs
+        half = size // 2
+        spot = lax.rem(spot + 2 * seqs, seqs)
+        return ref.at[pl.ds(pl.multiple_of(spot * size + way * half, half), half)]
+
+    def slot_of(index, way, step):
+        return slots[index].at[way, lax.rem(step, SLOTS)]
+
+    def up_copy(index, way, step, source):
+        turn = lax.rem(step, SLOTS)
+        return pltpu.make_async_remote_copy(
+            src_ref=source,
+            dst_ref=slot_of(index, way, step),
+            send_sem=send_up.at[turn, way, index],
+            recv_sem=recv_up.at[turn, way, index],
+            device_id=targets[way],
+            device_id_type=MESH,
+        )
+
+    def on_copy(index, way, step, source, target):
+        return pltpu.make_async_remote_copy(
+            src_ref=source,
+            dst_ref=target,
+            send_sem=send_on.at[step, way, index],
+            recv_sem=recv_on.at[step, way, index],
+            device_id=targets[way],
+            device_id_type=MESH,
+        )
+
+    def over(source, target, number):
+        return pltpu.make_async_remote_copy(
+            src_ref=source,
+            dst_ref=target,
+            send_sem=send_x.at[number],
+            recv_sem=recv_x.at[number],
+            device_id=partner,
+            device_id_type=MESH,
+        )
+
+    def hand_over(way, spot, step):
+        mine = block(whole_sum.at[head], way, spot)
+        return over(mine, mine, 2 + way * seqs + step)
+
+    def home(index, way):
+        return pltpu.make_async_copy(
+            slot_of(index, way, last),
+            block(results[index], way, place + signs[way]),
+            store.at[way, index],
+        )
+
+    def sum_up(group, step):
+        @pl.when(step >= SLOTS)
+        def _():
+            for way in range(2):
+                pl.semaphore_wait(free.at[group, way], 1)
+
+        for index, way in ways[group]:
+            got = slot_of(index, way, step - 1)
+            up_copy(index, way, step - 1, got).wait_recv()
+            got[...] += block(sources[index], way, place - signs[way] * step)[...]
+            up_copy(index, way, step, got).start()
+        for index, way in ways[group]:
+            up_copy(index, way, step - 1, slot_of(index, way, step)).wait_send()
+
+        @pl.when(jnp.logical_and(step >= 2, step + 1 < seqs - 1))
+        def _():
+            for way in range(2):
+                pl.semaphore_signal(
+                    free.at[group, way], inc=1, device_id=targets[1 - way], device_id_type=MESH
+                )
+
+    def turn_round(group):
+        for index, way in ways[group]:
+            got = slot_of(index, way, last)
+            up_copy(index, way, last, got).wait_recv()
+            spot = place + signs[way]
+            got[...] += block(sources[index], way, spot)[...]
+            target = block(results[index], way, spot)
+            on_copy(index, way, 0, got, target).start()
+            home(index, way).start()
+            if index == count - 1:
+                over(got, target, 2 + way * seqs).start()
+
+    def pass_on(group, step):
+        for index, way in ways[group]:
+            spot = place - signs[way] * (step - 1)
+            here = block(results[index], way, spot)
+            on_copy(index, way, step - 1, here, here).wait_recv()
+
+            @pl.when(step < seqs - 1)
+            def _(index=index, way=way, here=here):
+                on_copy(index, way, step, here, here).start()
+
+            if index == count - 1:
+                hand_over(way, spot, step).start()
+
+    def advance(group, step):
+        @pl.when(step < seqs - 1)
+        def _():
+            sum_up(group, step)
+
+        @pl.when(step == seqs - 1)
+        def _():
+            turn_round(group)
+
+        @pl.when(jnp.logical_and(step >= seqs, step < 2 * seqs - 1))
+        def _():
+            pass_on(group, step - seqs + 1)
+
+    def begin(*indices):
+        for index in indices:
+            for way in range(2):
+                up_copy(index, way, 0, block(sources[index], way, place)).start()
+
+    for micro in range(micros):
+        unit, _ = unit_rows(hidden[micro])
+        normed[micro] = unit * gains[1:2] + biases[1:2]
+    for at, tile in inner_tiles:
+        cut = slice(at, at + tile)
+        w_down[cut] = mm_tn(both(pre.at[:, :, cut]), both(d_out))
+    begin(0)
+    for at, tile in inner_tiles:
+        cut = slice(at, at + tile)
+        w_up[:, cut] = mm_tn(both(normed), both(d_pre.at[:, :, cut]))
+    begin(1, 2)
 
     def attention_back(micro):
         unit, inverse = unit_rows(hidden[micro])
@@ -983,7 +1146,6 @@
             tile_copy(MIX, micro, index).wait()
             got_part[micro, :, cut] += part[micro, :, cut]
         d_mixed = got_part[micro]
-        normed[micro] = unit * gains[1:2] + biases[1:2]
         hidden[micro] = d_out[micro] + unit_rows_back(d_mixed * gains[1:2], unit, inverse)
         add_small(6, 0.5 * column_sum(d_mixed * unit))
         add_small(18, 0.5 * column_sum(d_mixed))
@@ -1033,7 +1195,11 @@
         add_small(48, column_sum(qkv[micro, :, :share]))
         add_small(51, column_sum(qkv[micro, :, 2 * share :]))
 
-    each_micro(attention_back)
+    def attention_back_and_ring(micro):
+        attention_back(micro)
+        sum_up(0, micro + 1)
+
+    each_micro(attention_back_and_ring)
 
     def finish(micro, d_normed, at_rows):
         unit, inverse = unit_rows(rows[micro, at_rows])
@@ -1057,75 +1223,6 @@
             row = 56 + (at // 128) * half_mem
             g_small[row : row + half_mem] += d_tokens[:, at : at + 128]
 
-    along = seqs // lanes
-    z, lane_y = seq // lanes, lax.rem(seq, lanes)
-    place = lane_y * along + jnp.where(lax.rem(lane_y, 2) == 0, z, along - 1 - z)
-
-    def device(spot):
-        row = spot // along
-        column = lax.rem(spot, along)
-        column = jnp.where(lax.rem(row, 2) == 0, column, along - 1 - column)
-        return {SEQ: column * lanes + row}
-
-    targets = (device(lax.rem(place + 1, seqs)), device(lax.rem(place + seqs - 1, seqs)))
-    signs = (1, -1)
-    kinds = range(w_in.shape[0])
-    sources = [w_down, w_value, w_up, w_out, *(w_in.at[kind] for kind in kinds), g_small, got_whole]
-    results = [down_sum, value_sum, up_sum, out_sum, *(in_sum.at[kind] for kind in kinds)]
-    results += [small_sum, whole_sum.at[head]]
-    count = len(sources)
-    ways = [(index, way) for index in range(count) for way in range(2)]
-    last = seqs - 2
-
-    def block(ref, way, spot):
-        size = ref.shape[0] // seqs
-        half = size // 2
-        spot = lax.rem(spot + 2 * seqs, seqs)
-        return ref.at[pl.ds(pl.multiple_of(spot * size + way * half, half), half)]
-
-    def slot_of(index, way, step):
-        return slots[index].at[way, lax.rem(step, SLOTS)]
-
-    def up_copy(index, way, step, source):
-        turn = lax.rem(step, SLOTS)
-        return pltpu.make_async_remote_copy(
-            src_ref=source,
-            dst_ref=slot_of(index, way, step),
-            send_sem=send_up.at[turn, way, index],
-            recv_sem=recv_up.at[turn, way, index],
-            device_id=targets[way],
-            device_id_type=MESH,
-        )
-
-    def on_copy(index, way, step, source, target):
-        return pltpu.make_async_remote_copy(
-            src_ref=source,
-            dst_ref=target,
-            send_sem=send_on.at[step, way, index],
-            recv_sem=recv_on.at[step, way, index],
-            device_id=targets[way],
-            device_id_type=MESH,
-        )
-
-    def over(source, target, number):
-        return pltpu.make_async_remote_copy(
-            src_ref=source,
-            dst_ref=target,
-            send_sem=send_x.at[number],
-            recv_sem=recv_x.at[number],
-            device_id=partner,
-            device_id_type=MESH,
-        )
-
-    def begin(*indices):
-        for index in indices:
-            for way in range(2):
-                up_copy(index, way, 0, block(sources[index], way, place)).start()
-
-    for at, tile in inner_tiles:
-        cut = slice(at, at + tile)
-        w_down[cut] = mm_tn(both(pre.at[:, :, cut]), both(d_out))
-    begin(0, 1)
     each_micro(rows_back)
     small_copy = over(g_small, got_small, 0)
     small_copy.start()
@@ -1139,18 +1236,17 @@
         def _(matrix=matrix):
             whole_copy(1 - matrix).start()
 
-    for at, tile in inner_tiles:
-        cut = slice(at, at + tile)
-        w_up[:, cut] = mm_tn(both(normed), both(d_pre.at[:, :, cut]))
-    begin(2)
     w_out_all[head] = mm_tn(both(attended), both(hidden))
     begin(3)
+    sum_up(0, jnp.int32(3))
     for micro in range(micros):
         unit, _ = unit_rows(rows[micro])
         normed[micro] = unit * gains[0:1] + biases[0:1]
     for kind in kinds:
         w_in[kind] = mm_tn(both(normed), both(qkv.at[:, :, kind * share : (kind + 1) * share]))
         begin(4 + kind)
+        if kind == 1:
+            sum_up(0, jnp.int32(4))
     small_copy.wait()
     g_small[0:SHARED_ROWS] += got_small[0:SHARED_ROWS]
     begin(count - 2)
@@ -1163,75 +1259,18 @@
 
     begin(count - 1)
 
-    def sum_up(step, carry):
-        @pl.when(step >= SLOTS)
-        def _():
-            for way in range(2):
-                pl.semaphore_wait(free.at[way], 1)
-
-        for index, way in ways:
-            got = slot_of(index, way, step - 1)
-            up_copy(index, way, step - 1, got).wait_recv()
-            got[...] += block(sources[index], way, place - signs[way] * step)[...]
-            up_copy(index, way, step, got).start()
-        for index, way in ways:
-            up_copy(index, way, step - 1, slot_of(index, way, step)).wait_send()
-
-        @pl.when(jnp.logical_and(step >= 2, step + 1 < seqs - 1))
-        def _():
-            for way in range(2):
-                pl.semaphore_signal(
-                    free.at[way], inc=1, device_id=targets[1 - way], device_id_type=MESH
-                )
-
+    def ring_turn(turn, carry):
+        advance(0, turn + AHEAD)
+        advance(1, turn)
         return carry
 
-    lax.fori_loop(1, seqs - 1, sum_up, 0)
-
-    def hand_over(way, spot, step):
-        mine = block(whole_sum.at[head], way, spot)
-        return over(mine, mine, 2 + way * seqs + step)
-
-    def home(index, way):
-        return pltpu.make_async_copy(
-            slot_of(index, way, last),
-            block(results[index], way, place + signs[way]),
-            store.at[way, index],
-        )
-
-    for index, way in ways:
-        got = slot_of(index, way, last)
-        up_copy(index, way, last, got).wait_recv()
-        spot = place + signs[way]
-        got[...] += block(sources[index], way, spot)[...]
-        target = block(results[index], way, spot)
-        on_copy(index, way, 0, got, target).start()
-        home(index, way).start()
-        if index == count - 1:
-            over(got, target, 2 + way * seqs).start()
-
-    def pass_on(step, carry):
-        for index, way in ways:
-            spot = place - signs[way] * (step - 1)
-            here = block(results[index], way, spot)
-            on_copy(index, way, step - 1, here, here).wait_recv()
-            on_copy(index, way, step, here, here).start()
-            if index == count - 1:
-                hand_over(way, spot, step).start()
-        return carry
-
-    lax.fori_loop(1, seqs - 1, pass_on, 0)
-    for index, way in ways:
-        spot = place - signs[way] * last
-        here = block(results[index], way, spot)
-        on_copy(index, way, last, here, here).wait_recv()
-        if index == count - 1:
-            hand_over(way, spot, seqs - 1).start()
+    lax.fori_loop(1, 2 * seqs - 1, ring_turn, 0)
+    for index, way in ways[0] + ways[1]:
         home(index, way).wait()
         up_copy(index, way, last, slot_of(index, way, last)).wait_send()
 
     def passed(step, carry):
-        for index, way in ways:
+        for index, way in ways[0] + ways[1]:
             own = slot_of(index, way, 0)
             on_copy(index, way, step, own, own).wait_send()
         return carry
@@ -1344,7 +1383,7 @@
     w_out = projection_out[0]
     few = (norm_gains[0], norm_biases[0], head_bias[0], residual_bias[0], up_bias, memory_tokens[0])
     slots = 2 + micros * COPY_SLOTS
-    ring = [w.shape for w in (down_weight[0], value_memory[0], up_weight[0], w_out)]
+    ring = [w.shape for w in (down_weight[0], up_weight[0], value_memory[0], w_out)]
     ring += [w_in.shape[1:]] * 3 + [(16 * seqs, 128), (width, dk)]
     g_down, g_up, g_in, g_out, g_value, small, whole, y, grad_x = pl.pallas_call(
         functools.partial(layers_kernel, 2),
@@ -1394,31 +1433,106 @@
         + [dma(seqs), dma(seqs)]
         + [dma(SLOTS, 2, len(ring)), dma(SLOTS, 2, len(ring))]
         + [dma(seqs - 1, 2, len(ring)), dma(seqs - 1, 2, len(ring))]
-        + [dma(2 + 2 * seqs), dma(2 + 2 * seqs), pltpu.SemaphoreType.REGULAR((2,))],
+        + [dma(2 + 2 * seqs), dma(2 + 2 * seqs), pltpu.SemaphoreType.REGULAR((2, 2)), pltpu.SemaphoreType.REGULAR],
         compiler_params=params_of(0),
         name="layers",
     )(short_items, x, *few, *weights, w_out)
+    outs = (
+        (1, *x.shape),
+        norm_gains.shape,
+        norm_biases.shape,
+        (1, *w_in.shape),
+        head_bias.shape,
+        projection_out.shape,
+        residual_bias.shape,
+        up_weight.shape,
+        up_bias.shape,
+        down_weight.shape,
+        memory_tokens.shape,
+        query_memory.shape,
+        key_memory.shape,
+        value_memory.shape,
+    )
+    outs = pl.pallas_call(
+        finish_kernel,
+        out_shape=shapes_of(*outs),
+        in_specs=[HBM] * 5 + [VMEM] + [HBM] * 3,
+        out_specs=(HBM, VMEM, VMEM, HBM, VMEM, HBM, VMEM, HBM, VMEM, HBM, VMEM, HBM, HBM, HBM),
+        scratch_shapes=buffers(
+            g_down.shape,
+            g_up.shape,
+            g_in.shape,
+            g_out.shape,
+            g_value.shape,
+            whole.shape[1:],
+            whole.shape[1:],
+            y.shape,
+        )
+        + [dma(8), dma(8)],
+        compiler_params=pltpu.CompilerParams(vmem_limit_bytes=62 << 20),
+        name="finish",
+    )(g_down, g_up, g_in, g_out, g_value, small, whole, y, grad_x)
+    return (*outs[:3], outs[3].transpose(0, 2, 1, 3), *outs[4:])
+
+
+def finish_kernel(
+    g_down, g_up, g_in, g_out, g_value, small, whole, y, grad_x,
+    rows, gains, biases, proj_in, head_bias, proj_out, residual, up, up_bias, down, tokens, query, key,
+    value, *refs
+):
+    *held, loaded, stored = refs
+    pairs = (
+        (g_down, down.at[0]),
+        (g_up, up.at[0]),
+        (g_in, proj_in.at[0]),
+        (g_out, proj_out.at[0]),
+        (g_value, value.at[0]),
+        (whole.at[0], query.at[0]),
+        (whole.at[1], key.at[0]),
+        (y, rows.at[0]),
+    )
     section = lax.axis_index(SECTION)
-    vectors = small[:36].reshape(3, 1, 2, width)
-    return (
-        jnp.where(section == 0, grad_x, y)[None],
-        vectors[0],
-        vectors[1],
-        g_in.transpose(1, 0, 2)[None],
-        small[48:54].reshape(1, 2, share),
-        g_out[None],
-        vectors[2],
-        g_up[None],
-        small[36:48].reshape(1, inner),
-        g_down[None],
-        small[56 : 56 + 6 * half_mem]
-        .reshape(6, half_mem, 128)
-        .transpose(1, 0, 2)
-        .reshape(1, half_mem, width),
-        whole[0][None],
-        whole[1][None],
-        g_value[None],
-    )
+
+    def fetch(index, source):
+        return pltpu.make_async_copy(source, held[index], loaded.at[index])
+
+    def put(index):
+        return pltpu.make_async_copy(held[index], pairs[index][1], stored.at[index])
+
+    last = len(pairs) - 1
+    for index in range(last):
+        fetch(index, pairs[index][0]).start()
+
+    @pl.when(section == 0)
+    def _():
+        fetch(last, grad_x).start()
+
+    @pl.when(section != 0)
+    def _():
+        fetch(last, y).start()
+
+    def spread(target, row, first):
+        for at in range(0, target.shape[-1], 128):
+            target[0, row : row + 1, at : at + 128] = small[first + at // 128 : first + at // 128 + 1]
+
+    lanes = gains.shape[2] // 128
+    for index, target in enumerate((gains, biases, residual)):
+        for row in range(2):
+            spread(target, row, (2 * index + row) * lanes)
+    for at in range(0, up_bias.shape[1], 128):
+        first = 6 * lanes + at // 128
+        up_bias[:, at : at + 128] = small[first : first + 1]
+    for row in range(2):
+        spread(head_bias, row, 8 * lanes + row * (head_bias.shape[2] // 128))
+    count = tokens.shape[1]
+    for at in range(0, tokens.shape[2], 128):
+        first = 56 + (at // 128) * count
+        tokens[0, :, at : at + 128] = small[first : first + count]
+    for index, (source, _) in enumerate(pairs):
+        fetch(index, source).wait()
+        put(index).start()
+    for index in range(len(pairs)):
+        put(index).wait()
 
 
 def solution(mesh):

time: 544 us -> 517 us (0.950)
  local copies, waits for them, and re-layouts: 16.9 us -> 0 us
  Pallas kernels: 518 us -> 511 us
    pallas_call x1, Pallas kernels: 518 us -> 497 us  [shards_of_two(): pl.pallas_call(functools.partial(layers_kernel, 2), out_shape=shapes_of(d...]
    pallas_call x0 -> x1, Pallas kernels: none -> 13.6 us  [shards_of_two(): pl.pallas_call(finish_kernel, out_shape=shapes_of(*outs), in_specs=[HBM]...]
    unnamed x23 -> x0, local copies, waits for them, and re-layouts: 10.5 us -> none
where the time goes in v5:
time: 517 us; the launch traced here: 512 us
  Pallas kernels  511 us (99%)
    pallas_call x1, Pallas kernels, shards_of_two(): pl.pallas_call(functools.partial(layers_kernel, 2), out_shape=shapes_of(d...  497 us
    pallas_call x1, Pallas kernels, shards_of_two(): pl.pallas_call(finish_kernel, out_shape=shapes_of(*outs), in_specs=[HBM]...  13.6 us

profile of v5, /device:TPU:0, one launch (start us, length us, event | category | flops | bytes accessed | tf_op | source)
XLA Modules:
  0.0 511.7 jit_solution(10119527661571302739)
XLA Ops:
  0.7 497.0 %layers.1 = (f32[1536,768]{1,0:T(8,128)}, f32[768,1536]{1,0:T(8,128)}, f32[3,768,384]{2,1,0:T(8,128)}, f32[384,768]{1,0:T(8,128)}, f32[768,384]{1,0:T(8,128)}, /...) custom-call(s32[1,3]{1,0:T(1,128)} %refs_0_.1, ...), custom_call_target="tpu_custom_call" | custom-call | tf_op jit(solution)/shard_map/layers/pallas_call | solution.py:1388
  497.7 13.6 %finish.1 = (f32[1,2,128,768]{3,2,1,0:T(8,128)}, f32[1,2,768]{2,1,0:T(2,128)}, f32[1,2,768]{2,1,0:T(2,128)}, f32[1,3,768,384]{3,2,1,0:T(8,128)}, f32[1,2,384]{2,...) custom-call(f32[1536,768]{1,0:T(8,128)} %get-tuple-element.37.g_down, ...), custom_call_target="tpu_custom_call" | custom-call | tf_op jit(solution)/shard_map/finish/pallas_call | solution.py:1456

commit v6 on v5

--- a/solution.py
+++ b/solution.py
@@ -474,7 +474,7 @@
 
 
 SLOTS = 3
-AHEAD = 4
+AHEAD = 7
 
 
 def layers_kernel(lanes, *refs):
@@ -1180,6 +1180,8 @@
             qkv[micro, mem_rows, query] = mem_query
             qkv[micro, seg_rows, key] = d_key
             qkv[micro, seg_rows, value] = d_value
+            if place == heads // 2:
+                sum_up(0, 2 * micro + 1)
         qkv[micro, mem_rows, share:] = jnp.zeros((mem, 2 * share), jnp.float32)
         qkv[micro, :, share : 2 * share] += mm_tn(wide_scores[...], wide_query[...])
         qkv[micro, :, 2 * share :] += mm_tn(wide_soft[...], wide_grad[...])
@@ -1197,7 +1199,7 @@
 
     def attention_back_and_ring(micro):
         attention_back(micro)
-        sum_up(0, micro + 1)
+        sum_up(0, 2 * micro + 2)
 
     each_micro(attention_back_and_ring)
 
@@ -1236,9 +1238,10 @@
         def _(matrix=matrix):
             whole_copy(1 - matrix).start()
 
+    sum_up(0, jnp.int32(5))
     w_out_all[head] = mm_tn(both(attended), both(hidden))
     begin(3)
-    sum_up(0, jnp.int32(3))
+    sum_up(0, jnp.int32(6))
     for micro in range(micros):
         unit, _ = unit_rows(rows[micro])
         normed[micro] = unit * gains[0:1] + biases[0:1]
@@ -1246,7 +1249,7 @@
         w_in[kind] = mm_tn(both(normed), both(qkv.at[:, :, kind * share : (kind + 1) * share]))
         begin(4 + kind)
         if kind == 1:
-            sum_up(0, jnp.int32(4))
+            turn_round(0)
     small_copy.wait()
     g_small[0:SHARED_ROWS] += got_small[0:SHARED_ROWS]
     begin(count - 2)
@@ -1324,7 +1327,7 @@
 
 def params_of(number):
     return pltpu.CompilerParams(
-        collective_id=number, has_side_effects=True, vmem_limit_bytes=62 << 20
+        collective_id=number, has_side_effects=True, vmem_limit_bytes=63 << 20
     )
 
 

time: 517 us -> 508 us (0.983)
  Pallas kernels: 511 us -> 502 us
    pallas_call x1, Pallas kernels: 497 us -> 488 us  [shards_of_two(): pl.pallas_call(functools.partial(layers_kernel, 2), out_shape=shapes_of(d...]
where the time goes in v6:
time: 508 us; the launch traced here: 503 us
  Pallas kernels  502 us (99%)
    pallas_call x1, Pallas kernels, shards_of_two(): pl.pallas_call(functools.partial(layers_kernel, 2), out_shape=shapes_of(d...  488 us
    pallas_call x1, Pallas kernels, shards_of_two(): pl.pallas_call(finish_kernel, out_shape=shapes_of(*outs), in_specs=[HBM]...  13.6 us

profile of v6, /device:TPU:0, one launch (start us, length us, event | category | flops | bytes accessed | tf_op | source)
XLA Modules:
  0.0 502.8 jit_solution(13942885751177107990)
XLA Ops:
  0.7 488.1 %layers.1 = (f32[1536,768]{1,0:T(8,128)}, f32[768,1536]{1,0:T(8,128)}, f32[3,768,384]{2,1,0:T(8,128)}, f32[384,768]{1,0:T(8,128)}, f32[768,384]{1,0:T(8,128)}, /...) custom-call(s32[1,3]{1,0:T(1,128)} %refs_0_.1, ...), custom_call_target="tpu_custom_call" | custom-call | tf_op jit(solution)/shard_map/layers/pallas_call | solution.py:1391
  488.8 13.6 %finish.1 = (f32[1,2,128,768]{3,2,1,0:T(8,128)}, f32[1,2,768]{2,1,0:T(2,128)}, f32[1,2,768]{2,1,0:T(2,128)}, f32[1,3,768,384]{3,2,1,0:T(8,128)}, f32[1,2,384]{2,...) custom-call(f32[1536,768]{1,0:T(8,128)} %get-tuple-element.37.g_down, ...), custom_call_target="tpu_custom_call" | custom-call | tf_op jit(solution)/shard_map/finish/pallas_call | solution.py:1459

commit v7 on v5

--- a/solution.py
+++ b/solution.py
@@ -474,7 +474,7 @@
 
 
 SLOTS = 3
-AHEAD = 4
+AHEAD = (3, 9)
 
 
 def layers_kernel(lanes, *refs):
@@ -487,7 +487,7 @@
     items, x, gains, biases, head_bias, residual, b_up, mem_tokens = take(8)
     weights_in = take(len(WEIGHTS))
     (w_out_in,) = take(1)
-    down_sum, up_sum, in_sum, out_sum, value_sum, small_sum, whole_sum = take(7)
+    down_sum, up_sum, in_sum, out_sum, value_sum, key_sum, small_sum, half_sum = take(8)
     y, grad_x = take(2)
     held = take(len(WEIGHTS))
     w_in, w_up, w_down, w_value, w_query, w_key = held
@@ -497,13 +497,11 @@
     (
         normed, d_pre, d_out, part, got_part, got_out, mem_all, key_block, value_block, from_k, from_v,
         mem_part, got_mem, grad_y, wide_scores, wide_soft, wide_query, wide_grad,
-        g_small, got_small, got_whole,
-    ) = take(21)
+        g_small, got_small, got_half, got_key, all_mem, all_value, all_key,
+    ) = take(25)
     d_keys, d_values = keys, read
-    slots = take(9)
-    load, store, send, recv, send_k, recv_k, send_v, recv_v = take(8)
-    back_sk, back_rk, back_sv, back_rv, send_w, recv_w = take(6)
-    send_up, recv_up, send_on, recv_on, send_x, recv_x, free, go = refs
+    slots = take(8)
+    load, store, send, recv, send_w, recv_w, send_up, recv_up, send_x, recv_x, send_f, recv_f, free, go = refs
 
     section, seq, head = (lax.axis_index(name) for name in (SECTION, SEQ, HEAD))
     seqs = lax.axis_size(SEQ)
@@ -525,6 +523,12 @@
     column_tiles = [(at, width // 3) for at in range(0, width, width // 3)]
     inner_tiles = lane_tiles(inner)
 
+    def key_slot(micro, place):
+        return 2 + micros * COPY_SLOTS + micro * 3 * seqs + place
+
+    def value_slot(micro, place, of_head):
+        return key_slot(micro, seqs + 2 * place + of_head)
+
     def copy(slot, source, target, device):
         return pltpu.make_async_remote_copy(
             src_ref=source,
@@ -642,8 +646,8 @@
         return pltpu.make_async_remote_copy(
             src_ref=key_block.at[micro],
             dst_ref=keys.at[micro, rows_at(source * mem, mem)],
-            send_sem=send_k.at[micro, target],
-            recv_sem=recv_k.at[micro, source],
+            send_sem=send.at[key_slot(micro, target)],
+            recv_sem=recv.at[key_slot(micro, source)],
             device_id={SEQ: target},
             device_id_type=MESH,
         )
@@ -654,8 +658,8 @@
             dst_ref=values.at[
                 micro, rows_at(source * mem, mem), pl.ds(pl.multiple_of(source_head * dv, 128), dv)
             ],
-            send_sem=send_v.at[micro, target, target_head],
-            recv_sem=recv_v.at[micro, source, source_head],
+            send_sem=send.at[value_slot(micro, target, target_head)],
+            recv_sem=recv.at[value_slot(micro, source, source_head)],
             device_id={SEQ: target, HEAD: target_head},
             device_id_type=MESH,
         )
@@ -881,8 +885,8 @@
         return pltpu.make_async_remote_copy(
             src_ref=d_keys.at[micro, rows_at(target * mem, mem)],
             dst_ref=from_k.at[micro, source],
-            send_sem=back_sk.at[micro, target],
-            recv_sem=back_rk.at[micro, source],
+            send_sem=send.at[key_slot(micro, target)],
+            recv_sem=recv.at[key_slot(micro, source)],
             device_id={SEQ: target},
             device_id_type=MESH,
         )
@@ -893,9 +897,42 @@
                 micro, rows_at(target * mem, mem), pl.ds(pl.multiple_of(target_head * dv, 128), dv)
             ],
             dst_ref=from_v.at[micro, source, source_head],
-            send_sem=back_sv.at[micro, target, target_head],
-            recv_sem=back_rv.at[micro, source, source_head],
+            send_sem=send.at[value_slot(micro, target, target_head)],
+            recv_sem=recv.at[value_slot(micro, source, source_head)],
             device_id={SEQ: target, HEAD: target_head},
+            device_id_type=MESH,
+        )
+
+    factors = ((out_mem, all_mem), (value_block, all_value), (key_block, all_key))
+
+    def factor_copy(kind, source, target):
+        own, everyone = factors[kind]
+        return pltpu.make_async_remote_copy(
+            src_ref=own,
+            dst_ref=everyone.at[:, rows_at(source * mem, mem)],
+            send_sem=send_f.at[kind, target],
+            recv_sem=recv_f.at[kind, source],
+            device_id={SEQ: target},
+            device_id_type=MESH,
+        )
+
+    def others(t):
+        return t != seq
+
+    def spread_factor(kind):
+        own, everyone = factors[kind]
+        everyone[:, rows_at(seq * mem, mem)] = own[...]
+        each_seq(others, lambda t: factor_copy(kind, seq, t).start())
+
+    spread_factor(0)
+
+    def key_half_copy(micro):
+        return pltpu.make_async_remote_copy(
+            src_ref=key_block.at[micro],
+            dst_ref=got_key.at[micro],
+            send_sem=send_x.at[micro],
+            recv_sem=recv_x.at[micro],
+            device_id=partner,
             device_id_type=MESH,
         )
 
@@ -957,6 +994,7 @@
             value_block[micro], w_value[...]
         )
         mem_copy(micro).start()
+        key_half_copy(micro).start()
 
     def forward_sent(micro):
         def sent(t):
@@ -973,8 +1011,11 @@
         return ref[...].reshape(micros * ref.shape[1], ref.shape[2])
 
     w_query[...] = mm_tn(both(out_local), both(query_proj))
-    w_key[...] = mm_tn(both(out_mem), both(key_block))
-    w_value[...] = mm_tn(both(out_mem), both(value_block))
+    spread_factor(1)
+    for micro in range(micros):
+        key_half_copy(micro).wait()
+        key_block[micro] += got_key[micro]
+    spread_factor(2)
     def feed_forward_back(micro):
         mem_copy(micro).wait()
         d_out[micro, mem_rows] = mem_part[micro] + got_mem[micro]
@@ -1005,9 +1046,9 @@
     targets = (device(lax.rem(place + 1, seqs)), device(lax.rem(place + seqs - 1, seqs)))
     signs = (1, -1)
     kinds = range(w_in.shape[0])
-    sources = [w_down, w_up, w_value, w_out, *(w_in.at[kind] for kind in kinds), g_small, got_whole]
-    results = [down_sum, up_sum, value_sum, out_sum, *(in_sum.at[kind] for kind in kinds)]
-    results += [small_sum, whole_sum.at[head]]
+    sources = [w_down, w_up, w_out, *(w_in.at[kind] for kind in kinds), g_small, got_half]
+    results = [down_sum, up_sum, out_sum, *(in_sum.at[kind] for kind in kinds)]
+    results += [small_sum, half_sum.at[head]]
     count = len(sources)
     ways = [[(index, way) for index in group for way in range(2)] for group in (range(2), range(2, count))]
     last = seqs - 2
@@ -1036,8 +1077,8 @@
         return pltpu.make_async_remote_copy(
             src_ref=source,
             dst_ref=target,
-            send_sem=send_on.at[step, way, index],
-            recv_sem=recv_on.at[step, way, index],
+            send_sem=send.at[(step * 2 + way) * count + index],
+            recv_sem=recv.at[(step * 2 + way) * count + index],
             device_id=targets[way],
             device_id_type=MESH,
         )
@@ -1053,7 +1094,7 @@
         )
 
     def hand_over(way, spot, step):
-        mine = block(whole_sum.at[head], way, spot)
+        mine = block(half_sum.at[head], way, spot)
         return over(mine, mine, 2 + way * seqs + step)
 
     def home(index, way):
@@ -1137,7 +1178,7 @@
     for at, tile in inner_tiles:
         cut = slice(at, at + tile)
         w_up[:, cut] = mm_tn(both(normed), both(d_pre.at[:, :, cut]))
-    begin(1, 2)
+    begin(1)
 
     def attention_back(micro):
         unit, inverse = unit_rows(hidden[micro])
@@ -1180,6 +1221,12 @@
             qkv[micro, mem_rows, query] = mem_query
             qkv[micro, seg_rows, key] = d_key
             qkv[micro, seg_rows, value] = d_value
+            if place % 2 == 1 and place + 1 < heads:
+
+                @pl.when(section == 1)
+                def _(place=place):
+                    sum_up(0, 3 * micro + (place + 1) // 2)
+
         qkv[micro, mem_rows, share:] = jnp.zeros((mem, 2 * share), jnp.float32)
         qkv[micro, :, share : 2 * share] += mm_tn(wide_scores[...], wide_query[...])
         qkv[micro, :, 2 * share :] += mm_tn(wide_soft[...], wide_grad[...])
@@ -1197,7 +1244,7 @@
 
     def attention_back_and_ring(micro):
         attention_back(micro)
-        sum_up(0, micro + 1)
+        sum_up(0, jnp.where(section == 1, 3 * micro + 3, micro + 1))
 
     each_micro(attention_back_and_ring)
 
@@ -1227,63 +1274,9 @@
     small_copy = over(g_small, got_small, 0)
     small_copy.start()
 
-    def whole_copy(matrix):
-        return over((w_query, w_key)[matrix], got_whole, 1)
-
-    for matrix in range(2):
-
-        @pl.when(head == matrix)
-        def _(matrix=matrix):
-            whole_copy(1 - matrix).start()
-
-    w_out_all[head] = mm_tn(both(attended), both(hidden))
-    begin(3)
-    sum_up(0, jnp.int32(3))
-    for micro in range(micros):
-        unit, _ = unit_rows(rows[micro])
-        normed[micro] = unit * gains[0:1] + biases[0:1]
-    for kind in kinds:
-        w_in[kind] = mm_tn(both(normed), both(qkv.at[:, :, kind * share : (kind + 1) * share]))
-        begin(4 + kind)
-        if kind == 1:
-            sum_up(0, jnp.int32(4))
-    small_copy.wait()
-    g_small[0:SHARED_ROWS] += got_small[0:SHARED_ROWS]
-    begin(count - 2)
-    whole_copy(0).wait()
-    for matrix in range(2):
-
-        @pl.when(head == matrix)
-        def _(matrix=matrix):
-            got_whole[...] += (w_query, w_key)[matrix][...]
-
-    begin(count - 1)
-
-    def ring_turn(turn, carry):
-        advance(0, turn + AHEAD)
-        advance(1, turn)
-        return carry
-
-    lax.fori_loop(1, 2 * seqs - 1, ring_turn, 0)
-    for index, way in ways[0] + ways[1]:
-        home(index, way).wait()
-        up_copy(index, way, last, slot_of(index, way, last)).wait_send()
-
-    def passed(step, carry):
-        for index, way in ways[0] + ways[1]:
-            own = slot_of(index, way, 0)
-            on_copy(index, way, step, own, own).wait_send()
-        return carry
-
-    lax.fori_loop(0, seqs - 1, passed, 0)
-
-    def crossed(step, carry):
-        for way in range(2):
-            theirs = block(whole_sum.at[other], way, place - signs[way] * (step - 1))
-            over(theirs, theirs, 2 + way * seqs + step).wait()
-        return carry
-
-    lax.fori_loop(0, seqs, crossed, 0)
+    half = width // 2
+    half_copy = over(w_query.at[rows_at(other * half, half)], got_half, 1)
+    half_copy.start()
 
     tokens.wait_send()
     over_out().wait_send()
@@ -1309,6 +1302,78 @@
 
     each_micro(all_sent)
 
+    @pl.when(section == 1)
+    def _():
+        turn_round(0)
+
+    w_out_all[head] = mm_tn(both(attended), both(hidden))
+    begin(2)
+
+    @pl.when(section == 1)
+    def _():
+        pass_on(0, jnp.int32(1))
+
+    @pl.when(section == 0)
+    def _():
+        sum_up(0, jnp.int32(3))
+
+    for micro in range(micros):
+        unit, _ = unit_rows(rows[micro])
+        normed[micro] = unit * gains[0:1] + biases[0:1]
+    for kind in kinds:
+        w_in[kind] = mm_tn(both(normed), both(qkv.at[:, :, kind * share : (kind + 1) * share]))
+        begin(3 + kind)
+        if kind == 1:
+
+            @pl.when(section == 1)
+            def _():
+                pass_on(0, jnp.int32(2))
+
+    small_copy.wait()
+    g_small[0:SHARED_ROWS] += got_small[0:SHARED_ROWS]
+    begin(count - 2)
+    half_copy.wait()
+    got_half[...] += w_query[rows_at(head * half, half)]
+    begin(count - 1)
+    for kind in range(3):
+        each_seq(others, lambda t, kind=kind: factor_copy(kind, t, t).wait_recv())
+    w_key[...] = mm_tn(both(all_mem), both(all_key))
+    w_value[...] = mm_tn(both(all_mem), both(all_value))
+    value_out = pltpu.make_async_copy(w_value, value_sum, load.at[0])
+    key_out = pltpu.make_async_copy(w_key, key_sum, load.at[1])
+    value_out.start()
+    key_out.start()
+
+    def ring_turn(turn, carry):
+        advance(0, turn + jnp.where(section == 1, AHEAD[1], AHEAD[0]))
+        advance(1, turn)
+        return carry
+
+    lax.fori_loop(1, 2 * seqs - 1, ring_turn, 0)
+    value_out.wait()
+    key_out.wait()
+    for kind in range(3):
+        each_seq(others, lambda t, kind=kind: factor_copy(kind, seq, t).wait_send())
+    for index, way in ways[0] + ways[1]:
+        home(index, way).wait()
+        up_copy(index, way, last, slot_of(index, way, last)).wait_send()
+
+    def passed(step, carry):
+        for index, way in ways[0] + ways[1]:
+            own = slot_of(index, way, 0)
+            on_copy(index, way, step, own, own).wait_send()
+        return carry
+
+    lax.fori_loop(0, seqs - 1, passed, 0)
+
+    def crossed(step, carry):
+        for way in range(2):
+            theirs = block(half_sum.at[other], way, place - signs[way] * (step - 1))
+            over(theirs, theirs, 2 + way * seqs + step).wait()
+        return carry
+
+    lax.fori_loop(0, seqs, crossed, 0)
+
 
 def shapes_of(*shapes):
     return tuple(jax.ShapeDtypeStruct(shape, jnp.float32) for shape in shapes)
@@ -1324,7 +1389,7 @@
 
 def params_of(number):
     return pltpu.CompilerParams(
-        collective_id=number, has_side_effects=True, vmem_limit_bytes=62 << 20
+        collective_id=number, has_side_effects=True, vmem_limit_bytes=63 << 20
     )
 
 
@@ -1382,10 +1447,10 @@
     )
     w_out = projection_out[0]
     few = (norm_gains[0], norm_biases[0], head_bias[0], residual_bias[0], up_bias, memory_tokens[0])
-    slots = 2 + micros * COPY_SLOTS
-    ring = [w.shape for w in (down_weight[0], up_weight[0], value_memory[0], w_out)]
-    ring += [w_in.shape[1:]] * 3 + [(16 * seqs, 128), (width, dk)]
-    g_down, g_up, g_in, g_out, g_value, small, whole, y, grad_x = pl.pallas_call(
+    ring = [w.shape for w in (down_weight[0], up_weight[0], w_out)]
+    ring += [w_in.shape[1:]] * 3 + [(16 * seqs, 128), (width // 2, dk)]
+    slots = max(2 + micros * (COPY_SLOTS + 3 * seqs), 2 * (seqs - 1) * len(ring))
+    g_down, g_up, g_in, g_out, g_value, g_key, small, g_query, y, grad_x = pl.pallas_call(
         functools.partial(layers_kernel, 2),
         out_shape=shapes_of(
             down_weight[0].shape,
@@ -1393,13 +1458,14 @@
             w_in.shape,
             w_out.shape,
             value_memory[0].shape,
+            key_memory[0].shape,
             (16 * seqs, 128),
-            (2, width, dk),
+            (2, width // 2, dk),
             (micros, local, width),
             (micros, local, width),
         ),
         in_specs=[SMEM, HBM] + [VMEM] * len(few) + [HBM] * (len(weights) + 1),
-        out_specs=(HBM,) * 7 + (VMEM,) * 2,
+        out_specs=(HBM,) * 8 + (VMEM,) * 2,
         scratch_shapes=buffers(
             *(w.shape for w in weights),
             *((micros, *record) for record in records),
@@ -1425,15 +1491,17 @@
             (mem * (share // HEAD_DIM), share),
             (16 * seqs, 128),
             (16 * seqs, 128),
-            (width, dk),
+            (width // 2, dk),
+            (micros, mem, dk),
+            (micros, stored, width),
+            (micros, stored, dv),
+            (micros, stored, dk),
             *((2, SLOTS, height // (2 * seqs), columns) for height, columns in ring),
         )
         + [dma(len(weights) + 1 + micros), dma(2, len(ring)), dma(slots), dma(slots)]
-        + [dma(micros, seqs), dma(micros, seqs), dma(micros, seqs, 2), dma(micros, seqs, 2)] * 2
         + [dma(seqs), dma(seqs)]
         + [dma(SLOTS, 2, len(ring)), dma(SLOTS, 2, len(ring))]
-        + [dma(seqs - 1, 2, len(ring)), dma(seqs - 1, 2, len(ring))]
-        + [dma(2 + 2 * seqs), dma(2 + 2 * seqs), pltpu.SemaphoreType.REGULAR((2, 2)), pltpu.SemaphoreType.REGULAR],
+        + [dma(2 + 2 * seqs), dma(2 + 2 * seqs), dma(3, seqs), dma(3, seqs), pltpu.SemaphoreType.REGULAR((2, 2)), pltpu.SemaphoreType.REGULAR],
         compiler_params=params_of(0),
         name="layers",
     )(short_items, x, *few, *weights, w_out)
@@ -1456,7 +1524,7 @@
     outs = pl.pallas_call(
         finish_kernel,
         out_shape=shapes_of(*outs),
-        in_specs=[HBM] * 5 + [VMEM] + [HBM] * 3,
+        in_specs=[HBM] * 5 + [VMEM] + [HBM] * 4,
         out_specs=(HBM, VMEM, VMEM, HBM, VMEM, HBM, VMEM, HBM, VMEM, HBM, VMEM, HBM, HBM, HBM),
         scratch_shapes=buffers(
             g_down.shape,
@@ -1464,19 +1532,19 @@
             g_in.shape,
             g_out.shape,
             g_value.shape,
-            whole.shape[1:],
-            whole.shape[1:],
+            g_key.shape,
+            g_key.shape,
             y.shape,
         )
         + [dma(8), dma(8)],
         compiler_params=pltpu.CompilerParams(vmem_limit_bytes=62 << 20),
         name="finish",
-    )(g_down, g_up, g_in, g_out, g_value, small, whole, y, grad_x)
+    )(g_down, g_up, g_in, g_out, g_value, small, g_query.reshape(width, dk), g_key, y, grad_x)
     return (*outs[:3], outs[3].transpose(0, 2, 1, 3), *outs[4:])
 
 
 def finish_kernel(
-    g_down, g_up, g_in, g_out, g_value, small, whole, y, grad_x,
+    g_down, g_up, g_in, g_out, g_value, small, g_query, g_key, y, grad_x,
     rows, gains, biases, proj_in, head_bias, proj_out, residual, up, up_bias, down, tokens, query, key,
     value, *refs
 ):
@@ -1487,8 +1555,8 @@
         (g_in, proj_in.at[0]),
         (g_out, proj_out.at[0]),
         (g_value, value.at[0]),
-        (whole.at[0], query.at[0]),
-        (whole.at[1], key.at[0]),
+        (g_query, query.at[0]),
+        (g_key, key.at[0]),
         (y, rows.at[0]),
     )
     section = lax.axis_index(SECTION)

time: 517 us -> 491 us (0.950)
  Pallas kernels: 511 us -> 485 us
    pallas_call x1, Pallas kernels: 497 us -> 472 us  [shards_of_two(): pl.pallas_call(functools.partial(layers_kernel, 2), out_shape=shapes_of(d...]
where the time goes in v7:
time: 491 us; the launch traced here: 486 us
  Pallas kernels  485 us (99%)
    pallas_call x1, Pallas kernels, shards_of_two(): pl.pallas_call(functools.partial(layers_kernel, 2), out_shape=shapes_of(d...  472 us
    pallas_call x1, Pallas kernels, shards_of_two(): pl.pallas_call(finish_kernel, out_shape=shapes_of(*outs), in_specs=[HBM]...  13.6 us

profile of v7, /device:TPU:0, one launch (start us, length us, event | category | flops | bytes accessed | tf_op | source)
XLA Modules:
  0.0 486.4 jit_solution(17951296815876561654)
XLA Ops:
  0.7 471.7 %layers.1 = (f32[1536,768]{1,0:T(8,128)}, f32[768,1536]{1,0:T(8,128)}, f32[3,768,384]{2,1,0:T(8,128)}, f32[384,768]{1,0:T(8,128)}, f32[768,384]{1,0:T(8,128)}, /...) custom-call(s32[1,3]{1,0:T(1,128)} %refs_0_.1, ...), custom_call_target="tpu_custom_call" | custom-call | tf_op jit(solution)/shard_map/layers/pallas_call | solution.py:1453
  472.4 13.6 %finish.1 = (f32[1,2,128,768]{3,2,1,0:T(8,128)}, f32[1,2,768]{2,1,0:T(2,128)}, f32[1,2,768]{2,1,0:T(2,128)}, f32[1,3,768,384]{3,2,1,0:T(8,128)}, f32[1,2,384]{2,...) custom-call(f32[1536,768]{1,0:T(8,128)} %get-tuple-element.38.g_down, ...), custom_call_target="tpu_custom_call" | custom-call | tf_op jit(solution)/shard_map/finish/pallas_call | solution.py:1524

commit v8 on v7

--- a/solution.py
+++ b/solution.py
@@ -474,7 +474,7 @@
 
 
 SLOTS = 3
-AHEAD = (3, 9)
+AHEAD = (3, 7)
 
 
 def layers_kernel(lanes, *refs):
@@ -1221,11 +1221,11 @@
             qkv[micro, mem_rows, query] = mem_query
             qkv[micro, seg_rows, key] = d_key
             qkv[micro, seg_rows, value] = d_value
-            if place % 2 == 1 and place + 1 < heads:
+            if place == heads // 2:
 
                 @pl.when(section == 1)
-                def _(place=place):
-                    sum_up(0, 3 * micro + (place + 1) // 2)
+                def _():
+                    sum_up(0, 2 * micro + 1)
 
         qkv[micro, mem_rows, share:] = jnp.zeros((mem, 2 * share), jnp.float32)
         qkv[micro, :, share : 2 * share] += mm_tn(wide_scores[...], wide_query[...])
@@ -1244,7 +1244,7 @@
 
     def attention_back_and_ring(micro):
         attention_back(micro)
-        sum_up(0, jnp.where(section == 1, 3 * micro + 3, micro + 1))
+        sum_up(0, jnp.where(section == 1, 2 * micro + 2, micro + 1))
 
     each_micro(attention_back_and_ring)
 
@@ -1304,14 +1304,14 @@
 
     @pl.when(section == 1)
     def _():
-        turn_round(0)
+        sum_up(0, jnp.int32(5))
 
     w_out_all[head] = mm_tn(both(attended), both(hidden))
     begin(2)
 
     @pl.when(section == 1)
     def _():
-        pass_on(0, jnp.int32(1))
+        sum_up(0, jnp.int32(6))
 
     @pl.when(section == 0)
     def _():
@@ -1327,7 +1327,7 @@
 
             @pl.when(section == 1)
             def _():
-                pass_on(0, jnp.int32(2))
+                turn_round(0)
 
     small_copy.wait()
     g_small[0:SHARED_ROWS] += got_small[0:SHARED_ROWS]

time: 491 us -> 492 us (level)
  no operation moved by 1% of the time
where the time goes in v8:
time: 492 us; the launch traced here: 487 us
  Pallas kernels  486 us (99%)
    pallas_call x1, Pallas kernels, shards_of_two(): pl.pallas_call(functools.partial(layers_kernel, 2), out_shape=shapes_of(d...  472 us
    pallas_call x1, Pallas kernels, shards_of_two(): pl.pallas_call(finish_kernel, out_shape=shapes_of(*outs), in_specs=[HBM]...  13.6 us

profile of v8, /device:TPU:0, one launch (start us, length us, event | category | flops | bytes accessed | tf_op | source)
XLA Modules:
  0.0 486.7 jit_solution(8295745704382952157)
XLA Ops:
  0.7 472.0 %layers.1 = (f32[1536,768]{1,0:T(8,128)}, f32[768,1536]{1,0:T(8,128)}, f32[3,768,384]{2,1,0:T(8,128)}, f32[384,768]{1,0:T(8,128)}, f32[768,384]{1,0:T(8,128)}, /...) custom-call(s32[1,3]{1,0:T(1,128)} %refs_0_.1, ...), custom_call_target="tpu_custom_call" | custom-call | tf_op jit(solution)/shard_map/layers/pallas_call | solution.py:1453
  472.6 13.6 %finish.1 = (f32[1,2,128,768]{3,2,1,0:T(8,128)}, f32[1,2,768]{2,1,0:T(2,128)}, f32[1,2,768]{2,1,0:T(2,128)}, f32[1,3,768,384]{3,2,1,0:T(8,128)}, f32[1,2,384]{2,...) custom-call(f32[1536,768]{1,0:T(8,128)} %get-tuple-element.38.g_down, ...), custom_call_target="tpu_custom_call" | custom-call | tf_op jit(solution)/shard_map/finish/pallas_call | solution.py:1524
